TPU v7x, 32 devices: a whole 2x2x4 slice. The times are simulated.
32 devices in a mesh: rep: 4 (over x, core), fsdp: 8 (over z, y).
Axes of the slice: x: 2, y: 2, z: 4, core: 2. Of those that a mesh axis runs over, the one named last changes fastest.
Arguments:
- image_tokens: bfloat16 [32, 256, 2048], P(('rep', 'fsdp')), may hold values from -6 to 6
- text_tokens: bfloat16 [32, 128, 2048], P(('rep', 'fsdp')), may hold values from -6 to 6
- text_lengths: int32 [32], P(('rep', 'fsdp')), may hold values from 1 to 128, as said below
- timesteps: int32 [32], P(('rep', 'fsdp')), may hold values from 0 to 999
- cotangent: bfloat16 [32, 256, 2048], P(('rep', 'fsdp')), may hold values from -6 to 6
- mod_weight: bfloat16 [2048, 12288], P('fsdp'), may hold values from -0.125 to 0.125
- qkv_weight: bfloat16 [2048, 6144], P('fsdp'), may hold values from -0.125 to 0.125
- out_weight: bfloat16 [2048, 2048], P('fsdp'), may hold values from -1 to 1
- query_weight: bfloat16 [2048, 2048], P('fsdp'), may hold values from -0.125 to 0.125
- keyval_weight: bfloat16 [2048, 4096], P('fsdp'), may hold values from -0.125 to 0.125
- merge_weight: bfloat16 [2048, 2048], P('fsdp'), may hold values from -0.75 to 0.75
- cross_gain: bfloat16 [2048], P('fsdp'), may hold values from 0.25 to 1.75
- up_weight: bfloat16 [2048, 8192], P('fsdp'), may hold values from -0.125 to 0.125
- down_weight: bfloat16 [8192, 2048], P('fsdp'), may hold values from -0.0625 to 0.0625
Outputs:
- block_out: bfloat16 [32, 256, 2048], P(('rep', 'fsdp'))
- image_grad: bfloat16 [32, 256, 2048], P(('rep', 'fsdp'))
- text_grad: bfloat16 [32, 128, 2048], P(('rep', 'fsdp'))
- mod_grad: float32 [2048, 12288], P('fsdp')
- qkv_grad: float32 [2048, 6144], P('fsdp')
- out_grad: float32 [2048, 2048], P('fsdp')
- query_grad: float32 [2048, 2048], P('fsdp')
- keyval_grad: float32 [2048, 4096], P('fsdp')
- merge_grad: float32 [2048, 2048], P('fsdp')
- gain_grad: float32 [2048], P('fsdp')
- up_grad: float32 [2048, 8192], P('fsdp')
- down_grad: float32 [8192, 2048], P('fsdp')
Inputs may be any that keep to these rules, and one draw needn't show every extreme that they name: `text_lengths`: valid text tokens of each image; slots from it on are padding. Some image uses all 128 slots.
All inputs are finite; a program needn't handle non-finite values.
Results may differ from a plain program's by a relative error of at most 0.025.
Values may be sent and summed in bfloat16 or wider, within the bound.
No kernel may reach another device: no remote copies, remote signals or barrier semaphores. Data moves between devices by JAX's collectives and lax.ppermute only.
A program may use at most 512 MiB of HBM per device.

v0:
```python
import math

import jax
import jax.numpy as jnp
from jax import lax
from jax.sharding import PartitionSpec as P

HEADS = 16


EPSILON = 1e-06


def matmul(left, right):
    return jnp.dot(left, right, preferred_element_type=jnp.float32)


def outer_sum(left, right):
    return lax.dot_general(
        left, right, (((0,), (0,)), ((), ())), preferred_element_type=jnp.float32
    )


def back_product(left, right):
    return lax.dot_general(
        left, right, (((1,), (1,)), ((), ())), preferred_element_type=jnp.float32
    )


def normed(value):
    return value * lax.rsqrt(jnp.mean(value * value, axis=-1, keepdims=True) + EPSILON)


def normed_back(value, grad):
    return jax.vjp(normed, value)[1](grad)[0]


def smooth_gate(value):
    return jax.nn.gelu(value, approximate=True)


def flatten(value):
    return value.reshape(-1, value.shape[-1])


def split_heads(value, images):
    return value.reshape(images, -1, HEADS, value.shape[-1] // HEADS)


def attend(queries, keys, values, key_valid, score_scale):
    scores = (
        jnp.einsum("nqhd,nkhd->nhqk", queries, keys, preferred_element_type=jnp.float32)
        * score_scale
    )
    if key_valid is not None:
        scores = jnp.where(key_valid, scores, -jnp.inf)
    row_top = jnp.max(scores, axis=-1, keepdims=True)
    raised = jnp.exp(scores - row_top)
    totals = jnp.sum(raised, axis=-1, keepdims=True)
    weights = (raised / totals).astype(jnp.bfloat16)
    mixed_heads = jnp.einsum("nhqk,nkhd->nqhd", weights, values, preferred_element_type=jnp.float32)
    return (mixed_heads.astype(jnp.bfloat16), row_top + jnp.log(totals))


def attend_back(queries, keys, values, logsum, grad_mixed, key_valid, score_scale):
    scores = (
        jnp.einsum("nqhd,nkhd->nhqk", queries, keys, preferred_element_type=jnp.float32)
        * score_scale
    )
    if key_valid is not None:
        scores = jnp.where(key_valid, scores, -jnp.inf)
    weights = jnp.exp(scores - logsum)
    grad_weights = jnp.einsum(
        "nqhd,nkhd->nhqk", grad_mixed, values, preferred_element_type=jnp.float32
    )
    grad_values = jnp.einsum(
        "nhqk,nqhd->nkhd",
        weights.astype(jnp.bfloat16),
        grad_mixed,
        preferred_element_type=jnp.float32,
    )
    inner_sum = jnp.sum(weights * grad_weights, axis=-1, keepdims=True)
    grad_scores = (score_scale * (weights * (grad_weights - inner_sum))).astype(jnp.bfloat16)
    grad_queries = jnp.einsum(
        "nhqk,nkhd->nqhd", grad_scores, keys, preferred_element_type=jnp.float32
    )
    grad_keys = jnp.einsum(
        "nhqk,nqhd->nkhd", grad_scores, queries, preferred_element_type=jnp.float32
    )
    return (grad_queries, grad_keys, grad_values)


def body(
    image_tokens,
    text_tokens,
    text_lengths,
    timesteps,
    cotangent,
    mod_weight,
    qkv_weight,
    out_weight,
    query_weight,
    keyval_weight,
    merge_weight,
    cross_gain,
    up_weight,
    down_weight,
):
    images, length, model_width = image_tokens.shape
    text_count = text_tokens.shape[1]
    token_rows = images * length
    score_scale = (model_width // HEADS) ** (-0.5)
    shard_rows = mod_weight.shape[0]
    member = lax.axis_index("fsdp")
    residual = image_tokens.astype(jnp.float32)

    def fetch_self():
        return (
            lax.all_gather(qkv_weight, "fsdp", axis=0, tiled=True),
            lax.all_gather(out_weight, "fsdp", axis=0, tiled=True),
        )

    def fetch_cross():
        return (
            lax.all_gather(query_weight, "fsdp", axis=0, tiled=True),
            lax.all_gather(keyval_weight, "fsdp", axis=0, tiled=True),
            lax.all_gather(merge_weight, "fsdp", axis=0, tiled=True),
            lax.all_gather(cross_gain, "fsdp", axis=0, tiled=True),
            lax.all_gather(up_weight, "fsdp", axis=0, tiled=True),
        )

    def fetch_down():
        return lax.all_gather(down_weight, "fsdp", axis=0, tiled=True)

    def share_rows(left, right):

        def row_term(row_start, row_count):
            return outer_sum(left, right)

        return lax.psum_scatter(
            row_term(
                jnp.int32(0), left.shape[1] // lax.axis_size("fsdp") * lax.axis_size("fsdp")
            ).astype(jnp.bfloat16),
            "fsdp",
            scatter_dimension=0,
            tiled=True,
        ).astype(jnp.float32)

    half_width = model_width // 2
    frequency = jnp.exp(-math.log(10000.0) * jnp.arange(half_width, dtype=jnp.float32) / half_width)
    angles = timesteps.astype(jnp.float32)[:, None] * frequency[None, :]
    condition = jnp.concatenate([jnp.sin(angles), jnp.cos(angles)], axis=1).astype(jnp.bfloat16)
    cond_group = lax.all_gather(condition, "fsdp", axis=0, tiled=True)
    cond_slice = lax.dynamic_slice_in_dim(cond_group, member * shard_rows, shard_rows, 1)
    modulation = lax.psum_scatter(
        matmul(cond_slice, mod_weight), "fsdp", scatter_dimension=0, tiled=True
    )
    pieces = modulation.reshape(images, 6, 1, model_width)
    shift_self, scale_self, gate_self = (pieces[:, 0], pieces[:, 1], pieces[:, 2])
    shift_mlp, scale_mlp, gate_mlp = (pieces[:, 3], pieces[:, 4], pieces[:, 5])
    qkv_full, out_full = fetch_self()
    norm_one = normed(residual)
    act_one = flatten(norm_one * (1.0 + scale_self) + shift_self).astype(jnp.bfloat16)
    qkv_act = matmul(act_one, qkv_full).astype(jnp.bfloat16)
    queries = split_heads(qkv_act[:, :model_width], images)
    keys_self = split_heads(qkv_act[:, model_width : 2 * model_width], images)
    values_self = split_heads(qkv_act[:, 2 * model_width :], images)
    mixed_self, logsum_self = attend(queries, keys_self, values_self, None, score_scale)
    mixed_flat = mixed_self.reshape(token_rows, model_width)
    branch_one = matmul(mixed_flat, out_full).reshape(images, length, model_width)
    hidden_one = residual + gate_self * branch_one
    query_full, keyval_full, merge_full, gain_full, up_full = fetch_cross()
    norm_two = normed(hidden_one)
    act_two = flatten(norm_two * gain_full).astype(jnp.bfloat16)
    cross_queries = split_heads(matmul(act_two, query_full).astype(jnp.bfloat16), images)
    text_flat = flatten(text_tokens)
    keyval = matmul(text_flat, keyval_full).astype(jnp.bfloat16)
    cross_keys = split_heads(keyval[:, :model_width], images)
    cross_values = split_heads(keyval[:, model_width:], images)
    key_valid = (jnp.arange(text_count, dtype=jnp.int32)[None, :] < text_lengths[:, None])[
        :, None, None, :
    ]
    mixed_cross, logsum_cross = attend(
        cross_queries, cross_keys, cross_values, key_valid, score_scale
    )
    cross_flat = mixed_cross.reshape(token_rows, model_width)
    hidden_two = hidden_one + matmul(cross_flat, merge_full).reshape(images, length, model_width)
    norm_three = normed(hidden_two)
    act_three = flatten(norm_three * (1.0 + scale_mlp) + shift_mlp).astype(jnp.bfloat16)
    pre_act = matmul(act_three, up_full)
    activated = smooth_gate(pre_act).astype(jnp.bfloat16)
    down_full = fetch_down()
    branch_three = matmul(activated, down_full).reshape(images, length, model_width)
    block_out = (hidden_two + gate_mlp * branch_three).astype(jnp.bfloat16)
    grad_block = cotangent.astype(jnp.float32)
    grad_gate_mlp = jnp.sum(grad_block * branch_three, axis=1)
    grad_three = flatten(gate_mlp * grad_block).astype(jnp.bfloat16)
    query_full, keyval_full, merge_full, gain_full, up_full = fetch_cross()
    down_full = fetch_down()
    grad_activated = back_product(grad_three, down_full)

    def row_term(row_start, row_count):
        return outer_sum(activated, grad_three)

    down_grad = lax.psum_scatter(
        row_term(
            jnp.int32(0), activated.shape[1] // lax.axis_size("fsdp") * lax.axis_size("fsdp")
        ).astype(jnp.bfloat16),
        "fsdp",
        scatter_dimension=0,
        tiled=True,
    )
    grad_pre = jax.vjp(smooth_gate, pre_act)[1](grad_activated)[0].astype(jnp.bfloat16)
    up_grad = share_rows(act_three, grad_pre)
    grad_act_three = back_product(grad_pre, up_full).reshape(images, length, model_width)
    grad_shift_mlp = jnp.sum(grad_act_three, axis=1)
    grad_scale_mlp = jnp.sum(grad_act_three * norm_three, axis=1)
    grad_two = grad_block + normed_back(hidden_two, grad_act_three * (1.0 + scale_mlp))
    grad_merge = flatten(grad_two).astype(jnp.bfloat16)
    merge_term = outer_sum(cross_flat, grad_merge)
    grad_mixed_cross = back_product(grad_merge, merge_full).astype(jnp.bfloat16)
    grad_cross_queries, grad_cross_keys, grad_cross_values = attend_back(
        cross_queries,
        cross_keys,
        cross_values,
        logsum_cross,
        split_heads(grad_mixed_cross, images),
        key_valid,
        score_scale,
    )
    grad_query_flat = grad_cross_queries.reshape(token_rows, model_width).astype(jnp.bfloat16)
    grad_keyval = jnp.concatenate(
        [grad_cross_keys.reshape(-1, model_width), grad_cross_values.reshape(-1, model_width)],
        axis=1,
    ).astype(jnp.bfloat16)
    query_term = outer_sum(act_two, grad_query_flat)
    keyval_term = outer_sum(text_flat, grad_keyval)
    text_grad = (
        back_product(grad_keyval, keyval_full).astype(jnp.bfloat16).reshape(text_tokens.shape)
    )
    grad_act_two = back_product(grad_query_flat, query_full).reshape(images, length, model_width)
    gain_term = jnp.sum(grad_act_two * norm_two, axis=(0, 1))
    grad_one = grad_two + normed_back(hidden_one, grad_act_two * gain_full)
    query_grad, keyval_grad, merge_grad, gain_grad = (
        lax.psum_scatter(
            query_term.astype(jnp.bfloat16), "fsdp", scatter_dimension=0, tiled=True
        ).astype(jnp.float32),
        lax.psum_scatter(
            keyval_term.astype(jnp.bfloat16), "fsdp", scatter_dimension=0, tiled=True
        ).astype(jnp.float32),
        lax.psum_scatter(
            merge_term.astype(jnp.bfloat16), "fsdp", scatter_dimension=0, tiled=True
        ).astype(jnp.float32),
        lax.psum_scatter(
            gain_term.astype(jnp.bfloat16), "fsdp", scatter_dimension=0, tiled=True
        ).astype(jnp.float32),
    )
    grad_gate_self = jnp.sum(grad_one * branch_one, axis=1)
    grad_out = flatten(gate_self * grad_one).astype(jnp.bfloat16)
    qkv_full, out_full = fetch_self()
    out_grad = share_rows(mixed_flat, grad_out)
    grad_mixed_self = back_product(grad_out, out_full).astype(jnp.bfloat16)
    grad_queries, grad_keys, grad_values = attend_back(
        queries,
        keys_self,
        values_self,
        logsum_self,
        split_heads(grad_mixed_self, images),
        None,
        score_scale,
    )
    grad_qkv = jnp.concatenate(
        [
            grad_queries.reshape(token_rows, model_width),
            grad_keys.reshape(token_rows, model_width),
            grad_values.reshape(token_rows, model_width),
        ],
        axis=1,
    ).astype(jnp.bfloat16)
    qkv_grad = share_rows(act_one, grad_qkv)
    grad_act_one = back_product(grad_qkv, qkv_full).reshape(images, length, model_width)
    grad_shift_self = jnp.sum(grad_act_one, axis=1)
    grad_scale_self = jnp.sum(grad_act_one * norm_one, axis=1)
    image_grad = (grad_one + normed_back(residual, grad_act_one * (1.0 + scale_self))).astype(
        jnp.bfloat16
    )
    grad_modulation = (
        jnp.stack(
            [
                grad_shift_self,
                grad_scale_self,
                grad_gate_self,
                grad_shift_mlp,
                grad_scale_mlp,
                grad_gate_mlp,
            ],
            axis=1,
        )
        .reshape(images, 6 * model_width)
        .astype(jnp.bfloat16)
    )
    grad_group = lax.all_gather(grad_modulation, "fsdp", axis=0, tiled=True)
    mod_term = outer_sum(cond_slice, grad_group)
    summed = (
        lax.psum(mod_term.astype(jnp.bfloat16), "rep").astype(jnp.float32),
        lax.psum(qkv_grad.astype(jnp.bfloat16), "rep").astype(jnp.float32),
        lax.psum(out_grad.astype(jnp.bfloat16), "rep").astype(jnp.float32),
        lax.psum(query_grad.astype(jnp.bfloat16), "rep").astype(jnp.float32),
        lax.psum(keyval_grad.astype(jnp.bfloat16), "rep").astype(jnp.float32),
        lax.psum(merge_grad.astype(jnp.bfloat16), "rep").astype(jnp.float32),
        lax.psum(gain_grad.astype(jnp.bfloat16), "rep").astype(jnp.float32),
        lax.psum(up_grad.astype(jnp.bfloat16), "rep").astype(jnp.float32),
        lax.psum(down_grad, "rep").astype(jnp.float32),
    )
    return (
        block_out,
        image_grad,
        text_grad,
        summed[0],
        summed[1],
        summed[2],
        summed[3],
        summed[4],
        summed[5],
        summed[6],
        summed[7],
        summed[8],
    )


def solution(mesh):
    placed = (
        P(("rep", "fsdp"), None, None),
        P(("rep", "fsdp"), None, None),
        P(("rep", "fsdp")),
        P(("rep", "fsdp")),
        P(("rep", "fsdp"), None, None),
        P("fsdp", None),
        P("fsdp", None),
        P("fsdp", None),
        P("fsdp", None),
        P("fsdp", None),
        P("fsdp", None),
        P("fsdp"),
        P("fsdp", None),
        P("fsdp", None),
    )
    return jax.shard_map(
        body,
        mesh=mesh,
        in_specs=placed,
        out_specs=(
            P(("rep", "fsdp"), None, None),
            P(("rep", "fsdp"), None, None),
            P(("rep", "fsdp"), None, None),
            P("fsdp", None),
            P("fsdp", None),
            P("fsdp", None),
            P("fsdp", None),
            P("fsdp", None),
            P("fsdp", None),
            P("fsdp"),
            P("fsdp", None),
            P("fsdp", None),
        ),
        check_vma=False,
    )
```

profile of v0, /device:TPU:0, one launch (start us, length us, event | category | flops | bytes accessed | tf_op | source)
XLA Modules:
  0.0 5246.4 jit_solution(12876416990434002429)
XLA Ops:
  8.0 32.3 all-gather
  50.9 20.5 all-gather.1
  72.4 45.3 all-reduce.6.cloned.1.call-done
  119.6 227.2 %all-gather.15.cloned.1.call-done = bf16[2048,4096]{1,0:T(8,128)(2,1)} async-done(((bf16[256,4096]{1,0:T(8,128)(2,1)}), bf16[2048,4096]{1,0:T(8,128)(2,1)}) %all-gather.15.cloned.1.call-update) | async-done | bytes 16777232 | tf_op jit(solution)/shard_map/all_gather | solution.py:126
  356.0 471.1 %all-gather.11.cloned.1.call-done = bf16[2048,6144]{1,0:T(8,128)(2,1)} async-done(((bf16[256,6144]{1,0:T(8,128)(2,1)}), bf16[2048,6144]{1,0:T(8,128)(2,1)}) %all-gather.11.cloned.1.call-update) | async-done | bytes 25165840 | tf_op jit(solution)/shard_map/all_gather | solution.py:119
  827.1 11.9 convolution_convert_fusion.4
  848.1 106.3 %all-gather.13.cloned.1.call-done = bf16[2048,2048]{1,0:T(8,128)(2,1)} async-done(((bf16[256,2048]{1,0:T(8,128)(2,1)}), bf16[2048,2048]{1,0:T(8,128)(2,1)}) %all-gather.13.cloned.1.call-update) | async-done | bytes 8388624 | tf_op jit(solution)/shard_map/all_gather | solution.py:120
  962.1 117.6 %all-gather.17.cloned.1.call-done = bf16[2048,2048]{1,0:T(8,128)(2,1)} async-done(((bf16[256,2048]{1,0:T(8,128)(2,1)}), bf16[2048,2048]{1,0:T(8,128)(2,1)}) %all-gather.17.cloned.1.call-update) | async-done | bytes 8388624 | tf_op jit(solution)/shard_map/all_gather | solution.py:125
  1094.3 110.8 %all-gather.19.cloned.1.call-done = bf16[2048,2048]{1,0:T(8,128)(2,1)} async-done(((bf16[256,2048]{1,0:T(8,128)(2,1)}), bf16[2048,2048]{1,0:T(8,128)(2,1)}) %all-gather.19.cloned.1.call-update) | async-done | bytes 8388624 | tf_op jit(solution)/shard_map/all_gather | solution.py:127
  1212.5 630.1 %all-gather.21.cloned.1.call-done = bf16[2048,8192]{1,0:T(8,128)(2,1)} async-done(((bf16[256,8192]{1,0:T(8,128)(2,1)}), bf16[2048,8192]{1,0:T(8,128)(2,1)}) %all-gather.21.cloned.1.call-update) | async-done | bytes 33554448 | tf_op jit(solution)/shard_map/all_gather | solution.py:129
  1842.6 19.4 fusion.144
  1862.1 619.9 %all-gather.23.cloned.1.call-done = bf16[8192,2048]{1,0:T(8,128)(2,1)} async-done(((bf16[1024,2048]{1,0:T(8,128)(2,1)}), bf16[8192,2048]{1,0:T(8,128)(2,1)}) %all-gather.23.cloned.1.call-update) | async-done | bytes 33554448 | tf_op jit(solution)/shard_map/all_gather | solution.py:133
  2482.0 20.8 fusion.8
  2502.7 18.7 fusion.37
  2521.5 26.1 fusion.30
  2604.2 9.4 convert_bitcast_fusion
  2628.8 9.4 fusion.70
  2638.1 9.4 fusion.73
  2652.2 14.8 convolution_convert_fusion.2
  2667.3 18.9 convolution_convert_fusion
  2686.9 16.9 convolution_convert_fusion.1
  2705.6 14.3 fusion.26
  2721.8 33.3 all-gather.2
  2759.7 116.6 %reduce-scatter.10.cloned.1.call-done = bf16[256,2048]{1,0:T(8,128)(2,1)} async-done(((bf16[2048,2048]{1,0:T(8,128)(2,1)}), bf16[256,2048]{1,0:T(8,128)(2,1)}) %reduce-scatter.10.cloned.1.call-update) | async-done | bytes 1048592 | tf_op jit(solution)/shard_map/reduce_scatter | solution.py:140
  2876.3 152.1 %reduce-scatter.16.cloned.1.call-done = bf16[256,2048]{1,0:T(8,128)(2,1)} async-done(((bf16[2048,2048]{1,0:T(8,128)(2,1)}), bf16[256,2048]{1,0:T(8,128)(2,1)}) %reduce-scatter.16.cloned.1.call-update) | async-done | bytes 1048592 | tf_op jit(solution)/shard_map/reduce_scatter | solution.py:251
  3028.4 285.4 %reduce-scatter.14.cloned.1.call-done = bf16[256,4096]{0,1:T(8,128)(2,1)} async-done(((bf16[2048,4096]{0,1:T(8,128)(2,1)}), bf16[256,4096]{0,1:T(8,128)(2,1)}) %reduce-scatter.14.cloned.1.call-update) | async-done | bytes 2097168 | tf_op jit(solution)/shard_map/reduce_scatter | solution.py:248
  3313.8 407.2 %reduce-scatter.8.cloned.1.call-done = bf16[256,6144]{1,0:T(8,128)(2,1)} async-done(((bf16[2048,6144]{1,0:T(8,128)(2,1)}), bf16[256,6144]{1,0:T(8,128)(2,1)}) %reduce-scatter.8.cloned.1.call-update) | async-done | bytes 3145744 | tf_op jit(solution)/shard_map/reduce_scatter | solution.py:140
  3721.1 546.4 %reduce-scatter.20.cloned.1.call-done = bf16[1024,2048]{1,0:T(8,128)(2,1)} async-done(((bf16[8192,2048]{1,0:T(8,128)(2,1)}), bf16[1024,2048]{1,0:T(8,128)(2,1)}) %reduce-scatter.20.cloned.1.call-update) | async-done | bytes 4194320 | tf_op jit(solution)/shard_map/reduce_scatter | solution.py:205
  4267.5 546.6 %reduce-scatter.18.cloned.1.call-done = bf16[256,8192]{1,0:T(8,128)(2,1)} async-done(((bf16[2048,8192]{1,0:T(8,128)(2,1)}), bf16[256,8192]{1,0:T(8,128)(2,1)}) %reduce-scatter.18.cloned.1.call-update) | async-done | bytes 4194320 | tf_op jit(solution)/shard_map/reduce_scatter | solution.py:140
  4814.8 19.6 all-reduce.1
  4844.9 12.4 fusion.23
  4857.3 353.6 %all-reduce.8.cloned.1.call-done = (bf16[256,4096]{0,1:T(8,128)(2,1)}, bf16[256,12288]{1,0:T(8,128)(2,1)}, bf16[256,6144]{1,0:T(8,128)(2,1)}, bf16[256,2048]{1,0...) async-done(((bf16[256,4096]{0,1:T(8,128)(2,1)}, bf16[256,12288]{1,0:T(8,128)(2,1)}, ...) | async-done | bytes 23068688 | tf_op jit(solution)/shard_map/psum | solution.py:309
  (204 shorter events, 184.9 us)
Async XLA Ops:
  7.2 339.6 %copy-start = (bf16[1,128,2048]{2,1,0:T(8,128)(2,1)S(1)}, bf16[1,128,2048]{2,1,0:T(8,128)(2,1)}, u32[]{:S(2)}) copy-start(bf16[1,128,2048]{2,1,0:T(8,128)(2,1)} %param.15) | copy-start | bytes 1572868
  7.2 110.5 %all-reduce.6.cloned.1.call-start = ((), (), s32[]{:S(2)}) async-start(), calls=%async_computation.21 | async-start | bytes 786432
  45.4 301.4 %all-gather.15.cloned.1.call-start = ((), (), s32[]{:S(2)}) async-start(), calls=%async_computation.9 | async-start | bytes 18874368 | tf_op jit(solution)/shard_map/all_gather | solution.py:126
  46.2 780.9 %all-gather.11.cloned.1.call-start = ((), (), s32[]{:S(2)}) async-start(), calls=%async_computation.7 | async-start | bytes 28311552 | tf_op jit(solution)/shard_map/all_gather | solution.py:119
  46.9 907.5 %all-gather.13.cloned.1.call-start = ((), (), s32[]{:S(2)}) async-start(), calls=%async_computation.8 | async-start | bytes 9437184 | tf_op jit(solution)/shard_map/all_gather | solution.py:120
  47.5 1032.2 %all-gather.17.cloned.1.call-start = ((), (), s32[]{:S(2)}) async-start(), calls=%async_computation.10 | async-start | bytes 9437184 | tf_op jit(solution)/shard_map/all_gather | solution.py:125
  48.1 1157.0 %all-gather.19.cloned.1.call-start = ((), (), s32[]{:S(2)}) async-start(), calls=%async_computation.11 | async-start | bytes 9437184 | tf_op jit(solution)/shard_map/all_gather | solution.py:127
  48.6 1794.0 %all-gather.21.cloned.1.call-start = ((), (), s32[]{:S(2)}) async-start(), calls=%async_computation.12 | async-start | bytes 37748736 | tf_op jit(solution)/shard_map/all_gather | solution.py:129
  49.4 22.0 copy-start.44
  49.4 22.7 copy-start.7
  49.4 2432.5 %all-gather.23.cloned.1.call-start = ((), (), s32[]{:S(2)}) async-start(), calls=%async_computation.13 | async-start | bytes 37748736 | tf_op jit(solution)/shard_map/all_gather | solution.py:133
  50.2 2709.5 %reduce-scatter.12.cloned.1.call-start = ((), (), s32[]{:S(2)}) async-start(), calls=%async_computation.16 | async-start | bytes 9437184 | tf_op jit(solution)/shard_map/reduce_scatter | solution.py:245
  72.4 45.4 copy-start.40
  72.4 754.7 %copy-start.34 = (f32[256]{0:T(256)}, f32[256]{0:T(256)S(1)}, u32[]{:S(2)}) copy-start(f32[256]{0:T(256)S(1)} %fusion.122) | copy-start | bytes 3076
  119.6 707.5 %copy-start.26 = (f32[1,1,1,2048]{3,1,2,0:T(1,128)}, f32[1,1,1,2048]{3,1,2,0:T(1,128)S(1)}, u32[]{:S(2)}) copy-start(f32[1,1,1,2048]{3,1,2,0:T(1,128)S(1)} %get-tuple-element.78) | copy-start | bytes 24580
  119.6 707.4 %copy-start.28 = (f32[1,1,1,2048]{3,1,2,0:T(1,128)}, f32[1,1,1,2048]{3,1,2,0:T(1,128)S(1)}, u32[]{:S(2)}) copy-start(f32[1,1,1,2048]{3,1,2,0:T(1,128)S(1)} %get-tuple-element.77) | copy-start | bytes 24580
  119.6 1723.0 %copy-start.30 = (f32[1,1,1,2048]{3,1,2,0:T(1,128)}, f32[1,1,1,2048]{3,1,2,0:T(1,128)S(1)}, u32[]{:S(2)}) copy-start(f32[1,1,1,2048]{3,1,2,0:T(1,128)S(1)} %get-tuple-element.75) | copy-start | bytes 24580
  2573.5 302.8 %reduce-scatter.10.cloned.1.call-start = ((), (), s32[]{:S(2)}) async-start(), calls=%async_computation.15 | async-start | bytes 9437184 | tf_op jit(solution)/shard_map/reduce_scatter | solution.py:140
  2573.5 6.5 copy-start.11
  2573.5 6.5 copy-start.12
  2588.0 440.4 %reduce-scatter.16.cloned.1.call-start = ((), (), s32[]{:S(2)}) async-start(), calls=%async_computation.18 | async-start | bytes 9437184 | tf_op jit(solution)/shard_map/reduce_scatter | solution.py:251
  2596.4 717.4 %reduce-scatter.14.cloned.1.call-start = ((), (), s32[]{:S(2)}) async-start(), calls=%async_computation.17 | async-start | bytes 18874368 | tf_op jit(solution)/shard_map/reduce_scatter | solution.py:248
  2613.6 1107.4 %reduce-scatter.8.cloned.1.call-start = ((), (), s32[]{:S(2)}) async-start(), calls=%async_computation.14 | async-start | bytes 28311552 | tf_op jit(solution)/shard_map/reduce_scatter | solution.py:140
  2647.5 4.6 copy-start.29
  2667.0 1600.4 %reduce-scatter.20.cloned.1.call-start = ((), (), s32[]{:S(2)}) async-start(), calls=%async_computation.20 | async-start | bytes 37748736 | tf_op jit(solution)/shard_map/reduce_scatter | solution.py:205
  2686.2 2127.9 %reduce-scatter.18.cloned.1.call-start = ((), (), s32[]{:S(2)}) async-start(), calls=%async_computation.19 | async-start | bytes 37748736 | tf_op jit(solution)/shard_map/reduce_scatter | solution.py:140
  2703.8 2507.2 %all-reduce.8.cloned.1.call-start = ((), (), s32[]{:S(2)}) async-start(), calls=%async_computation.22 | async-start | bytes 46137344 | tf_op jit(solution)/shard_map/psum | solution.py:309
  2705.6 49.5 copy-start.39
  4814.1 27.1 copy-start.41
  5223.5 5.2 copy-start.13
  5223.5 9.7 slice-start
  5233.2 6.3 copy-start.1
  (31 other events, 76.4 us)
Sparse Core Ops, SparseCore 0:
  45.5 72.1 all-reduce.5
  120.1 226.6 all-gather.14
  348.4 478.6 all-gather.10
  829.3 125.0 all-gather.12
  956.6 123.1 all-gather.16
  1081.9 123.1 all-gather.18
  1206.7 635.8 all-gather.20
  1844.2 637.6 all-gather.22
  2573.6 149.0 reduce-scatter.11
  2726.7 149.5 reduce-scatter.9
  2880.3 148.0 reduce-scatter.15
  3032.0 281.7 reduce-scatter.13
  3318.2 402.7 reduce-scatter.7
  3725.2 542.2 reduce-scatter.19
  4271.6 542.4 reduce-scatter.17
  4818.1 392.7 all-reduce.7
where the time goes:
time: 5250 us
  waiting for transfers between devices  4740 us (90%)
  matrix products  312 us (6%)
  blocking collectives  112 us (2%)
    reduce_scatter x3, waiting for transfers between devices, share_rows(): lax.psum_scatter(row_term(jnp.int32(0), left.shape[1] // lax.axis_size('f...  1070 us
    all_gather x1, waiting for transfers between devices, fetch_cross(): lax.all_gather(up_weight, 'fsdp', axis=0, tiled=True)  630 us
    all_gather x1, waiting for transfers between devices, fetch_down(): return lax.all_gather(down_weight, 'fsdp', axis=0, tiled=True)  620 us
    reduce_scatter x1, waiting for transfers between devices, body(): lax.psum_scatter(row_term(jnp.int32(0), activated.shape[1] // lax.axis_si...  546 us
    all_gather x1, waiting for transfers between devices, fetch_self(): lax.all_gather(qkv_weight, 'fsdp', axis=0, tiled=True)  471 us
    psum x1, waiting for transfers between devices, body(): lax.psum(keyval_grad.astype(jnp.bfloat16), 'rep').astype(jnp.float32)  354 us
    reduce_scatter x1, waiting for transfers between devices, body(): lax.psum_scatter(keyval_term.astype(jnp.bfloat16), 'fsdp', scatter_dimens...  285 us
    all_gather x1, waiting for transfers between devices, fetch_cross(): lax.all_gather(keyval_weight, 'fsdp', axis=0, tiled=True)  227 us
  transfers between devices with their start and end apart: 16, of which 15 were waited for; matrix products, arithmetic and copies ran while one was open for 5% of the time, Pallas kernels for 0%

commit v1 on v0

v1 whole, which is shorter than its diff:
```python
import math

import jax
import jax.numpy as jnp
from jax import lax
from jax.sharding import PartitionSpec as P

HEADS = 16


EPSILON = 1e-06


def matmul(left, right):
    return jnp.dot(left, right, preferred_element_type=jnp.float32)


def outer_sum(left, right):
    return lax.dot_general(
        left, right, (((0,), (0,)), ((), ())), preferred_element_type=jnp.float32
    )


def back_product(left, right):
    return lax.dot_general(
        left, right, (((1,), (1,)), ((), ())), preferred_element_type=jnp.float32
    )


def normed(value):
    return value * lax.rsqrt(jnp.mean(value * value, axis=-1, keepdims=True) + EPSILON)


def normed_back(value, grad):
    return jax.vjp(normed, value)[1](grad)[0]


def smooth_gate(value):
    return jax.nn.gelu(value, approximate=True)


def attend(queries, keys, values, key_valid, score_scale):
    scores = (
        jnp.einsum("nqhd,nkhd->nhqk", queries, keys, preferred_element_type=jnp.float32)
        * score_scale
    )
    if key_valid is not None:
        scores = jnp.where(key_valid, scores, -jnp.inf)
    row_top = jnp.max(scores, axis=-1, keepdims=True)
    raised = jnp.exp(scores - row_top)
    totals = jnp.sum(raised, axis=-1, keepdims=True)
    weights = (raised / totals).astype(jnp.bfloat16)
    mixed_heads = jnp.einsum("nhqk,nkhd->nqhd", weights, values, preferred_element_type=jnp.float32)
    return (mixed_heads.astype(jnp.bfloat16), row_top + jnp.log(totals))


def attend_back(queries, keys, values, logsum, grad_mixed, key_valid, score_scale):
    scores = (
        jnp.einsum("nqhd,nkhd->nhqk", queries, keys, preferred_element_type=jnp.float32)
        * score_scale
    )
    if key_valid is not None:
        scores = jnp.where(key_valid, scores, -jnp.inf)
    weights = jnp.exp(scores - logsum)
    grad_weights = jnp.einsum(
        "nqhd,nkhd->nhqk", grad_mixed, values, preferred_element_type=jnp.float32
    )
    grad_values = jnp.einsum(
        "nhqk,nqhd->nkhd",
        weights.astype(jnp.bfloat16),
        grad_mixed,
        preferred_element_type=jnp.float32,
    )
    inner_sum = jnp.sum(weights * grad_weights, axis=-1, keepdims=True)
    grad_scores = (score_scale * (weights * (grad_weights - inner_sum))).astype(jnp.bfloat16)
    grad_queries = jnp.einsum(
        "nhqk,nkhd->nqhd", grad_scores, keys, preferred_element_type=jnp.float32
    )
    grad_keys = jnp.einsum(
        "nhqk,nqhd->nkhd", grad_scores, queries, preferred_element_type=jnp.float32
    )
    return (grad_queries, grad_keys, grad_values)


PEERS = 4


def swap(value, mask):
    return lax.ppermute(value, "rep", [(peer, peer ^ mask) for peer in range(PEERS)])


def group_rows(value):
    far = swap(value, 2)
    near = swap(value, 1)
    return jnp.concatenate([value, near, swap(far, 1), far], axis=0)


def group_sum(left, right, product):
    rows = left.shape[0] // PEERS
    sent = product(left[rows : 3 * rows], right).astype(jnp.bfloat16)
    got = swap(sent, 1)
    across = product(left[3 * rows :], right) + got[rows:].astype(jnp.float32)
    crossed = swap(across.astype(jnp.bfloat16), 2)
    own = product(left[:rows], right) + got[:rows].astype(jnp.float32)
    return own + crossed.astype(jnp.float32)


def body(
    image_tokens,
    text_tokens,
    text_lengths,
    timesteps,
    cotangent,
    mod_weight,
    qkv_weight,
    out_weight,
    query_weight,
    keyval_weight,
    merge_weight,
    cross_gain,
    up_weight,
    down_weight,
):
    images, length, width = image_tokens.shape
    text_count, text_width = text_tokens.shape[1:]
    group = lax.axis_size("fsdp")
    rank = lax.axis_index("rep")
    member = lax.axis_index("fsdp")
    heads = HEADS // PEERS
    head_width = width // HEADS
    part = width // PEERS
    score_scale = head_width ** (-0.5)
    shard_rows = mod_weight.shape[0]
    hidden = up_weight.shape[1]
    rows = images * length
    all_images = PEERS * images

    def gather(value):
        return lax.all_gather(value, "fsdp", axis=0, tiled=True)

    def scatter(value):
        return lax.psum_scatter(
            value.astype(jnp.bfloat16), "fsdp", scatter_dimension=0, tiled=True
        )

    def own_part(value, blocks):
        count = value.shape[1] // (blocks * PEERS)
        return lax.dynamic_index_in_dim(
            value.reshape(value.shape[0], blocks, PEERS, count), rank, 2, keepdims=False
        ).reshape(value.shape[0], blocks * count)

    def all_parts(value, blocks):
        count = value.shape[1] // blocks
        found = lax.all_gather(value.reshape(value.shape[0], blocks, count), "rep", axis=2)
        return found.reshape(value.shape[0], -1).astype(jnp.float32)

    def ordered(found):
        stacked = jnp.stack(found)
        return [
            lax.dynamic_index_in_dim(stacked, rank ^ place, 0, keepdims=False)
            for place in range(PEERS)
        ]

    def columns_to_rows(value):
        blocks = value.reshape(PEERS, part, -1)
        found = [
            lax.dynamic_index_in_dim(blocks, rank ^ mask, 0, keepdims=False)
            for mask in range(PEERS)
        ]
        found = [found[0]] + [swap(found[mask], mask) for mask in range(1, PEERS)]
        return jnp.concatenate(ordered(found), axis=1)

    def rows_to_columns(value):
        count = value.shape[1] // PEERS
        found = [
            lax.dynamic_slice_in_dim(value, (rank ^ mask) * count, count, 1)
            for mask in range(PEERS)
        ]
        found = [found[0]] + [swap(found[mask], mask) for mask in range(1, PEERS)]
        return jnp.concatenate(ordered(found), axis=0)

    half_width = width // 2
    all_steps = lax.all_gather(timesteps, ("rep", "fsdp"), axis=0, tiled=True)
    column = member * shard_rows + jnp.arange(shard_rows, dtype=jnp.int32)
    place = jnp.where(column < half_width, column, column - half_width)
    frequency = jnp.exp(-math.log(10000.0) * place.astype(jnp.float32) / half_width)
    angles = all_steps.astype(jnp.float32)[:, None] * frequency[None, :]
    cond_slice = jnp.where(column < half_width, jnp.sin(angles), jnp.cos(angles)).astype(
        jnp.bfloat16
    )
    cond_group = lax.dynamic_slice_in_dim(cond_slice, rank * group * images, group * images, 0)
    terms = matmul(cond_group, mod_weight)
    found = lax.all_to_all(
        terms.reshape(group, images, -1), "fsdp", split_axis=0, concat_axis=0, tiled=True
    )
    modulation = jnp.sum(found, axis=0)
    pieces = modulation.reshape(images, 6, 1, width)
    shift_self, scale_self, gate_self = (pieces[:, 0], pieces[:, 1], pieces[:, 2])
    shift_mlp, scale_mlp, gate_mlp = (pieces[:, 3], pieces[:, 4], pieces[:, 5])

    def flatten(value):
        return value.reshape(-1, value.shape[-1])

    def own_rows(value):
        return value.reshape(images, length, width)

    def split_heads(value):
        return value.reshape(all_images, -1, heads, head_width)

    qkv_part = gather(own_part(qkv_weight, 3))
    keyval_part = gather(own_part(keyval_weight, 2))
    out_part = columns_to_rows(gather(own_part(out_weight, 1)))
    gain_full = gather(cross_gain)
    query_part = gather(own_part(query_weight, 1))
    merge_part = columns_to_rows(gather(own_part(merge_weight, 1)))
    up_part = gather(own_part(up_weight, group))
    down_part = gather(
        lax.dynamic_index_in_dim(
            down_weight.reshape(PEERS, -1, width), rank, 0, keepdims=False
        )
    )

    residual = image_tokens.astype(jnp.float32)
    norm_one = normed(residual)
    act_one = group_rows(flatten(norm_one * (1.0 + scale_self) + shift_self).astype(jnp.bfloat16))
    text_all = group_rows(flatten(text_tokens))
    length_all = group_rows(text_lengths)
    qkv_act = matmul(act_one, qkv_part).astype(jnp.bfloat16)
    queries = split_heads(qkv_act[:, :part])
    keys_self = split_heads(qkv_act[:, part : 2 * part])
    values_self = split_heads(qkv_act[:, 2 * part :])
    mixed_self, logsum_self = attend(queries, keys_self, values_self, None, score_scale)
    mixed_flat = mixed_self.reshape(-1, part)
    branch_one = own_rows(group_sum(mixed_flat, out_part, matmul))
    hidden_one = residual + gate_self * branch_one

    norm_two = normed(hidden_one)
    act_two = group_rows(flatten(norm_two * gain_full).astype(jnp.bfloat16))
    cross_queries = split_heads(matmul(act_two, query_part).astype(jnp.bfloat16))
    keyval = matmul(text_all, keyval_part).astype(jnp.bfloat16)
    cross_keys = split_heads(keyval[:, :part])
    cross_values = split_heads(keyval[:, part:])
    key_valid = (jnp.arange(text_count, dtype=jnp.int32)[None, :] < length_all[:, None])[
        :, None, None, :
    ]
    mixed_cross, logsum_cross = attend(
        cross_queries, cross_keys, cross_values, key_valid, score_scale
    )
    cross_flat = mixed_cross.reshape(-1, part)
    hidden_two = hidden_one + own_rows(group_sum(cross_flat, merge_part, matmul))

    norm_three = normed(hidden_two)
    act_three = group_rows(
        flatten(norm_three * (1.0 + scale_mlp) + shift_mlp).astype(jnp.bfloat16)
    )
    pre_act = matmul(act_three, up_part)
    activated = smooth_gate(pre_act).astype(jnp.bfloat16)
    branch_three = own_rows(group_sum(activated, down_part, matmul))
    block_out = (hidden_two + gate_mlp * branch_three).astype(jnp.bfloat16)

    grad_block = cotangent.astype(jnp.float32)
    grad_gate_mlp = jnp.sum(grad_block * branch_three, axis=1)
    grad_three = group_rows(flatten(gate_mlp * grad_block).astype(jnp.bfloat16))
    grad_activated = back_product(grad_three, down_part)
    down_grad = scatter(outer_sum(activated, grad_three))
    grad_pre = jax.vjp(smooth_gate, pre_act)[1](grad_activated)[0].astype(jnp.bfloat16)
    up_grad = scatter(outer_sum(act_three, grad_pre))
    grad_act_three = own_rows(group_sum(grad_pre, up_part, back_product))
    grad_shift_mlp = jnp.sum(grad_act_three, axis=1)
    grad_scale_mlp = jnp.sum(grad_act_three * norm_three, axis=1)
    grad_two = grad_block + normed_back(hidden_two, grad_act_three * (1.0 + scale_mlp))

    grad_merge = group_rows(flatten(grad_two).astype(jnp.bfloat16))
    merge_grad = scatter(
        rows_to_columns(outer_sum(cross_flat, grad_merge).astype(jnp.bfloat16))
    )
    grad_mixed_cross = back_product(grad_merge, merge_part).astype(jnp.bfloat16)
    grad_cross_queries, grad_cross_keys, grad_cross_values = attend_back(
        cross_queries,
        cross_keys,
        cross_values,
        logsum_cross,
        split_heads(grad_mixed_cross),
        key_valid,
        score_scale,
    )
    grad_query = grad_cross_queries.reshape(-1, part).astype(jnp.bfloat16)
    grad_keyval = jnp.concatenate(
        [grad_cross_keys.reshape(-1, part), grad_cross_values.reshape(-1, part)], axis=1
    ).astype(jnp.bfloat16)
    query_grad = scatter(outer_sum(act_two, grad_query))
    keyval_grad = scatter(outer_sum(text_all, grad_keyval))
    text_grad = (
        group_sum(grad_keyval, keyval_part, back_product)
        .astype(jnp.bfloat16)
        .reshape(text_tokens.shape)
    )
    grad_act_two = own_rows(group_sum(grad_query, query_part, back_product))
    gain_term = jnp.sum(grad_act_two * norm_two, axis=1)
    grad_one = grad_two + normed_back(hidden_one, grad_act_two * gain_full)

    grad_gate_self = jnp.sum(grad_one * branch_one, axis=1)
    grad_out = group_rows(flatten(gate_self * grad_one).astype(jnp.bfloat16))
    out_grad = scatter(rows_to_columns(outer_sum(mixed_flat, grad_out).astype(jnp.bfloat16)))
    grad_mixed_self = back_product(grad_out, out_part).astype(jnp.bfloat16)
    grad_queries, grad_keys, grad_values = attend_back(
        queries,
        keys_self,
        values_self,
        logsum_self,
        split_heads(grad_mixed_self),
        None,
        score_scale,
    )
    grad_qkv = jnp.concatenate(
        [
            grad_queries.reshape(-1, part),
            grad_keys.reshape(-1, part),
            grad_values.reshape(-1, part),
        ],
        axis=1,
    ).astype(jnp.bfloat16)
    qkv_grad = scatter(outer_sum(act_one, grad_qkv))
    grad_act_one = own_rows(group_sum(grad_qkv, qkv_part, back_product))
    grad_shift_self = jnp.sum(grad_act_one, axis=1)
    grad_scale_self = jnp.sum(grad_act_one * norm_one, axis=1)
    image_grad = (grad_one + normed_back(residual, grad_act_one * (1.0 + scale_self))).astype(
        jnp.bfloat16
    )

    vectors = jnp.concatenate(
        [
            grad_shift_self,
            grad_scale_self,
            grad_gate_self,
            grad_shift_mlp,
            grad_scale_mlp,
            grad_gate_mlp,
            gain_term,
        ],
        axis=1,
    ).astype(jnp.bfloat16)
    all_vectors = lax.all_gather(vectors, ("rep", "fsdp"), axis=0, tiled=True)
    mod_grad = outer_sum(cond_slice, all_vectors[:, : 6 * width])
    gain_grad = jnp.sum(
        lax.dynamic_slice_in_dim(
            all_vectors, 6 * width + member * shard_rows, shard_rows, 1
        ).astype(jnp.float32),
        axis=0,
    )
    return (
        block_out,
        image_grad,
        text_grad,
        mod_grad,
        all_parts(qkv_grad, 3),
        all_parts(out_grad, 1),
        all_parts(query_grad, 1),
        all_parts(keyval_grad, 2),
        all_parts(merge_grad, 1),
        gain_grad,
        all_parts(up_grad, group),
        lax.all_gather(down_grad, "rep", axis=0, tiled=True).astype(jnp.float32),
    )


def solution(mesh):
    placed = (
        P(("rep", "fsdp"), None, None),
        P(("rep", "fsdp"), None, None),
        P(("rep", "fsdp")),
        P(("rep", "fsdp")),
        P(("rep", "fsdp"), None, None),
        P("fsdp", None),
        P("fsdp", None),
        P("fsdp", None),
        P("fsdp", None),
        P("fsdp", None),
        P("fsdp", None),
        P("fsdp"),
        P("fsdp", None),
        P("fsdp", None),
    )
    return jax.shard_map(
        body,
        mesh=mesh,
        in_specs=placed,
        out_specs=(
            P(("rep", "fsdp"), None, None),
            P(("rep", "fsdp"), None, None),
            P(("rep", "fsdp"), None, None),
            P("fsdp", None),
            P("fsdp", None),
            P("fsdp", None),
            P("fsdp", None),
            P("fsdp", None),
            P("fsdp", None),
            P("fsdp"),
            P("fsdp", None),
            P("fsdp", None),
        ),
        check_vma=False,
    )
```

time: 5250 us -> 1690 us (0.32)
  waiting for transfers between devices: 4740 us -> 1050 us
  local copies, waits for them, and re-layouts: 30.1 us -> 127 us
  matrix products: 312 us -> 255 us
    all_gather x7 -> x14, waiting for transfers between devices: 2280 us -> 238 us  [the longest x7 214 us: gather(): return lax.all_gather(value, 'fsdp', axis=0, tiled=True)]
    reduce_scatter x7, waiting for transfers between devices: 2050 us -> 459 us  [scatter(): lax.psum_scatter(value.astype(jnp.bfloat16), 'fsdp', scatter_dimension=0,...]
    psum x1 -> x0, waiting for transfers between devices: 354 us -> none  [body(): lax.psum(keyval_grad.astype(jnp.bfloat16), 'rep').astype(jnp.float32)]
    ppermute x0 -> x50, waiting for transfers between devices: none -> 327 us  [swap(): lax.ppermute(value, 'rep', [(peer, peer ^ mask) for peer in range(PEERS)])]
  transfers between devices with their start and end apart: 16 -> 72, of which waited for: 15 -> 37; matrix products, arithmetic and copies ran while one was open for 5% -> 21% of each run, Pallas kernels for 0% -> 0%
where the time goes in v1:
time: 1690 us; the launch traced here: 1680 us
  waiting for transfers between devices  1050 us (62%)
  matrix products  255 us (15%)
  blocking collectives  142 us (8%)
  local copies, waits for them, and re-layouts  127 us (8%)
  other arithmetic  56.8 us (3%)
  starting transfers between devices  39.7 us (2%)
  between operations  17.6 us (1%)
    reduce_scatter x7, waiting for transfers between devices, scatter(): lax.psum_scatter(value.astype(jnp.bfloat16), 'fsdp', scatter_dimension=0,...  459 us
    ppermute x50, waiting for transfers between devices, swap(): lax.ppermute(value, 'rep', [(peer, peer ^ mask) for peer in range(PEERS)])  327 us
    all_gather x7, waiting for transfers between devices, gather(): return lax.all_gather(value, 'fsdp', axis=0, tiled=True)  214 us
    all_gather x1, blocking collectives, body(): all_vectors = lax.all_gather(vectors, ('rep', 'fsdp'), axis=0, tiled=True)  79.5 us
    dot_general x15, matrix products, back_product(): lax.dot_general(left, right, (((1,), (1,)), ((), ())), preferred_element_...  76.6 us
    dot_general x14, matrix products, matmul(): return jnp.dot(left, right, preferred_element_type=jnp.float32)  67.5 us
    dot_general x8, matrix products, outer_sum(): lax.dot_general(left, right, (((0,), (0,)), ((), ())), preferred_element_...  67.2 us
    unnamed x215, local copies, waits for them, and re-layouts  53.2 us
  transfers between devices with their start and end apart: 72, of which 37 were waited for; matrix products, arithmetic and copies ran while one was open for 21% of the time, Pallas kernels for 0%

profile of v1, /device:TPU:0, one launch (start us, length us, event | category | flops | bytes accessed | tf_op | source)
XLA Modules:
  0.0 1683.9 jit_solution(2121736629988920858)
XLA Ops:
  31.1 43.6 %all-reduce = s32[32]{0:T(128)S(1)} all-reduce(s32[32]{0:T(128)S(1)} %dynamic-update-slice), channel_id=1, replica_groups=mesh['rep'=4,'fsdp'=8] {'rep','fsdp'}, use_global_device_ids=true, to_apply=%add | all-reduce | flops 32 | bytes 256
  87.6 21.7 %all-to-all-done = f32[8,1,12288]{2,1,0:T(1,128)S(1)} async-done(((f32[8,1,12288]{2,1,0:T(1,128)}), f32[8,1,12288]{2,1,0:T(1,128)S(1)}, u32[]{:S(2)}, u32[]{:S(2)}) %all-to-all-start) | async-done | bytes 393248 | tf_op jit(solution)/shard_map/all_to_all | solution.py:193
  112.5 15.8 collective-permute-done.1
  133.5 12.0 collective-permute-done.5
  145.5 11.5 collective-permute-done.4
  158.6 17.8 %all-gather.24.cloned.1.call-done = bf16[2048,1536]{0,1:T(8,128)(2,1)} async-done(((bf16[256,1536]{0,1:T(8,128)(2,1)}), bf16[2048,1536]{0,1:T(8,128)(2,1)}) %all-gather.24.cloned.1.call-update) | async-done | bytes 6291472 | tf_op jit(solution)/shard_map/all_gather | solution.py:139
  176.4 11.4 convolution_convert_fusion.3
  213.5 18.4 %all-gather.7 = bf16[8,1,256]{2,1,0:T(2,128)(2,1)S(1)} all-gather(bf16[1,1,256]{2,1,0:T(2,128)(2,1)S(1)} %reshape.573), channel_id=1, replica_groups=mesh['rep'=4,'fsdp'=8] {'fsdp'}, dimensions={0}, use_global_device_ids=true | all-gather | bytes 4608 | tf_op jit(solution)/shard_map/all_gather | solution.py:139
  245.6 33.8 %collective-permute-done.12 = s32[1]{0:T(128)} collective-permute-done((s32[1]{0:T(128)}, s32[1]{0:T(128)}, u32[]{:S(2)}, u32[]{:S(2)}) %collective-permute-start.12) | collective-permute-done | bytes 36 | tf_op jit(solution)/shard_map/ppermute | solution.py:89
  309.7 46.2 %all-gather.40.cloned.1.call-done = bf16[2048,1,1,512]{0,3,2,1:T(8,128)(2,1)} async-done(((bf16[256,1,1,512]{0,3,2,1:T(8,128)(2,1)}), bf16[2048,1,1,512]{0,3,2,1:T(8,128)(2,1)}) %all-gather.40.cloned.1.call-update) | async-done | bytes 2097168 | tf_op jit(solution)/shard_map/all_gather | solution.py:139
  375.7 23.0 %collective-permute-done.21 = bf16[256,2048]{1,0:T(8,128)(2,1)S(1)} collective-permute-done((bf16[256,2048]{1,0:T(8,128)(2,1)S(1)}, bf16[256,2048]{1,0:T(8,128)(2,1)S(1)}, u32[]{:S(2)}, u32[]{:S(2)}) %collective-permute-start.21) | collective-permute-done | bytes 1048608 | tf_op jit(solution)/shard_map/ppermute | solution.py:89
  403.9 23.2 %collective-permute-done.23 = bf16[256,2048]{1,0:T(8,128)(2,1)} collective-permute-done((bf16[256,2048]{1,0:T(8,128)(2,1)}, bf16[256,2048]{1,0:T(8,128)(2,1)}, u32[]{:S(2)}, u32[]{:S(2)}) %collective-permute-start.23) | collective-permute-done | bytes 1048608 | tf_op jit(solution)/shard_map/ppermute | solution.py:89
  427.6 20.3 %collective-permute-done.28 = bf16[256,2048]{1,0:T(8,128)(2,1)} collective-permute-done((bf16[256,2048]{1,0:T(8,128)(2,1)}, bf16[256,2048]{1,0:T(8,128)(2,1)}, u32[]{:S(2)}, u32[]{:S(2)}) %collective-permute-start.28) | collective-permute-done | bytes 1048608 | tf_op jit(solution)/shard_map/ppermute | solution.py:89
  447.9 34.0 %all-gather.28.cloned.1.call-done = bf16[2048,2048]{0,1:T(8,128)(2,1)} async-done(((bf16[256,2048]{0,1:T(8,128)(2,1)}), bf16[2048,2048]{0,1:T(8,128)(2,1)}) %all-gather.28.cloned.1.call-update) | async-done | bytes 8388624 | tf_op jit(solution)/shard_map/all_gather | solution.py:139
  481.9 18.4 %multiply_convert_fusion = (bf16[1024,2048]{1,0:T(8,128)(2,1)}, f32[1024,2048]{1,0:T(8,128)}) fusion(bf16[2048,2048]{0,1:T(8,128)(2,1)} %all-gather.28.cloned.1.call-done, bf16[256,2048]{1,0:T(8,128)(2,1)} %collective-permute-done.23, bf16[256,2048]{1,0:T(8,128)(2,1)} %collective-permute-done.24, bf16[256,2048]{1,0:T(8,128)(2,1)} %collective-permute-done.22, ...), kind=kOutput, calls=%fused_computation.20 | convolution fusion | flops 8625586176 | bytes 25165824 | tf_op jit(solution)/shard_map/dot_general | solution.py:15
  500.4 107.4 %all-gather.44.cloned.1.call-done = bf16[1,2048,2048]{2,1,0:T(8,128)(2,1)} async-done(((bf16[1,256,2048]{2,1,0:T(8,128)(2,1)}), bf16[1,2048,2048]{2,1,0:T(8,128)(2,1)}) %all-gather.44.cloned.1.call-update) | async-done | bytes 8388624 | tf_op jit(solution)/shard_map/all_gather | solution.py:139
  607.7 21.3 %fusion.8 = bf16[1024,2048]{1,0:T(8,128)(2,1)} fusion(f32[1024,2048]{1,0:T(8,128)} %get-tuple-element.122, bf16[1,2048,2048]{2,1,0:T(8,128)(2,1)} %all-gather.44.cloned.1.call-done, bf16[256,2048]{1,0:T(8,128)(2,1)} %collective-permute-done.28, bf16[256,2048]{1,0:T(8,128)(2,1)} %collective-permute-done.29, bf16[256,2048]{1,0:T(8,128)(2,1)} %collective-permute-done.27, ...), kind=kOutput, calls=%fused_computation.11 | convolution fusion | flops 8648654848 | bytes 25165824 | tf_op jit(solution)/shard_map/dot_general | solution.py:25
  657.8 19.1 %collective-permute-done.31 = bf16[256,2048]{1,0:T(8,128)(2,1)S(1)} collective-permute-done((bf16[256,2048]{1,0:T(8,128)(2,1)S(1)}, bf16[256,2048]{1,0:T(8,128)(2,1)S(1)}, u32[]{:S(2)}, u32[]{:S(2)}) %collective-permute-start.31) | collective-permute-done | bytes 1048608 | tf_op jit(solution)/shard_map/ppermute | solution.py:89
  679.3 19.2 %collective-permute-done.26 = bf16[256,2048]{1,0:T(8,128)(2,1)S(1)} collective-permute-done((bf16[256,2048]{1,0:T(8,128)(2,1)S(1)}, bf16[256,2048]{1,0:T(8,128)(2,1)S(1)}, u32[]{:S(2)}, u32[]{:S(2)}) %collective-permute-start.26) | collective-permute-done | bytes 1048608 | tf_op jit(solution)/shard_map/ppermute | solution.py:89
  703.0 22.8 %collective-permute-done.33 = bf16[256,2048]{1,0:T(8,128)(2,1)S(1)} collective-permute-done((bf16[256,2048]{1,0:T(8,128)(2,1)S(1)}, bf16[256,2048]{1,0:T(8,128)(2,1)S(1)}, u32[]{:S(2)}, u32[]{:S(2)}) %collective-permute-start.33) | collective-permute-done | bytes 1048608 | tf_op jit(solution)/shard_map/ppermute | solution.py:89
  791.1 24.2 %collective-permute-done.36 = bf16[256,2048]{1,0:T(8,128)(2,1)S(1)} collective-permute-done((bf16[256,2048]{1,0:T(8,128)(2,1)S(1)}, bf16[256,2048]{1,0:T(8,128)(2,1)S(1)}, u32[]{:S(2)}, u32[]{:S(2)}) %collective-permute-start.36) | collective-permute-done | bytes 1048608 | tf_op jit(solution)/shard_map/ppermute | solution.py:89
  826.9 21.4 %collective-permute-done.38 = bf16[256,2048]{1,0:T(8,128)(2,1)} collective-permute-done((bf16[256,2048]{1,0:T(8,128)(2,1)S(1)}, bf16[256,2048]{1,0:T(8,128)(2,1)}, u32[]{:S(2)}, u32[]{:S(2)}) %collective-permute-start.38) | collective-permute-done | bytes 1048608 | tf_op jit(solution)/shard_map/ppermute | solution.py:89
  889.5 11.7 collective-permute-done.45
  905.3 14.1 convolution_convert_fusion.1
  919.4 14.1 convolution_convert_fusion
  984.1 71.2 %reduce-scatter.10.cloned.1.call-done = bf16[256,512]{1,0:T(8,128)(2,1)} async-done(((bf16[2048,512]{1,0:T(8,128)(2,1)}), bf16[256,512]{1,0:T(8,128)(2,1)}) %reduce-scatter.10.cloned.1.call-update) | async-done | bytes 262160 | tf_op jit(solution)/shard_map/reduce_scatter | solution.py:142
  1055.4 152.5 %reduce-scatter.18.cloned.1.call-done = bf16[256,2048]{1,0:T(8,128)(2,1)} async-done(((bf16[2048,2048]{1,0:T(8,128)(2,1)}), bf16[256,2048]{1,0:T(8,128)(2,1)}) %reduce-scatter.18.cloned.1.call-update) | async-done | bytes 1048592 | tf_op jit(solution)/shard_map/reduce_scatter | solution.py:142
  1210.5 149.7 %reduce-scatter.20.cloned.1.call-done = bf16[256,2048]{1,0:T(8,128)(2,1)} async-done(((bf16[2048,2048]{1,0:T(8,128)(2,1)}), bf16[256,2048]{1,0:T(8,128)(2,1)}) %reduce-scatter.20.cloned.1.call-update) | async-done | bytes 1048592 | tf_op jit(solution)/shard_map/reduce_scatter | solution.py:142
  1397.0 14.7 collective-permute-done.41
  1414.9 84.9 %reduce-scatter.8.cloned.1.call-done = bf16[256,1536]{1,0:T(8,128)(2,1)} async-done(((bf16[2048,1536]{1,0:T(8,128)(2,1)}), bf16[256,1536]{1,0:T(8,128)(2,1)}) %reduce-scatter.8.cloned.1.call-update) | async-done | bytes 786448 | tf_op jit(solution)/shard_map/reduce_scatter | solution.py:142
  1504.4 79.5 %all-gather.8 = bf16[32,1,14336]{2,1,0:T(2,128)(2,1)S(1)} all-gather(bf16[1,1,14336]{2,1,0:T(2,128)(2,1)S(1)} %bitcast.368), channel_id=1, replica_groups=mesh['rep'=4,'fsdp'=8] {'rep','fsdp'}, dimensions={0}, use_global_device_ids=true | all-gather | bytes 946176 | tf_op jit(solution)/shard_map/all_gather | solution.py:343
  1640.2 23.6 %all-gather.30.cloned.1.call-done = bf16[256,3,4,512]{3,0,1,2:T(8,128)(2,1)} async-done(((bf16[256,3,1,512]{3,0,1,2:T(8,128)(2,1)}), bf16[256,3,4,512]{3,0,1,2:T(8,128)(2,1)}) %all-gather.30.cloned.1.call-update) | async-done | bytes 3145744 | tf_op jit(solution)/shard_map/all_gather | solution.py:154
  (510 shorter events, 463.9 us)
Async XLA Ops:
  7.2 121.1 %all-gather.38.cloned.1.call-start = ((), (), s32[]{:S(2)}) async-start(), calls=%async_computation.22 | async-start | bytes 2359296 | tf_op jit(solution)/shard_map/all_gather | solution.py:139
  9.5 166.9 %all-gather.24.cloned.1.call-start = ((), (), s32[]{:S(2)}) async-start(), calls=%async_computation.8 | async-start | bytes 7077888 | tf_op jit(solution)/shard_map/all_gather | solution.py:139
  13.7 218.3 %all-gather.42.cloned.1.call-start = ((), (), s32[]{:S(2)}) async-start(), calls=%async_computation.24 | async-start | bytes 2359296 | tf_op jit(solution)/shard_map/all_gather | solution.py:139
  16.0 288.1 %all-gather.26.cloned.1.call-start = ((), (), s32[]{:S(2)}) async-start(), calls=%async_computation.9 | async-start | bytes 4718592 | tf_op jit(solution)/shard_map/all_gather | solution.py:139
  20.2 335.6 %all-gather.40.cloned.1.call-start = ((), (), s32[]{:S(2)}) async-start(), calls=%async_computation.23 | async-start | bytes 2359296 | tf_op jit(solution)/shard_map/all_gather | solution.py:139
  21.6 460.4 %all-gather.28.cloned.1.call-start = ((), (), s32[]{:S(2)}) async-start(), calls=%async_computation.10 | async-start | bytes 9437184 | tf_op jit(solution)/shard_map/all_gather | solution.py:139
  86.4 521.4 %all-gather.44.cloned.1.call-start = ((), (), s32[]{:S(2)}) async-start(), calls=%async_computation.25 | async-start | bytes 9437184 | tf_op jit(solution)/shard_map/all_gather | solution.py:139
  112.5 46.1 %collective-permute-start = (bf16[256,2048]{1,0:T(8,128)(2,1)}, bf16[256,2048]{1,0:T(8,128)(2,1)}, u32[]{:S(2)}, u32[]{:S(2)}) collective-permute-start(bf16[256,2048]{1,0:T(8,128)(2,1)} %fusion.126), channel_id=1, source_target_pairs={{0,8},{8,0},{16,24},{24,16},{1,9},{9,1},{17,25},{25,17},{2,10},{10... | collective-permute-start | bytes 3145736 | tf_op jit(solution)/shard_map/ppermute | solution.py:89
  210.5 73.2 %collective-permute-start.9 = (bf16[128,2048]{1,0:T(8,128)(2,1)}, bf16[128,2048]{1,0:T(8,128)(2,1)}, u32[]{:S(2)}, u32[]{:S(2)}) collective-permute-start(bf16[128,2048]{1,0:T(8,128)(2,1)} %bitcast.24), channel_id=1, source_target_pairs={{0,16},{8,24},{16,0},{24,8},{1,17},{9,25},{17,1},{25,9},{2,18},{10... | collective-permute-start | bytes 1572872 | tf_op jit(solution)/shard_map/ppermute | solution.py:89
  213.4 720.8 %reduce-scatter.12.cloned.1.call-start = ((), (), s32[]{:S(2)}) async-start(), calls=%async_computation.14 | async-start | bytes 2359296 | tf_op jit(solution)/shard_map/reduce_scatter | solution.py:142
  241.8 52.3 %collective-permute-start.15 = (bf16[256,2048]{1,0:T(8,128)(2,1)}, bf16[256,2048]{1,0:T(8,128)(2,1)}, u32[]{:S(2)}, u32[]{:S(2)}) collective-permute-start(bf16[256,2048]{1,0:T(8,128)(2,1)} %fusion.122), channel_id=1, source_target_pairs={{0,16},{8,24},{16,0},{24,8},{1,17},{9,25},{17,1},{25,9},{2,18},{10... | collective-permute-start | bytes 3145736 | tf_op jit(solution)/shard_map/ppermute | solution.py:89
  294.0 61.9 %collective-permute-start.14 = (bf16[256,2048]{1,0:T(8,128)(2,1)}, bf16[256,2048]{1,0:T(8,128)(2,1)S(1)}, u32[]{:S(2)}, u32[]{:S(2)}) collective-permute-start(bf16[256,2048]{1,0:T(8,128)(2,1)} %fusion.122), channel_id=1, source_target_pairs={{0,8},{8,0},{16,24},{24,16},{1,9},{9,1},{17,25},{25,17},{2,10},{10... | collective-permute-start | bytes 3145736 | tf_op jit(solution)/shard_map/ppermute | solution.py:89
  294.1 62.7 %collective-permute-start.16 = (bf16[256,2048]{1,0:T(8,128)(2,1)}, bf16[256,2048]{1,0:T(8,128)(2,1)}, u32[]{:S(2)}, u32[]{:S(2)}) collective-permute-start(bf16[256,2048]{1,0:T(8,128)(2,1)} %collective-permute-done.15), channel_id=1, source_target_pairs={{0,8},{8,0},{16,24},{24,16},{1,9},{9,1},{17,25},{25,17},{2,10},{10... | collective-permute-start | bytes 3145736 | tf_op jit(solution)/shard_map/ppermute | solution.py:89
  403.3 44.6 %collective-permute-start.28 = (bf16[256,2048]{1,0:T(8,128)(2,1)}, bf16[256,2048]{1,0:T(8,128)(2,1)}, u32[]{:S(2)}, u32[]{:S(2)}) collective-permute-start(bf16[256,2048]{1,0:T(8,128)(2,1)} %fusion.125), channel_id=1, source_target_pairs={{0,16},{8,24},{16,0},{24,8},{1,17},{9,25},{17,1},{25,9},{2,18},{10... | collective-permute-start | bytes 3145736 | tf_op jit(solution)/shard_map/ppermute | solution.py:89
  403.9 78.0 %collective-permute-start.22 = (bf16[256,2048]{1,0:T(8,128)(2,1)}, bf16[256,2048]{1,0:T(8,128)(2,1)}, u32[]{:S(2)}, u32[]{:S(2)}) collective-permute-start(bf16[256,2048]{1,0:T(8,128)(2,1)} %fusion.123), channel_id=1, source_target_pairs={{0,8},{8,0},{16,24},{24,16},{1,9},{9,1},{17,25},{25,17},{2,10},{10... | collective-permute-start | bytes 3145736 | tf_op jit(solution)/shard_map/ppermute | solution.py:89
  427.1 54.9 %collective-permute-start.24 = (bf16[256,2048]{1,0:T(8,128)(2,1)}, bf16[256,2048]{1,0:T(8,128)(2,1)}, u32[]{:S(2)}, u32[]{:S(2)}) collective-permute-start(bf16[256,2048]{1,0:T(8,128)(2,1)} %collective-permute-done.23), channel_id=1, source_target_pairs={{0,8},{8,0},{16,24},{24,16},{1,9},{9,1},{17,25},{25,17},{2,10},{10... | collective-permute-start | bytes 3145736 | tf_op jit(solution)/shard_map/ppermute | solution.py:89
  427.1 73.3 %collective-permute-start.27 = (bf16[256,2048]{1,0:T(8,128)(2,1)}, bf16[256,2048]{1,0:T(8,128)(2,1)}, u32[]{:S(2)}, u32[]{:S(2)}) collective-permute-start(bf16[256,2048]{1,0:T(8,128)(2,1)} %fusion.125), channel_id=1, source_target_pairs={{0,8},{8,0},{16,24},{24,16},{1,9},{9,1},{17,25},{25,17},{2,10},{10... | collective-permute-start | bytes 3145736 | tf_op jit(solution)/shard_map/ppermute | solution.py:89
  447.9 52.4 %collective-permute-start.29 = (bf16[256,2048]{1,0:T(8,128)(2,1)}, bf16[256,2048]{1,0:T(8,128)(2,1)}, u32[]{:S(2)}, u32[]{:S(2)}) collective-permute-start(bf16[256,2048]{1,0:T(8,128)(2,1)} %collective-permute-done.28), channel_id=1, source_target_pairs={{0,8},{8,0},{16,24},{24,16},{1,9},{9,1},{17,25},{25,17},{2,10},{10... | collective-permute-start | bytes 3145736 | tf_op jit(solution)/shard_map/ppermute | solution.py:89
  654.8 43.7 %collective-permute-start.26 = (bf16[256,2048]{1,0:T(8,128)(2,1)S(1)}, bf16[256,2048]{1,0:T(8,128)(2,1)S(1)}, u32[]{:S(2)}, u32[]{:S(2)}) collective-permute-start(bf16[256,2048]{1,0:T(8,128)(2,1)S(1)} %add_convert_fusion.3), channel_id=1, source_target_pairs={{0,16},{8,24},{16,0},{24,8},{1,17},{9,25},{17,1},{25,9},{2,18},{10... | collective-permute-start | bytes 3145736 | tf_op jit(solution)/shard_map/ppermute | solution.py:89
  755.3 225.5 %reduce-scatter.14.cloned.1.call-start = ((), (), s32[]{:S(2)}) async-start(), calls=%async_computation.15 | async-start | bytes 4718592 | tf_op jit(solution)/shard_map/reduce_scatter | solution.py:142
  785.3 198.8 %reduce-scatter.16.cloned.1.call-start = ((), (), s32[]{:S(2)}) async-start(), calls=%async_computation.17 | async-start | bytes 2359296 | tf_op jit(solution)/shard_map/reduce_scatter | solution.py:142
  903.3 152.0 %reduce-scatter.10.cloned.1.call-start = ((), (), s32[]{:S(2)}) async-start(), calls=%async_computation.13 | async-start | bytes 2359296 | tf_op jit(solution)/shard_map/reduce_scatter | solution.py:142
  904.8 303.1 %reduce-scatter.18.cloned.1.call-start = ((), (), s32[]{:S(2)}) async-start(), calls=%async_computation.18 | async-start | bytes 9437184 | tf_op jit(solution)/shard_map/reduce_scatter | solution.py:142
  919.4 440.7 %reduce-scatter.20.cloned.1.call-start = ((), (), s32[]{:S(2)}) async-start(), calls=%async_computation.20 | async-start | bytes 9437184 | tf_op jit(solution)/shard_map/reduce_scatter | solution.py:142
  933.6 460.5 %all-gather.48.cloned.1.call-start = ((), (), s32[]{:S(2)}) async-start(), calls=%async_computation.27 | async-start | bytes 1310720 | tf_op jit(solution)/shard_map/all_gather | solution.py:154
  934.3 565.5 %reduce-scatter.8.cloned.1.call-start = ((), (), s32[]{:S(2)}) async-start(), calls=%async_computation.11 | async-start | bytes 7077888 | tf_op jit(solution)/shard_map/reduce_scatter | solution.py:142
  980.7 612.8 %all-gather.32.cloned.1.call-start = ((), (), s32[]{:S(2)}) async-start(), calls=%async_computation.16 | async-start | bytes 2621440 | tf_op jit(solution)/shard_map/all_gather | solution.py:154
  983.1 621.3 %all-gather.50.cloned.1.call-start = ((), (), s32[]{:S(2)}) async-start(), calls=%async_computation.28 | async-start | bytes 1310720 | tf_op jit(solution)/shard_map/all_gather | solution.py:154
  984.1 623.2 %all-gather.46.cloned.1.call-start = ((), (), s32[]{:S(2)}) async-start(), calls=%async_computation.26 | async-start | bytes 1310720 | tf_op jit(solution)/shard_map/all_gather | solution.py:154
  1055.4 555.0 %all-gather.34.cloned.1.call-start = ((), (), s32[]{:S(2)}) async-start(), calls=%async_computation.19 | async-start | bytes 5242880 | tf_op jit(solution)/shard_map/all_gather | solution.py:154
  1210.4 423.1 %all-gather.36.cloned.1.call-start = ((), (), s32[]{:S(2)}) async-start(), calls=%async_computation.21 | async-start | bytes 5242880 | tf_op jit(solution)/shard_map/all_gather | solution.py:363
  1360.2 303.6 %all-gather.30.cloned.1.call-start = ((), (), s32[]{:S(2)}) async-start(), calls=%async_computation.12 | async-start | bytes 3932160 | tf_op jit(solution)/shard_map/all_gather | solution.py:154
  (136 other events, 2216.7 us)
Sparse Core Ops, SparseCore 0:
  10.6 54.2 all-gather.37
  67.5 108.8 all-gather.23
  179.0 49.3 all-gather.41
  230.9 73.1 all-gather.25
  306.6 49.2 all-gather.39
  358.3 123.5 all-gather.27
  484.6 123.0 all-gather.43
  755.4 66.1 reduce-scatter.11
  825.2 86.8 reduce-scatter.13
  916.4 67.6 reduce-scatter.15
  988.6 66.6 reduce-scatter.9
  1059.8 148.0 reduce-scatter.17
  1212.1 147.9 reduce-scatter.19
  1361.6 15.7 all-gather.47
  1381.8 117.9 reduce-scatter.7
  1501.3 21.7 all-gather.31
  1524.5 17.6 all-gather.49
  1543.7 16.7 all-gather.45
  1562.7 34.7 all-gather.33
  1599.0 34.4 all-gather.35
  1635.2 28.5 all-gather.29

commit v2 on v1

v2 whole, which is shorter than its diff:
```python
import math

import jax
import jax.numpy as jnp
from jax import lax
from jax.experimental import pallas as pl
from jax.experimental.pallas import tpu as pltpu
from jax.sharding import PartitionSpec as P

HEADS = 16


EPSILON = 1e-06


def matmul(left, right):
    return jnp.dot(left, right, preferred_element_type=jnp.float32)


def outer_sum(left, right):
    return lax.dot_general(
        left, right, (((0,), (0,)), ((), ())), preferred_element_type=jnp.float32
    )


def back_product(left, right):
    return lax.dot_general(
        left, right, (((1,), (1,)), ((), ())), preferred_element_type=jnp.float32
    )


def normed(value):
    return value * lax.rsqrt(jnp.mean(value * value, axis=-1, keepdims=True) + EPSILON)


def normed_back(value, grad):
    return jax.vjp(normed, value)[1](grad)[0]


def smooth_gate(value):
    return jax.nn.gelu(value, approximate=True)


def row_block(rows, columns, column=0):
    return pl.BlockSpec((rows, columns), lambda image, *_: (image, column))


def parts_of(value, count):
    width = value.shape[1] // count
    return [value[:, i * width : (i + 1) * width] for i in range(count)]


def scores_of(queries, keys, limit, scale):
    scores = back_product(queries, keys) * scale
    if limit is not None:
        slot = lax.broadcasted_iota(jnp.int32, scores.shape, 1)
        scores = jnp.where(slot < limit, scores, -jnp.inf)
    return scores


def attend_heads(queries, keys, values, limit, scale, mixed_ref, logsum_ref):
    head_width = keys[0].shape[1]
    for head, (query, key, value) in enumerate(zip(queries, keys, values)):
        scores = scores_of(query, key, limit, scale)
        row_top = jnp.max(scores, axis=1, keepdims=True)
        raised = jnp.exp(scores - row_top)
        totals = jnp.sum(raised, axis=1, keepdims=True)
        weights = (raised / totals).astype(jnp.bfloat16)
        mixed_ref[:, head * head_width : (head + 1) * head_width] = matmul(weights, value).astype(
            jnp.bfloat16
        )
        logsum_ref[:, head : head + 1] = row_top + jnp.log(totals)


def attend_heads_back(queries, keys, values, limit, scale, logsum_ref, grads, outs):
    grad_query_ref, grad_key_ref, grad_value_ref = outs
    for head, (query, key, value, grad) in enumerate(zip(queries, keys, values, grads)):
        scores = scores_of(query, key, limit, scale)
        weights = jnp.exp(scores - logsum_ref[:, head : head + 1])
        grad_weights = back_product(grad, value)
        grad_value_ref(head, outer_sum(weights.astype(jnp.bfloat16), grad))
        inner_sum = jnp.sum(weights * grad_weights, axis=1, keepdims=True)
        grad_scores = (scale * (weights * (grad_weights - inner_sum))).astype(jnp.bfloat16)
        grad_query_ref(head, matmul(grad_scores, key))
        grad_key_ref(head, outer_sum(grad_scores, query))


def head_writer(ref, first, width):
    def write(head, value):
        start = first + head * width
        ref[:, start : start + width] = value.astype(jnp.bfloat16)

    return write


VMEM_LIMIT = 48 * 1024 * 1024


def attention_cost(images, length, slots, heads, width, products):
    pairs = images * heads * length * slots
    return pl.CostEstimate(
        flops=2 * products * pairs * width, bytes_accessed=8 * pairs, transcendentals=pairs
    )


def attend_self(qkv, images, heads, scale):
    rows, columns = qkv.shape
    length, part = rows // images, columns // 3

    def kernel(qkv_ref, mixed_ref, logsum_ref):
        blocks = parts_of(qkv_ref, 3 * heads)
        attend_heads(
            blocks[:heads],
            blocks[heads : 2 * heads],
            blocks[2 * heads :],
            None,
            scale,
            mixed_ref,
            logsum_ref,
        )

    return pl.pallas_call(
        kernel,
        grid=(images,),
        in_specs=[row_block(length, columns)],
        out_specs=[row_block(length, part), row_block(length, heads)],
        out_shape=[
            jax.ShapeDtypeStruct((rows, part), jnp.bfloat16),
            jax.ShapeDtypeStruct((rows, heads), jnp.float32),
        ],
        compiler_params=pltpu.CompilerParams(vmem_limit_bytes=VMEM_LIMIT),
        cost_estimate=attention_cost(images, length, length, heads, part // heads, 2),
        name="attend_self",
    )(qkv)


def attend_self_back(qkv, logsum, grad_mixed, images, heads, scale):
    rows, columns = qkv.shape
    length, part = rows // images, columns // 3

    def kernel(qkv_ref, logsum_ref, grad_ref, out_ref):
        blocks = parts_of(qkv_ref, 3 * heads)
        writers = [head_writer(out_ref, i * part, part // heads) for i in range(3)]
        attend_heads_back(
            blocks[:heads],
            blocks[heads : 2 * heads],
            blocks[2 * heads :],
            None,
            scale,
            logsum_ref,
            parts_of(grad_ref, heads),
            writers,
        )

    return pl.pallas_call(
        kernel,
        grid=(images,),
        in_specs=[row_block(length, columns), row_block(length, heads), row_block(length, part)],
        out_specs=row_block(length, columns),
        out_shape=jax.ShapeDtypeStruct((rows, columns), jnp.bfloat16),
        compiler_params=pltpu.CompilerParams(vmem_limit_bytes=VMEM_LIMIT),
        cost_estimate=attention_cost(images, length, length, heads, part // heads, 5),
        name="attend_self_back",
    )(qkv, logsum, grad_mixed)


def attend_cross(queries, keyval, limits, images, heads, scale):
    rows, part = queries.shape
    length, slots = rows // images, keyval.shape[0] // images

    def kernel(limits_ref, query_ref, keyval_ref, mixed_ref, logsum_ref):
        blocks = parts_of(keyval_ref, 2 * heads)
        attend_heads(
            parts_of(query_ref, heads),
            blocks[:heads],
            blocks[heads:],
            limits_ref[pl.program_id(0)],
            scale,
            mixed_ref,
            logsum_ref,
        )

    return pl.pallas_call(
        kernel,
        grid_spec=pltpu.PrefetchScalarGridSpec(
            num_scalar_prefetch=1,
            grid=(images,),
            in_specs=[row_block(length, part), row_block(slots, 2 * part)],
            out_specs=[row_block(length, part), row_block(length, heads)],
        ),
        out_shape=[
            jax.ShapeDtypeStruct((rows, part), jnp.bfloat16),
            jax.ShapeDtypeStruct((rows, heads), jnp.float32),
        ],
        compiler_params=pltpu.CompilerParams(vmem_limit_bytes=VMEM_LIMIT),
        cost_estimate=attention_cost(images, length, slots, heads, part // heads, 2),
        name="attend_cross",
    )(limits, queries, keyval)


def attend_cross_back(queries, keyval, limits, logsum, grad_mixed, images, heads, scale):
    rows, part = queries.shape
    length, slots = rows // images, keyval.shape[0] // images

    def kernel(limits_ref, query_ref, keyval_ref, logsum_ref, grad_ref, out_ref, text_ref):
        blocks = parts_of(keyval_ref, 2 * heads)
        width = part // heads
        attend_heads_back(
            parts_of(query_ref, heads),
            blocks[:heads],
            blocks[heads:],
            limits_ref[pl.program_id(0)],
            scale,
            logsum_ref,
            parts_of(grad_ref, heads),
            [
                head_writer(out_ref, 0, width),
                head_writer(text_ref, 0, width),
                head_writer(text_ref, part, width),
            ],
        )

    return pl.pallas_call(
        kernel,
        grid_spec=pltpu.PrefetchScalarGridSpec(
            num_scalar_prefetch=1,
            grid=(images,),
            in_specs=[
                row_block(length, part),
                row_block(slots, 2 * part),
                row_block(length, heads),
                row_block(length, part),
            ],
            out_specs=[row_block(length, part), row_block(slots, 2 * part)],
        ),
        out_shape=[
            jax.ShapeDtypeStruct((rows, part), jnp.bfloat16),
            jax.ShapeDtypeStruct((images * slots, 2 * part), jnp.bfloat16),
        ],
        compiler_params=pltpu.CompilerParams(vmem_limit_bytes=VMEM_LIMIT),
        cost_estimate=attention_cost(images, length, slots, heads, part // heads, 5),
        name="attend_cross_back",
    )(limits, queries, keyval, logsum, grad_mixed)


def pick_blocks(weights, counts, rank):
    rows = weights[0].shape[0]
    width = weights[0].shape[1] // (counts[0] * PEERS)
    firsts = [sum(counts[:i]) for i in range(len(counts))]

    def kernel(rank_ref, *refs):
        step = pl.program_id(0)
        out_ref = refs[-1]
        for ref, first, count in zip(refs, firsts, counts):

            @pl.when((step >= first) & (step < first + count))
            def _():
                out_ref[...] = ref[...]

    def spec(first, count):
        return pl.BlockSpec(
            (rows, width),
            lambda step, rank_ref: (
                0,
                jnp.clip(step - first, 0, count - 1) * PEERS + rank_ref[0],
            ),
        )

    return pl.pallas_call(
        kernel,
        grid_spec=pltpu.PrefetchScalarGridSpec(
            num_scalar_prefetch=1,
            grid=(sum(counts),),
            in_specs=[spec(first, count) for first, count in zip(firsts, counts)],
            out_specs=pl.BlockSpec((rows, width), lambda step, rank_ref: (0, step)),
        ),
        out_shape=jax.ShapeDtypeStruct((rows, width * sum(counts)), weights[0].dtype),
        name="pick_blocks",
    )(rank.reshape(1), *weights)


def spread_blocks(found, first, count, width):
    rows = found.shape[1]

    def kernel(found_ref, out_ref):
        out_ref[...] = found_ref[...].astype(jnp.float32)

    return pl.pallas_call(
        kernel,
        grid=(count, PEERS),
        in_specs=[
            pl.BlockSpec((None, rows, width), lambda block, peer: (peer, 0, first + block))
        ],
        out_specs=pl.BlockSpec((rows, width), lambda block, peer: (0, block * PEERS + peer)),
        out_shape=jax.ShapeDtypeStruct((rows, count * PEERS * width), jnp.float32),
        name="spread_blocks",
    )(found)


PEERS = 4


def swap(value, mask):
    return lax.ppermute(value, "rep", [(peer, peer ^ mask) for peer in range(PEERS)])


def group_rows(value):
    far = swap(value, 2)
    near = swap(value, 1)
    return jnp.concatenate([value, near, swap(far, 1), far], axis=0)


def group_sum(left, right, product):
    rows = left.shape[0] // PEERS
    sent = product(left[rows : 3 * rows], right).astype(jnp.bfloat16)
    got = swap(sent, 1)
    across = product(left[3 * rows :], right) + got[rows:].astype(jnp.float32)
    crossed = swap(across.astype(jnp.bfloat16), 2)
    own = product(left[:rows], right) + got[:rows].astype(jnp.float32)
    return own + crossed.astype(jnp.float32)


def ring_member(place, size):
    place = place % size
    return jnp.where(place < size // 2, 2 * place, 2 * (size - 1 - place) + 1)


def ring_pairs(size, step):
    order = [2 * i for i in range(size // 2)] + [2 * i + 1 for i in reversed(range(size // 2))]
    return [(order[i], order[(i + step) % size]) for i in range(size)]


def after(value, earlier):
    return lax.optimization_barrier((value, earlier))[0]


def ring_gather(value, size):
    rows = value.shape[0] // 2
    onward, back = [value[:rows]], [value[rows:]]
    for _ in range(size - 1):
        onward.append(lax.ppermute(onward[-1], "fsdp", ring_pairs(size, 1)))
        back.append(lax.ppermute(back[-1], "fsdp", ring_pairs(size, -1)))
    return onward, back


def lay_out(onward, back, starts, widths):
    size = len(onward)
    rows = onward[0].shape[0]
    total = 2 * size * rows
    count = len(widths)
    edges = [sum(widths[:i]) for i in range(count)]

    def kernel(*refs):
        starts_ref, halves, outs = refs[0], refs[1 : 1 + 2 * size], refs[1 + 2 * size : -1]
        done = refs[-1]
        copies = []
        for i, half in enumerate(halves):
            start = pl.multiple_of(starts_ref[i], rows)
            for j, out in enumerate(outs):
                copies.append(
                    pltpu.make_async_copy(
                        half.at[:, edges[j] : edges[j] + widths[j]],
                        out.at[pl.ds(start, rows), :],
                        done.at[i, j],
                    )
                )
        for copy in copies:
            copy.start()
        for copy in copies:
            copy.wait()

    return pl.pallas_call(
        kernel,
        out_shape=[jax.ShapeDtypeStruct((total, w), onward[0].dtype) for w in widths],
        in_specs=[pl.BlockSpec(memory_space=pltpu.SMEM)]
        + [pl.BlockSpec(memory_space=pltpu.VMEM)] * (2 * size),
        out_specs=[pl.BlockSpec(memory_space=pl.ANY)] * count,
        scratch_shapes=[pltpu.SemaphoreType.DMA((2 * size, count))],
        compiler_params=pltpu.CompilerParams(vmem_limit_bytes=VMEM_LIMIT),
        cost_estimate=pl.CostEstimate(
            flops=0, bytes_accessed=4 * total * sum(widths), transcendentals=0
        ),
        name="lay_out",
    )(starts, *onward, *back)


def ring_scatter(values, size, place, shard_rows):
    half = shard_rows // 2

    def piece(offset, lower):
        start = ring_member(place + offset, size) * shard_rows + (half if lower else 0)
        return jnp.concatenate(
            [lax.dynamic_slice_in_dim(v, start, half, 0) for v in values], axis=1
        )

    onward, back = piece(-1, False), piece(1, True)
    for step in range(1, size):
        onward = lax.ppermute(onward, "fsdp", ring_pairs(size, 1))
        back = lax.ppermute(back, "fsdp", ring_pairs(size, -1))
        mine_onward, mine_back = piece(-step - 1, False), piece(step + 1, True)
        onward = (onward.astype(jnp.float32) + mine_onward.astype(jnp.float32)).astype(jnp.bfloat16)
        back = (back.astype(jnp.float32) + mine_back.astype(jnp.float32)).astype(jnp.bfloat16)
    return jnp.concatenate([onward, back], axis=0)


def exchange(value, size):
    value = value[None]
    member = lax.axis_index("fsdp")
    mask = 1
    while mask < size:
        other = lax.ppermute(value, "fsdp", [(i, i ^ mask) for i in range(size)])
        low = (member & mask) == 0
        value = jnp.concatenate(
            [jnp.where(low, value, other), jnp.where(low, other, value)], axis=0
        )
        mask *= 2
    return value


def everyone(value, size):
    mask = size // 2
    while mask:
        pairs = [(i, i ^ mask) for i in range(size)]
        value = jnp.concatenate([value, lax.ppermute(value, "fsdp", pairs)], axis=0)
        mask //= 2
    value = jnp.concatenate([value, swap(value, 2)], axis=0)
    return jnp.concatenate([value, swap(value, 1)], axis=0)


def body(
    image_tokens,
    text_tokens,
    text_lengths,
    timesteps,
    cotangent,
    mod_weight,
    qkv_weight,
    out_weight,
    query_weight,
    keyval_weight,
    merge_weight,
    cross_gain,
    up_weight,
    down_weight,
):
    images, length, width = image_tokens.shape
    text_count, text_width = text_tokens.shape[1:]
    group = lax.axis_size("fsdp")
    rank = lax.axis_index("rep")
    member = lax.axis_index("fsdp")
    heads = HEADS // PEERS
    head_width = width // HEADS
    part = width // PEERS
    score_scale = head_width ** (-0.5)
    shard_rows = mod_weight.shape[0]
    hidden = up_weight.shape[1]
    rows = images * length
    all_images = PEERS * images

    def scatter(*values):
        return ring_scatter(
            [value.astype(jnp.bfloat16) for value in values],
            group,
            spot,
            values[0].shape[0] // group,
        )

    def own_part(value, blocks):
        count = value.shape[1] // (blocks * PEERS)
        return lax.dynamic_index_in_dim(
            value.reshape(value.shape[0], blocks, PEERS, count), rank, 2, keepdims=False
        ).reshape(value.shape[0], blocks * count)

    def ordered(found):
        stacked = jnp.stack(found)
        return [
            lax.dynamic_index_in_dim(stacked, rank ^ place, 0, keepdims=False)
            for place in range(PEERS)
        ]

    def columns_to_rows(value):
        blocks = value.reshape(PEERS, part, -1)
        found = [
            lax.dynamic_index_in_dim(blocks, rank ^ mask, 0, keepdims=False)
            for mask in range(PEERS)
        ]
        found = [found[0]] + [swap(found[mask], mask) for mask in range(1, PEERS)]
        return jnp.concatenate(ordered(found), axis=1)

    def rows_to_columns(value):
        count = value.shape[1] // PEERS
        found = [
            lax.dynamic_slice_in_dim(value, (rank ^ mask) * count, count, 1)
            for mask in range(PEERS)
        ]
        found = [found[0]] + [swap(found[mask], mask) for mask in range(1, PEERS)]
        return jnp.concatenate(ordered(found), axis=0)

    half_width = width // 2
    group_steps = exchange(timesteps, group).reshape(-1)
    all_steps = everyone(timesteps.reshape(images, 1), group).reshape(-1)
    gain_full = exchange(cross_gain.reshape(1, -1), group).reshape(-1)
    column = member * shard_rows + jnp.arange(shard_rows, dtype=jnp.int32)
    place = jnp.where(column < half_width, column, column - half_width)
    frequency = jnp.exp(-math.log(10000.0) * place.astype(jnp.float32) / half_width)

    def conditions(steps):
        angles = steps.astype(jnp.float32)[:, None] * frequency[None, :]
        return jnp.where(column < half_width, jnp.sin(angles), jnp.cos(angles)).astype(
            jnp.bfloat16
        )

    cond_group = conditions(group_steps)
    terms = matmul(cond_group, mod_weight)
    found = lax.all_to_all(
        terms.reshape(group, images, -1), "fsdp", split_axis=0, concat_axis=0, tiled=True
    )
    modulation = jnp.sum(found, axis=0)
    pieces = modulation.reshape(images, 6, 1, width)
    shift_self, scale_self, gate_self = (pieces[:, 0], pieces[:, 1], pieces[:, 2])
    shift_mlp, scale_mlp, gate_mlp = (pieces[:, 3], pieces[:, 4], pieces[:, 5])

    def flatten(value):
        return value.reshape(-1, value.shape[-1])

    def own_rows(value):
        return value.reshape(images, length, width)

    aligned = hidden // (group * PEERS) % 128 == 0
    spot = jnp.where(member % 2 == 0, member // 2, group - 1 - member // 2)
    starts = jnp.stack(
        [ring_member(spot - k, group) * shard_rows for k in range(group)]
        + [ring_member(spot + k, group) * shard_rows + shard_rows // 2 for k in range(group)]
    ).astype(jnp.int32)
    down_rows = down_weight.shape[0] // PEERS
    down_starts = starts // shard_rows * down_rows + starts % shard_rows // (shard_rows // 2) * (
        down_rows // 2
    )

    def gather(value, widths, begin, earlier):
        if earlier is not None:
            value = after(value, (earlier[0][-3], earlier[1][-3]))
        pieces_found = ring_gather(value, group)
        return lay_out(*pieces_found, begin, widths), pieces_found

    (qkv_part, out_part), ring = gather(
        pick_blocks([qkv_weight, out_weight], [3, 1], rank),
        [3 * part, part],
        starts,
        None,
    )
    (query_part, keyval_part, merge_part), ring = gather(
        pick_blocks([query_weight, keyval_weight, merge_weight], [1, 2, 1], rank),
        [part, 2 * part, part],
        starts,
        ring,
    )
    (up_part,), ring = gather(
        pick_blocks([up_weight], [group], rank) if aligned else own_part(up_weight, group),
        [hidden // PEERS],
        starts,
        ring,
    )
    (down_part,), ring = gather(
        lax.dynamic_index_in_dim(
            down_weight.reshape(PEERS, -1, width), rank, 0, keepdims=False
        ),
        [width],
        down_starts,
        ring,
    )
    out_part = columns_to_rows(out_part)
    merge_part = columns_to_rows(merge_part)

    residual = image_tokens.astype(jnp.float32)
    norm_one = normed(residual)
    act_one = group_rows(flatten(norm_one * (1.0 + scale_self) + shift_self).astype(jnp.bfloat16))
    text_all = group_rows(flatten(text_tokens))
    length_all = group_rows(text_lengths)
    qkv_act = matmul(act_one, qkv_part).astype(jnp.bfloat16)
    mixed_flat, logsum_self = attend_self(qkv_act, all_images, heads, score_scale)
    branch_one = own_rows(group_sum(mixed_flat, out_part, matmul))
    hidden_one = residual + gate_self * branch_one

    norm_two = normed(hidden_one)
    act_two = group_rows(flatten(norm_two * gain_full).astype(jnp.bfloat16))
    cross_queries = matmul(act_two, query_part).astype(jnp.bfloat16)
    keyval = matmul(text_all, keyval_part).astype(jnp.bfloat16)
    cross_flat, logsum_cross = attend_cross(
        cross_queries, keyval, length_all, all_images, heads, score_scale
    )
    hidden_two = hidden_one + own_rows(group_sum(cross_flat, merge_part, matmul))

    norm_three = normed(hidden_two)
    act_three = group_rows(
        flatten(norm_three * (1.0 + scale_mlp) + shift_mlp).astype(jnp.bfloat16)
    )
    pre_act = matmul(act_three, up_part)
    activated, slope_back = jax.vjp(smooth_gate, pre_act)
    activated, slope = lax.optimization_barrier(
        (
            activated.astype(jnp.bfloat16),
            slope_back(jnp.ones_like(pre_act))[0].astype(jnp.bfloat16),
        )
    )
    branch_three = own_rows(group_sum(activated, down_part, matmul))
    block_out = (hidden_two + gate_mlp * branch_three).astype(jnp.bfloat16)

    grad_block = cotangent.astype(jnp.float32)
    grad_gate_mlp = jnp.sum(grad_block * branch_three, axis=1)
    grad_three = group_rows(flatten(gate_mlp * grad_block).astype(jnp.bfloat16))
    grad_activated = back_product(grad_three, down_part)
    grad_pre = (grad_activated * slope.astype(jnp.float32)).astype(jnp.bfloat16)
    mlp_grads = scatter(outer_sum(activated, grad_three), outer_sum(act_three, grad_pre))
    grad_act_three = own_rows(group_sum(grad_pre, up_part, back_product))
    grad_shift_mlp = jnp.sum(grad_act_three, axis=1)
    grad_scale_mlp = jnp.sum(grad_act_three * norm_three, axis=1)
    grad_two = grad_block + normed_back(hidden_two, grad_act_three * (1.0 + scale_mlp))

    grad_merge = group_rows(flatten(grad_two).astype(jnp.bfloat16))
    merge_term = rows_to_columns(outer_sum(cross_flat, grad_merge).astype(jnp.bfloat16))
    grad_mixed_cross = back_product(grad_merge, merge_part).astype(jnp.bfloat16)
    grad_query, grad_keyval = attend_cross_back(
        cross_queries,
        keyval,
        length_all,
        logsum_cross,
        grad_mixed_cross,
        all_images,
        heads,
        score_scale,
    )
    cross_grads = scatter(
        outer_sum(act_two, grad_query), outer_sum(text_all, grad_keyval), merge_term
    )
    text_grad = (
        group_sum(grad_keyval, keyval_part, back_product)
        .astype(jnp.bfloat16)
        .reshape(text_tokens.shape)
    )
    grad_act_two = own_rows(group_sum(grad_query, query_part, back_product))
    gain_term = jnp.sum(grad_act_two * norm_two, axis=1)
    grad_one = grad_two + normed_back(hidden_one, grad_act_two * gain_full)

    grad_gate_self = jnp.sum(grad_one * branch_one, axis=1)
    grad_out = group_rows(flatten(gate_self * grad_one).astype(jnp.bfloat16))
    out_term = rows_to_columns(outer_sum(mixed_flat, grad_out).astype(jnp.bfloat16))
    grad_mixed_self = back_product(grad_out, out_part).astype(jnp.bfloat16)
    grad_qkv = attend_self_back(
        qkv_act, logsum_self, grad_mixed_self, all_images, heads, score_scale
    )
    self_grads = scatter(outer_sum(act_one, grad_qkv), out_term)
    grad_act_one = own_rows(group_sum(grad_qkv, qkv_part, back_product))
    grad_shift_self = jnp.sum(grad_act_one, axis=1)
    grad_scale_self = jnp.sum(grad_act_one * norm_one, axis=1)
    image_grad = (grad_one + normed_back(residual, grad_act_one * (1.0 + scale_self))).astype(
        jnp.bfloat16
    )

    early = everyone(
        jnp.concatenate(
            [grad_gate_self, grad_shift_mlp, grad_scale_mlp, grad_gate_mlp, gain_term], axis=1
        ).astype(jnp.bfloat16),
        group,
    )
    late = everyone(
        jnp.concatenate([grad_shift_self, grad_scale_self], axis=1).astype(jnp.bfloat16), group
    )
    all_vectors = jnp.concatenate([late, early[:, : 4 * width]], axis=1)
    mod_grad = outer_sum(conditions(all_steps), all_vectors)
    gain_grad = jnp.sum(
        lax.dynamic_slice_in_dim(
            early, 4 * width + member * shard_rows, shard_rows, 1
        ).astype(jnp.float32),
        axis=0,
    )
    self_all, cross_all, mlp_all = [
        lax.all_gather(found, "rep", axis=0) for found in (self_grads, cross_grads, mlp_grads)
    ]
    down_grad = mlp_all[:, :, :width].reshape(-1, width).astype(jnp.float32)
    if aligned:
        up_width = hidden // (group * PEERS)
        up_grad = spread_blocks(mlp_all, width // up_width, group, up_width)
    else:
        up_grad = (
            mlp_all[:, :, width:]
            .reshape(PEERS, shard_rows, group, -1)
            .transpose(1, 2, 0, 3)
            .reshape(shard_rows, hidden)
            .astype(jnp.float32)
        )
    return (
        block_out,
        image_grad,
        text_grad,
        mod_grad,
        spread_blocks(self_all, 0, 3, part),
        spread_blocks(self_all, 3, 1, part),
        spread_blocks(cross_all, 0, 1, part),
        spread_blocks(cross_all, 1, 2, part),
        spread_blocks(cross_all, 3, 1, part),
        gain_grad,
        up_grad,
        down_grad,
    )


def solution(mesh):
    placed = (
        P(("rep", "fsdp"), None, None),
        P(("rep", "fsdp"), None, None),
        P(("rep", "fsdp")),
        P(("rep", "fsdp")),
        P(("rep", "fsdp"), None, None),
        P("fsdp", None),
        P("fsdp", None),
        P("fsdp", None),
        P("fsdp", None),
        P("fsdp", None),
        P("fsdp", None),
        P("fsdp"),
        P("fsdp", None),
        P("fsdp", None),
    )
    return jax.shard_map(
        body,
        mesh=mesh,
        in_specs=placed,
        out_specs=(
            P(("rep", "fsdp"), None, None),
            P(("rep", "fsdp"), None, None),
            P(("rep", "fsdp"), None, None),
            P("fsdp", None),
            P("fsdp", None),
            P("fsdp", None),
            P("fsdp", None),
            P("fsdp", None),
            P("fsdp", None),
            P("fsdp"),
            P("fsdp", None),
            P("fsdp", None),
        ),
        check_vma=False,
    )
```

time: 1690 us -> 1270 us (0.75)
  waiting for transfers between devices: 1050 us -> 582 us
  blocking collectives: 142 us -> 0 us
  starting transfers between devices: 39.7 us -> 162 us
  Pallas kernels: 0 us -> 100 us
  matrix products: 255 us -> 206 us
  other arithmetic: 56.8 us -> 75.1 us
    reduce_scatter x7 -> x0, waiting for transfers between devices: 459 us -> none  [scatter(): lax.psum_scatter(value.astype(jnp.bfloat16), 'fsdp', scatter_dimension=0,...]
    ppermute x0 -> x113, waiting for transfers between devices: none -> 401 us  [the longest x28 140 us: ring_gather(): onward.append(lax.ppermute(onward[-1], 'fsdp', ring_pairs(size, 1)))]
    all_gather x14 -> x3, waiting for transfers between devices: 238 us -> 0.01 us  [body(): lax.all_gather(found, 'rep', axis=0)]
    ppermute x50 -> x56, waiting for transfers between devices: 327 us -> 173 us  [swap(): lax.ppermute(value, 'rep', [(peer, peer ^ mask) for peer in range(PEERS)])]
    ppermute x0 -> x113, starting transfers between devices: none -> 125 us  [the longest x28 34.6 us: ring_gather(): onward.append(lax.ppermute(onward[-1], 'fsdp', ring_pairs(size, 1)))]
    pallas_call x0 -> x17, Pallas kernels: none -> 100 us  [the longest x6 43.6 us: spread_blocks(): pl.pallas_call(kernel, grid=(count, PEERS), in_specs=[pl.BlockSpec((None,...]
    all_gather x2 -> x0, blocking collectives: 97.9 us -> none  [the longest x1 79.5 us: body(): all_vectors = lax.all_gather(vectors, ('rep', 'fsdp'), axis=0, tiled=True)]
    dot_general x12 -> x0, matrix products: 43.7 us -> none  [the longest x2 15.3 us: attend_back(): jnp.einsum('nhqk,nkhd->nqhd', grad_scores, keys, preferred_element_type=j...]
  transfers between devices with their start and end apart: 72 -> 173, of which waited for: 37 -> 76; matrix products, arithmetic and copies ran while one was open for 21% -> 27% of each run, Pallas kernels for 0% -> 7%
where the time goes in v2:
time: 1270 us; the launch traced here: 1260 us
  waiting for transfers between devices  582 us (46%)
  matrix products  206 us (16%)
  starting transfers between devices  162 us (13%)
  local copies, waits for them, and re-layouts  113 us (9%)
  Pallas kernels  100 us (8%)
  other arithmetic  75.1 us (6%)
  between operations  19.6 us (2%)
    ppermute x56, waiting for transfers between devices, swap(): lax.ppermute(value, 'rep', [(peer, peer ^ mask) for peer in range(PEERS)])  173 us
    ppermute x28, waiting for transfers between devices, ring_gather(): onward.append(lax.ppermute(onward[-1], 'fsdp', ring_pairs(size, 1)))  140 us
    ppermute x21, waiting for transfers between devices, ring_scatter(): back = lax.ppermute(back, 'fsdp', ring_pairs(size, -1))  133 us
    ppermute x21, waiting for transfers between devices, ring_scatter(): onward = lax.ppermute(onward, 'fsdp', ring_pairs(size, 1))  77.7 us
    dot_general x15, matrix products, back_product(): lax.dot_general(left, right, (((1,), (1,)), ((), ())), preferred_element_...  74.7 us
    dot_general x14, matrix products, matmul(): return jnp.dot(left, right, preferred_element_type=jnp.float32)  71.6 us
    dot_general x8, matrix products, outer_sum(): lax.dot_general(left, right, (((0,), (0,)), ((), ())), preferred_element_...  59.5 us
    pallas_call x6, Pallas kernels, spread_blocks(): pl.pallas_call(kernel, grid=(count, PEERS), in_specs=[pl.BlockSpec((None,...  43.6 us
  transfers between devices with their start and end apart: 173, of which 76 were waited for; matrix products, arithmetic and copies ran while one was open for 27% of the time, Pallas kernels for 7%

profile of v2, /device:TPU:0, one launch (start us, length us, event | category | flops | bytes accessed | tf_op | source)
XLA Modules:
  0.0 1258.0 jit_solution(5375265079093119783)
XLA Ops:
  129.6 11.3 convolution_convert_fusion.3.qkv_ref
  157.1 12.2 collective-permute-done.35.refs_3_
  171.4 11.4 collective-permute-done.36.refs_4_
  213.3 13.1 %collective-permute-done.24 = bf16[256,2048]{1,0:T(8,128)(2,1)} collective-permute-done((bf16[256,2048]{1,0:T(8,128)(2,1)}, bf16[256,2048]{1,0:T(8,128)(2,1)}, u32[]{:S(2)}, u32[]{:S(2)}) %collective-permute-start.24) | collective-permute-done | bytes 1048608 | tf_op jit(solution)/shard_map/ppermute | solution.py:304
  288.1 10.4 collective-permute-done.52
  315.0 12.2 collective-permute-done.62.refs_5_
  330.6 10.1 collective-permute-done.63.refs_6_
  343.1 10.5 collective-permute-done.73.refs_2_
  396.8 10.4 collective-permute-done.76.refs_5_
  462.6 21.0 %fusion.6 = (bf16[1024,2048]{1,0:T(8,128)(2,1)}, bf16[1024,2048]{1,0:T(8,128)(2,1)}) fusion(bf16[2048,2048]{1,0:T(8,128)(2,1)} %lay_out.6, bf16[256,2048]{1,0:T(8,128)(2,1)} %collective-permute-done.57, bf16[256,2048]{1,0:T(8,128)(2,1)} %collective-permute-done.58, bf16[256,2048]{1,0:T(8,128)(2,1)} %collective-permute-done.56, bf16[256,2048]{1,0:T(8,128)(2,1)} %fusion.41), kind=kOutput, calls=%fused_computation.9 | convolution fusion | flops 8648654848 | bytes 20971520 | tf_op jit(solution)/shard_map/dot_general | solution.py:17
  483.7 13.8 %multiply_convert_fusion = bf16[1024,2048]{1,0:T(8,128)(2,1)} fusion(bf16[1024,2048]{1,0:T(8,128)(2,1)} %get-tuple-element.39, bf16[2048,2048]{1,0:T(8,128)(2,1)S(1)} %copy-done.68, bf16[256,2048]{1,0:T(8,128)(2,1)} %collective-permute-done.90, bf16[256,2048]{1,0:T(8,128)(2,1)S(1)} %collective-permute-done.91, ...), kind=kOutput, calls=%fused_computation.10 | convolution fusion | flops 8613003264 | bytes 20971520 | tf_op jit(solution)/shard_map/dot_general | solution.py:27
  497.5 9.9 convolution_convert_fusion.10
  507.4 14.0 %convolution_convert_fusion = bf16[2048,2048]{0,1:T(8,128)(2,1)} fusion(bf16[1024,2048]{1,0:T(8,128)(2,1)} %multiply_convert_fusion, bf16[256,2048]{1,0:T(8,128)(2,1)} %collective-permute-done.57, bf16[256,2048]{1,0:T(8,128)(2,1)} %collective-permute-done.58, bf16[256,2048]{1,0:T(8,128)(2,1)} %collective-permute-done.56, bf16[256,2048]{1,0:T(8,128)(2,1)} %fusion.41), kind=kOutput, calls=%fused_computation.12 | convolution fusion | flops 8610906112 | bytes 16777216 | tf_op jit(solution)/shard_map/dot_general | solution.py:21
  528.1 13.9 %convolution_convert_fusion.1 = bf16[2048,2048]{0,1:T(8,128)(2,1)} fusion(bf16[1024,2048]{1,0:T(8,128)(2,1)} %get-tuple-element.37, bf16[256,2048]{1,0:T(8,128)(2,1)} %collective-permute-done.90, bf16[256,2048]{1,0:T(8,128)(2,1)S(1)} %copy-done.229, bf16[256,2048]{1,0:T(8,128)(2,1)S(1)} %copy-done.227, bf16[256,2048]{1,0:T(8,128)(2,1)} %fusion.43), kind=kOutput, calls=%fused_computation.13 | convolution fusion | flops 8610906112 | bytes 16777216 | tf_op jit(solution)/shard_map/dot_general | solution.py:21
  557.0 17.3 %collective-permute-done.162 = bf16[128,4096]{0,1:T(8,128)(2,1)S(1)} collective-permute-done((bf16[128,4096]{0,1:T(8,128)(2,1)S(1)}, bf16[128,4096]{0,1:T(8,128)(2,1)S(1)}, u32[]{:S(2)}, u32[]{:S(2)}) %collective-permute-start.162) | collective-permute-done | bytes 1048608 | tf_op jit(solution)/shard_map/ppermute | solution.py:399
  584.0 15.3 %collective-permute-done.163 = bf16[128,4096]{0,1:T(8,128)(2,1)S(1)} collective-permute-done((bf16[128,4096]{0,1:T(8,128)(2,1)S(1)}, bf16[128,4096]{0,1:T(8,128)(2,1)S(1)}, u32[]{:S(2)}, u32[]{:S(2)}) %collective-permute-start.163) | collective-permute-done | bytes 1048608 | tf_op jit(solution)/shard_map/ppermute | solution.py:399
  640.0 10.6 collective-permute-done.165
  693.3 9.6 collective-permute-done.139
  719.4 12.4 collective-permute-done.160
  735.0 21.7 %collective-permute-done.168 = bf16[128,4096]{0,1:T(8,128)(2,1)S(1)} collective-permute-done((bf16[128,4096]{0,1:T(8,128)(2,1)S(1)}, bf16[128,4096]{0,1:T(8,128)(2,1)S(1)}, u32[]{:S(2)}, u32[]{:S(2)}) %collective-permute-start.168) | collective-permute-done | bytes 1048608 | tf_op jit(solution)/shard_map/ppermute | solution.py:399
  757.7 23.0 %collective-permute-done.98 = bf16[256,2048]{1,0:T(8,128)(2,1)S(1)} collective-permute-done((bf16[256,2048]{1,0:T(8,128)(2,1)S(1)}, bf16[256,2048]{1,0:T(8,128)(2,1)S(1)}, u32[]{:S(2)}, u32[]{:S(2)}) %collective-permute-start.98) | collective-permute-done | bytes 1048608 | tf_op jit(solution)/shard_map/ppermute | solution.py:304
  793.4 32.7 %collective-permute-done.100 = bf16[256,2048]{1,0:T(8,128)(2,1)} collective-permute-done((bf16[256,2048]{1,0:T(8,128)(2,1)S(1)}, bf16[256,2048]{1,0:T(8,128)(2,1)}, u32[]{:S(2)}, u32[]{:S(2)}) %collective-permute-start.100) | collective-permute-done | bytes 1048608 | tf_op jit(solution)/shard_map/ppermute | solution.py:304
  858.8 22.3 %collective-permute-done.122 = bf16[512,512]{1,0:T(8,128)(2,1)S(1)} collective-permute-done((bf16[512,512]{1,0:T(8,128)(2,1)S(1)}, bf16[512,512]{1,0:T(8,128)(2,1)S(1)}, u32[]{:S(2)}, u32[]{:S(2)}) %collective-permute-start.122) | collective-permute-done | bytes 524320 | tf_op jit(solution)/shard_map/ppermute | solution.py:304
  915.3 11.5 collective-permute-done.148
  938.7 10.2 collective-permute-done.141
  963.0 9.6 collective-permute-done.134
  975.1 9.7 collective-permute-done.142
  1008.9 9.6 collective-permute-done.143
  1055.0 10.7 collective-permute-done.153
  1082.7 33.4 %collective-permute-done.103 = bf16[256,2048]{1,0:T(8,128)(2,1)} collective-permute-done((bf16[256,2048]{1,0:T(8,128)(2,1)}, bf16[256,2048]{1,0:T(8,128)(2,1)}, u32[]{:S(2)}, u32[]{:S(2)}) %collective-permute-start.103) | collective-permute-done | bytes 1048608 | tf_op jit(solution)/shard_map/ppermute | solution.py:304
  1175.5 11.9 copy.60
  1187.4 18.5 %spread_blocks.11 = f32[256,8192]{1,0:T(8,128)} custom-call(bf16[4,256,4096]{2,1,0:T(8,128)(2,1)} %bitcast.200), custom_call_target="tpu_custom_call" | custom-call | tf_op jit(solution)/shard_map/spread_blocks/pallas_call | solution.py:288
  (1005 shorter events, 774.2 us)
Async XLA Ops:
  49.4 1126.1 %all-gather.11.cloned.1.call-start = ((), (), s32[]{:S(2)}) async-start(), calls=%async_computation.3 | async-start | bytes 10485760 | tf_op jit(solution)/shard_map/all_gather | solution.py:678
  93.2 34.5 %collective-permute-start.3 = (bf16[256,2048]{1,0:T(8,128)(2,1)}, bf16[256,2048]{1,0:T(8,128)(2,1)}, u32[]{:S(2)}, u32[]{:S(2)}) collective-permute-start(bf16[256,2048]{1,0:T(8,128)(2,1)} %fusion.44), channel_id=1, source_target_pairs={{0,8},{8,0},{16,24},{24,16},{1,9},{9,1},{17,25},{25,17},{2,10},{10... | collective-permute-start | bytes 3145736 | tf_op jit(solution)/shard_map/ppermute | solution.py:304
  93.5 35.8 %collective-permute-start.5 = (bf16[256,2048]{1,0:T(8,128)(2,1)}, bf16[256,2048]{1,0:T(8,128)(2,1)}, u32[]{:S(2)}, u32[]{:S(2)}) collective-permute-start(bf16[256,2048]{1,0:T(8,128)(2,1)} %collective-permute-done.4), channel_id=1, source_target_pairs={{0,8},{8,0},{16,24},{24,16},{1,9},{9,1},{17,25},{25,17},{2,10},{10... | collective-permute-start | bytes 3145736 | tf_op jit(solution)/shard_map/ppermute | solution.py:304
  110.5 44.6 %collective-permute-start.34 = (bf16[128,2048]{1,0:T(8,128)(2,1)S(1)}, bf16[128,2048]{1,0:T(8,128)(2,1)S(1)}, u32[]{:S(2)}, u32[]{:S(2)}) collective-permute-start(bf16[128,2048]{1,0:T(8,128)(2,1)S(1)} %get-tuple-element.209.refs_1_), channel_id=1, source_target_pairs={{0,2},{2,4},{4,6},{6,7},{7,5},{5,3},{3,1},{1,0},{8,10},{10,12},{12... | collective-permute-start | bytes 1572872 | tf_op jit(solution)/shard_map/ppermute | solution.py:341
  117.4 39.0 %collective-permute-start.41 = (bf16[128,2048]{1,0:T(8,128)(2,1)S(1)}, bf16[128,2048]{1,0:T(8,128)(2,1)S(1)}, u32[]{:S(2)}, u32[]{:S(2)}) collective-permute-start(bf16[128,2048]{1,0:T(8,128)(2,1)S(1)} %get-tuple-element.208.refs_9_), channel_id=1, source_target_pairs={{0,1},{2,0},{4,2},{6,4},{7,6},{5,7},{3,5},{1,3},{8,9},{10,8},{12,1... | collective-permute-start | bytes 1572872 | tf_op jit(solution)/shard_map/ppermute | solution.py:342
  154.9 43.2 %collective-permute-start.23 = (bf16[512,2048]{1,0:T(8,128)(2,1)S(1)}, bf16[512,2048]{1,0:T(8,128)(2,1)S(1)}, u32[]{:S(2)}, u32[]{:S(2)}) collective-permute-start(bf16[512,2048]{1,0:T(8,128)(2,1)S(1)} %convolution_convert_fusion.13), channel_id=1, source_target_pairs={{0,8},{8,0},{16,24},{24,16},{1,9},{9,1},{17,25},{25,17},{2,10},{10... | collective-permute-start | bytes 6291464 | tf_op jit(solution)/shard_map/ppermute | solution.py:304
  235.9 34.8 %collective-permute-start.32 = (bf16[256,2048]{1,0:T(8,128)(2,1)}, bf16[256,2048]{1,0:T(8,128)(2,1)}, u32[]{:S(2)}, u32[]{:S(2)}) collective-permute-start(bf16[256,2048]{1,0:T(8,128)(2,1)} %fusion.40), channel_id=1, source_target_pairs={{0,16},{8,24},{16,0},{24,8},{1,17},{9,25},{17,1},{25,9},{2,18},{10... | collective-permute-start | bytes 3145736 | tf_op jit(solution)/shard_map/ppermute | solution.py:304
  270.6 30.4 %collective-permute-start.31 = (bf16[256,2048]{1,0:T(8,128)(2,1)}, bf16[256,2048]{1,0:T(8,128)(2,1)S(1)}, u32[]{:S(2)}, u32[]{:S(2)}) collective-permute-start(bf16[256,2048]{1,0:T(8,128)(2,1)} %fusion.40), channel_id=1, source_target_pairs={{0,8},{8,0},{16,24},{24,16},{1,9},{9,1},{17,25},{25,17},{2,10},{10... | collective-permute-start | bytes 3145736 | tf_op jit(solution)/shard_map/ppermute | solution.py:304
  270.7 30.3 %collective-permute-start.33 = (bf16[256,2048]{1,0:T(8,128)(2,1)}, bf16[256,2048]{1,0:T(8,128)(2,1)S(1)}, u32[]{:S(2)}, u32[]{:S(2)}) collective-permute-start(bf16[256,2048]{1,0:T(8,128)(2,1)} %collective-permute-done.32), channel_id=1, source_target_pairs={{0,8},{8,0},{16,24},{24,16},{1,9},{9,1},{17,25},{25,17},{2,10},{10... | collective-permute-start | bytes 3145736 | tf_op jit(solution)/shard_map/ppermute | solution.py:304
  312.8 43.0 %collective-permute-start.54 = (bf16[512,2048]{1,0:T(8,128)(2,1)S(1)}, bf16[512,2048]{1,0:T(8,128)(2,1)S(1)}, u32[]{:S(2)}, u32[]{:S(2)}) collective-permute-start(bf16[512,2048]{1,0:T(8,128)(2,1)S(1)} %convolution_convert_fusion.12), channel_id=1, source_target_pairs={{0,8},{8,0},{16,24},{24,16},{1,9},{9,1},{17,25},{25,17},{2,10},{10... | collective-permute-start | bytes 6291464 | tf_op jit(solution)/shard_map/ppermute | solution.py:304
  387.5 42.0 %collective-permute-start.57 = (bf16[256,2048]{1,0:T(8,128)(2,1)}, bf16[256,2048]{1,0:T(8,128)(2,1)}, u32[]{:S(2)}, u32[]{:S(2)}) collective-permute-start(bf16[256,2048]{1,0:T(8,128)(2,1)} %fusion.41), channel_id=1, source_target_pairs={{0,16},{8,24},{16,0},{24,8},{1,17},{9,25},{17,1},{25,9},{2,18},{10... | collective-permute-start | bytes 3145736 | tf_op jit(solution)/shard_map/ppermute | solution.py:304
  418.1 38.4 %collective-permute-start.90 = (bf16[256,2048]{1,0:T(8,128)(2,1)}, bf16[256,2048]{1,0:T(8,128)(2,1)}, u32[]{:S(2)}, u32[]{:S(2)}) collective-permute-start(bf16[256,2048]{1,0:T(8,128)(2,1)} %fusion.43), channel_id=1, source_target_pairs={{0,16},{8,24},{16,0},{24,8},{1,17},{9,25},{17,1},{25,9},{2,18},{10... | collective-permute-start | bytes 3145736 | tf_op jit(solution)/shard_map/ppermute | solution.py:304
  429.5 33.1 %collective-permute-start.56 = (bf16[256,2048]{1,0:T(8,128)(2,1)}, bf16[256,2048]{1,0:T(8,128)(2,1)}, u32[]{:S(2)}, u32[]{:S(2)}) collective-permute-start(bf16[256,2048]{1,0:T(8,128)(2,1)} %fusion.41), channel_id=1, source_target_pairs={{0,8},{8,0},{16,24},{24,16},{1,9},{9,1},{17,25},{25,17},{2,10},{10... | collective-permute-start | bytes 3145736 | tf_op jit(solution)/shard_map/ppermute | solution.py:304
  429.5 33.1 %collective-permute-start.58 = (bf16[256,2048]{1,0:T(8,128)(2,1)}, bf16[256,2048]{1,0:T(8,128)(2,1)}, u32[]{:S(2)}, u32[]{:S(2)}) collective-permute-start(bf16[256,2048]{1,0:T(8,128)(2,1)} %collective-permute-done.57), channel_id=1, source_target_pairs={{0,8},{8,0},{16,24},{24,16},{1,9},{9,1},{17,25},{25,17},{2,10},{10... | collective-permute-start | bytes 3145736 | tf_op jit(solution)/shard_map/ppermute | solution.py:304
  507.3 69.6 %collective-permute-start.92 = (bf16[512,2048]{1,0:T(8,128)(2,1)}, bf16[512,2048]{1,0:T(8,128)(2,1)}, u32[]{:S(2)}, u32[]{:S(2)}) collective-permute-start(bf16[512,2048]{1,0:T(8,128)(2,1)} %convolution_convert_fusion.10), channel_id=1, source_target_pairs={{0,8},{8,0},{16,24},{24,16},{1,9},{9,1},{17,25},{25,17},{2,10},{10... | collective-permute-start | bytes 6291464 | tf_op jit(solution)/shard_map/ppermute | solution.py:304
  556.7 75.2 %collective-permute-start.87 = (bf16[512,2048]{1,0:T(8,128)(2,1)}, bf16[512,2048]{1,0:T(8,128)(2,1)}, u32[]{:S(2)}, u32[]{:S(2)}) collective-permute-start(bf16[512,2048]{1,0:T(8,128)(2,1)} %convolution_convert_fusion.11), channel_id=1, source_target_pairs={{0,8},{8,0},{16,24},{24,16},{1,9},{9,1},{17,25},{25,17},{2,10},{10... | collective-permute-start | bytes 6291464 | tf_op jit(solution)/shard_map/ppermute | solution.py:304
  652.4 38.5 %collective-permute-start.166 = (bf16[128,4096]{0,1:T(8,128)(2,1)S(1)}, bf16[128,4096]{0,1:T(8,128)(2,1)S(1)}, u32[]{:S(2)}, u32[]{:S(2)}) collective-permute-start(bf16[128,4096]{0,1:T(8,128)(2,1)S(1)} %add_convert_fusion.3), channel_id=1, source_target_pairs={{0,1},{2,0},{4,2},{6,4},{7,6},{5,7},{3,5},{1,3},{8,9},{10,8},{12,1... | collective-permute-start | bytes 3145736 | tf_op jit(solution)/shard_map/ppermute | solution.py:399
  655.8 35.7 %collective-permute-start.159 = (bf16[128,4096]{0,1:T(8,128)(2,1)}, bf16[128,4096]{0,1:T(8,128)(2,1)S(1)}, u32[]{:S(2)}, u32[]{:S(2)}) collective-permute-start(bf16[128,4096]{0,1:T(8,128)(2,1)} %add_convert_fusion.10), channel_id=1, source_target_pairs={{0,2},{2,4},{4,6},{6,7},{7,5},{5,3},{3,1},{1,0},{8,10},{10,12},{12... | collective-permute-start | bytes 3145736 | tf_op jit(solution)/shard_map/ppermute | solution.py:398
  672.4 33.8 %collective-permute-start.104 = (bf16[256,2048]{1,0:T(8,128)(2,1)S(1)}, bf16[256,2048]{1,0:T(8,128)(2,1)S(1)}, u32[]{:S(2)}, u32[]{:S(2)}) collective-permute-start(bf16[256,2048]{1,0:T(8,128)(2,1)S(1)} %convolution_convert_fusion.14), channel_id=1, source_target_pairs={{0,8},{8,0},{16,24},{24,16},{1,9},{9,1},{17,25},{25,17},{2,10},{10... | collective-permute-start | bytes 3145736 | tf_op jit(solution)/shard_map/ppermute | solution.py:304
  692.4 440.2 %collective-permute-start.108 = (s32[4,1]{0,1:T(1,128)}, s32[4,1]{0,1:T(1,128)}, u32[]{:S(2)}, u32[]{:S(2)}) collective-permute-start(s32[4,1]{0,1:T(1,128)} %pad_add_fusion.4), channel_id=1, source_target_pairs={{0,1},{1,0},{2,3},{3,2},{4,5},{5,4},{6,7},{7,6},{8,9},{9,8},{10,11... | collective-permute-start | bytes 56 | tf_op jit(solution)/shard_map/ppermute | solution.py:424
  702.9 79.1 %collective-permute-start.88 = (bf16[256,2048]{1,0:T(8,128)(2,1)S(1)}, bf16[256,2048]{1,0:T(8,128)(2,1)S(1)}, u32[]{:S(2)}, u32[]{:S(2)}) collective-permute-start(bf16[256,2048]{1,0:T(8,128)(2,1)S(1)} %copy-done.224), channel_id=1, source_target_pairs={{0,16},{8,24},{16,0},{24,8},{1,17},{9,25},{17,1},{25,9},{2,18},{10... | collective-permute-start | bytes 3145736 | tf_op jit(solution)/shard_map/ppermute | solution.py:304
  717.1 429.1 %collective-permute-start.105 = (bf16[128,2048]{1,0:T(8,128)(2,1)}, bf16[128,2048]{1,0:T(8,128)(2,1)}, u32[]{:S(2)}, u32[]{:S(2)}) collective-permute-start(bf16[128,2048]{1,0:T(8,128)(2,1)} %fusion.19), channel_id=1, source_target_pairs={{0,16},{8,24},{16,0},{24,8},{1,17},{9,25},{17,1},{25,9},{2,18},{10... | collective-permute-start | bytes 1572872 | tf_op jit(solution)/shard_map/ppermute | solution.py:304
  790.6 35.5 %collective-permute-start.100 = (bf16[256,2048]{1,0:T(8,128)(2,1)S(1)}, bf16[256,2048]{1,0:T(8,128)(2,1)}, u32[]{:S(2)}, u32[]{:S(2)}) collective-permute-start(bf16[256,2048]{1,0:T(8,128)(2,1)S(1)} %fusion.42), channel_id=1, source_target_pairs={{0,16},{8,24},{16,0},{24,8},{1,17},{9,25},{17,1},{25,9},{2,18},{10... | collective-permute-start | bytes 3145736 | tf_op jit(solution)/shard_map/ppermute | solution.py:304
  791.1 35.0 %collective-permute-start.116 = (bf16[1,10240]{1,0:T(2,128)(2,1)S(1)}, bf16[1,10240]{1,0:T(2,128)(2,1)S(1)}, u32[]{:S(2)}, u32[]{:S(2)}) collective-permute-start(bf16[1,10240]{1,0:T(2,128)(2,1)S(1)} %constant_dynamic-update-slice_fusion.2), channel_id=1, source_target_pairs={{0,4},{1,5},{2,6},{3,7},{4,0},{5,1},{6,2},{7,3},{8,12},{9,13},{10,... | collective-permute-start | bytes 61448 | tf_op jit(solution)/shard_map/ppermute | solution.py:424
  793.2 419.9 %all-gather.7.cloned.1.call-start = ((), (), s32[]{:S(2)}) async-start(), calls=%async_computation.1 | async-start | bytes 5242880 | tf_op jit(solution)/shard_map/all_gather | solution.py:678
  793.3 33.5 %collective-permute-start.99 = (bf16[256,2048]{1,0:T(8,128)(2,1)S(1)}, bf16[256,2048]{1,0:T(8,128)(2,1)S(1)}, u32[]{:S(2)}, u32[]{:S(2)}) collective-permute-start(bf16[256,2048]{1,0:T(8,128)(2,1)S(1)} %fusion.42), channel_id=1, source_target_pairs={{0,8},{8,0},{16,24},{24,16},{1,9},{9,1},{17,25},{25,17},{2,10},{10... | collective-permute-start | bytes 3145736 | tf_op jit(solution)/shard_map/ppermute | solution.py:304
  833.1 47.9 %collective-permute-start.122 = (bf16[512,512]{1,0:T(8,128)(2,1)S(1)}, bf16[512,512]{1,0:T(8,128)(2,1)S(1)}, u32[]{:S(2)}, u32[]{:S(2)}) collective-permute-start(bf16[512,512]{1,0:T(8,128)(2,1)S(1)} %get-tuple-element.182), channel_id=1, source_target_pairs={{0,16},{8,24},{16,0},{24,8},{1,17},{9,25},{17,1},{25,9},{2,18},{10... | collective-permute-start | bytes 1572872 | tf_op jit(solution)/shard_map/ppermute | solution.py:304
  834.7 46.3 %collective-permute-start.121 = (bf16[512,512]{1,0:T(8,128)(2,1)S(1)}, bf16[512,512]{1,0:T(8,128)(2,1)S(1)}, u32[]{:S(2)}, u32[]{:S(2)}) collective-permute-start(bf16[512,512]{1,0:T(8,128)(2,1)S(1)} %get-tuple-element.183), channel_id=1, source_target_pairs={{0,8},{8,0},{16,24},{24,16},{1,9},{9,1},{17,25},{25,17},{2,10},{10... | collective-permute-start | bytes 1572872 | tf_op jit(solution)/shard_map/ppermute | solution.py:304
  858.7 195.1 %collective-permute-start.117 = (bf16[2,10240]{1,0:T(2,128)(2,1)}, bf16[2,10240]{1,0:T(2,128)(2,1)}, u32[]{:S(2)}, u32[]{:S(2)}) collective-permute-start(bf16[2,10240]{1,0:T(2,128)(2,1)} %pad_maximum_fusion.41), channel_id=1, source_target_pairs={{0,2},{1,3},{2,0},{3,1},{4,6},{5,7},{6,4},{7,5},{8,10},{9,11},{10,... | collective-permute-start | bytes 122888 | tf_op jit(solution)/shard_map/ppermute | solution.py:424
  1033.5 198.1 %all-gather.9.cloned.1.call-start = ((), (), s32[]{:S(2)}) async-start(), calls=%async_computation.2 | async-start | bytes 5242880 | tf_op jit(solution)/shard_map/all_gather | solution.py:678
  1065.7 60.0 %collective-permute-start.118 = (bf16[4,10240]{1,0:T(4,128)(2,1)S(1)}, bf16[4,10240]{1,0:T(4,128)(2,1)S(1)}, u32[]{:S(2)}, u32[]{:S(2)}) collective-permute-start(bf16[4,10240]{1,0:T(4,128)(2,1)S(1)} %pad_maximum_fusion.39), channel_id=1, source_target_pairs={{0,1},{1,0},{2,3},{3,2},{4,5},{5,4},{6,7},{7,6},{8,9},{9,8},{10,11... | collective-permute-start | bytes 245768 | tf_op jit(solution)/shard_map/ppermute | solution.py:424
  1079.2 36.9 %collective-permute-start.103 = (bf16[256,2048]{1,0:T(8,128)(2,1)}, bf16[256,2048]{1,0:T(8,128)(2,1)}, u32[]{:S(2)}, u32[]{:S(2)}) collective-permute-start(bf16[256,2048]{1,0:T(8,128)(2,1)} %fusion.14), channel_id=1, source_target_pairs={{0,16},{8,24},{16,0},{24,8},{1,17},{9,25},{17,1},{25,9},{2,18},{10... | collective-permute-start | bytes 3145736 | tf_op jit(solution)/shard_map/ppermute | solution.py:304
  (382 other events, 6687.1 us)
Sparse Core Ops, SparseCore 0:
  793.4 90.6 all-gather.10
  1033.6 33.8 all-gather.6
  1082.9 46.5 all-gather.8

commit v3 on v2

v3 whole, which is shorter than its diff:
```python
import math

import jax
import jax.numpy as jnp
from jax import lax
from jax.experimental import pallas as pl
from jax.experimental.pallas import tpu as pltpu
from jax.sharding import PartitionSpec as P

HEADS = 16


EPSILON = 1e-06


def matmul(left, right):
    return jnp.dot(left, right, preferred_element_type=jnp.float32)


def outer_sum(left, right):
    return lax.dot_general(
        left, right, (((0,), (0,)), ((), ())), preferred_element_type=jnp.float32
    )


def back_product(left, right):
    return lax.dot_general(
        left, right, (((1,), (1,)), ((), ())), preferred_element_type=jnp.float32
    )


def normed(value):
    return value * lax.rsqrt(jnp.mean(value * value, axis=-1, keepdims=True) + EPSILON)


def normed_back(value, grad):
    return jax.vjp(normed, value)[1](grad)[0]


def smooth_gate(value):
    return jax.nn.gelu(value, approximate=True)


def row_block(rows, columns, column=0):
    return pl.BlockSpec((rows, columns), lambda image, *_: (image, column))


def parts_of(value, count):
    width = value.shape[1] // count
    return [value[:, i * width : (i + 1) * width] for i in range(count)]


def scores_of(queries, keys, limit, scale):
    scores = back_product(queries, keys) * scale
    if limit is not None:
        slot = lax.broadcasted_iota(jnp.int32, scores.shape, 1)
        scores = jnp.where(slot < limit, scores, -jnp.inf)
    return scores


def attend_heads(queries, keys, values, limit, scale, mixed_ref, logsum_ref):
    head_width = keys[0].shape[1]
    for head, (query, key, value) in enumerate(zip(queries, keys, values)):
        scores = scores_of(query, key, limit, scale)
        row_top = jnp.max(scores, axis=1, keepdims=True)
        raised = jnp.exp(scores - row_top)
        totals = jnp.sum(raised, axis=1, keepdims=True)
        weights = (raised / totals).astype(jnp.bfloat16)
        mixed_ref[:, head * head_width : (head + 1) * head_width] = matmul(weights, value).astype(
            jnp.bfloat16
        )
        logsum_ref[:, head : head + 1] = row_top + jnp.log(totals)


def attend_heads_back(queries, keys, values, limit, scale, logsum_ref, grads, outs):
    grad_query_ref, grad_key_ref, grad_value_ref = outs
    for head, (query, key, value, grad) in enumerate(zip(queries, keys, values, grads)):
        scores = scores_of(query, key, limit, scale)
        weights = jnp.exp(scores - logsum_ref[:, head : head + 1])
        grad_weights = back_product(grad, value)
        grad_value_ref(head, outer_sum(weights.astype(jnp.bfloat16), grad))
        inner_sum = jnp.sum(weights * grad_weights, axis=1, keepdims=True)
        grad_scores = (scale * (weights * (grad_weights - inner_sum))).astype(jnp.bfloat16)
        grad_query_ref(head, matmul(grad_scores, key))
        grad_key_ref(head, outer_sum(grad_scores, query))


def head_writer(ref, first, width):
    def write(head, value):
        start = first + head * width
        ref[:, start : start + width] = value.astype(jnp.bfloat16)

    return write


VMEM_LIMIT = 48 * 1024 * 1024


def cost(flops, moved, transcendentals=0):
    return pl.CostEstimate(
        flops=int(flops), bytes_accessed=int(moved), transcendentals=int(transcendentals)
    )


def attention_cost(images, length, slots, heads, width, products):
    pairs = images * heads * length * slots
    return cost(2 * products * pairs * width, 8 * pairs, pairs)


def attend_self(qkv, images, heads, scale):
    rows, columns = qkv.shape
    length, part = rows // images, columns // 3

    def kernel(qkv_ref, mixed_ref, logsum_ref):
        blocks = parts_of(qkv_ref, 3 * heads)
        attend_heads(
            blocks[:heads],
            blocks[heads : 2 * heads],
            blocks[2 * heads :],
            None,
            scale,
            mixed_ref,
            logsum_ref,
        )

    return pl.pallas_call(
        kernel,
        grid=(images,),
        in_specs=[row_block(length, columns)],
        out_specs=[row_block(length, part), row_block(length, heads)],
        out_shape=[
            jax.ShapeDtypeStruct((rows, part), jnp.bfloat16),
            jax.ShapeDtypeStruct((rows, heads), jnp.float32),
        ],
        compiler_params=pltpu.CompilerParams(vmem_limit_bytes=VMEM_LIMIT),
        cost_estimate=attention_cost(images, length, length, heads, part // heads, 2),
        name="attend_self",
    )(qkv)


def attend_self_back(qkv, logsum, grad_mixed, images, heads, scale):
    rows, columns = qkv.shape
    length, part = rows // images, columns // 3

    def kernel(qkv_ref, logsum_ref, grad_ref, out_ref):
        blocks = parts_of(qkv_ref, 3 * heads)
        writers = [head_writer(out_ref, i * part, part // heads) for i in range(3)]
        attend_heads_back(
            blocks[:heads],
            blocks[heads : 2 * heads],
            blocks[2 * heads :],
            None,
            scale,
            logsum_ref,
            parts_of(grad_ref, heads),
            writers,
        )

    return pl.pallas_call(
        kernel,
        grid=(images,),
        in_specs=[row_block(length, columns), row_block(length, heads), row_block(length, part)],
        out_specs=row_block(length, columns),
        out_shape=jax.ShapeDtypeStruct((rows, columns), jnp.bfloat16),
        compiler_params=pltpu.CompilerParams(vmem_limit_bytes=VMEM_LIMIT),
        cost_estimate=attention_cost(images, length, length, heads, part // heads, 5),
        name="attend_self_back",
    )(qkv, logsum, grad_mixed)


def attend_cross(queries, keyval, limits, images, heads, scale):
    rows, part = queries.shape
    length, slots = rows // images, keyval.shape[0] // images

    def kernel(limits_ref, query_ref, keyval_ref, mixed_ref, logsum_ref):
        blocks = parts_of(keyval_ref, 2 * heads)
        attend_heads(
            parts_of(query_ref, heads),
            blocks[:heads],
            blocks[heads:],
            limits_ref[pl.program_id(0)],
            scale,
            mixed_ref,
            logsum_ref,
        )

    return pl.pallas_call(
        kernel,
        grid_spec=pltpu.PrefetchScalarGridSpec(
            num_scalar_prefetch=1,
            grid=(images,),
            in_specs=[row_block(length, part), row_block(slots, 2 * part)],
            out_specs=[row_block(length, part), row_block(length, heads)],
        ),
        out_shape=[
            jax.ShapeDtypeStruct((rows, part), jnp.bfloat16),
            jax.ShapeDtypeStruct((rows, heads), jnp.float32),
        ],
        compiler_params=pltpu.CompilerParams(vmem_limit_bytes=VMEM_LIMIT),
        cost_estimate=attention_cost(images, length, slots, heads, part // heads, 2),
        name="attend_cross",
    )(limits, queries, keyval)


def attend_cross_back(queries, keyval, limits, logsum, grad_mixed, images, heads, scale):
    rows, part = queries.shape
    length, slots = rows // images, keyval.shape[0] // images

    def kernel(limits_ref, query_ref, keyval_ref, logsum_ref, grad_ref, out_ref, text_ref):
        blocks = parts_of(keyval_ref, 2 * heads)
        width = part // heads
        attend_heads_back(
            parts_of(query_ref, heads),
            blocks[:heads],
            blocks[heads:],
            limits_ref[pl.program_id(0)],
            scale,
            logsum_ref,
            parts_of(grad_ref, heads),
            [
                head_writer(out_ref, 0, width),
                head_writer(text_ref, 0, width),
                head_writer(text_ref, part, width),
            ],
        )

    return pl.pallas_call(
        kernel,
        grid_spec=pltpu.PrefetchScalarGridSpec(
            num_scalar_prefetch=1,
            grid=(images,),
            in_specs=[
                row_block(length, part),
                row_block(slots, 2 * part),
                row_block(length, heads),
                row_block(length, part),
            ],
            out_specs=[row_block(length, part), row_block(slots, 2 * part)],
        ),
        out_shape=[
            jax.ShapeDtypeStruct((rows, part), jnp.bfloat16),
            jax.ShapeDtypeStruct((images * slots, 2 * part), jnp.bfloat16),
        ],
        compiler_params=pltpu.CompilerParams(vmem_limit_bytes=VMEM_LIMIT),
        cost_estimate=attention_cost(images, length, slots, heads, part // heads, 5),
        name="attend_cross_back",
    )(limits, queries, keyval, logsum, grad_mixed)


def pick_blocks(weights, counts, rank):
    rows = weights[0].shape[0]
    width = weights[0].shape[1] // (counts[0] * PEERS)
    firsts = [sum(counts[:i]) for i in range(len(counts))]

    def kernel(rank_ref, *refs):
        step = pl.program_id(0)
        out_ref = refs[-1]
        for ref, first, count in zip(refs, firsts, counts):

            @pl.when((step >= first) & (step < first + count))
            def _():
                out_ref[...] = ref[...]

    def spec(first, count):
        return pl.BlockSpec(
            (rows, width),
            lambda step, rank_ref: (
                0,
                jnp.clip(step - first, 0, count - 1) * PEERS + rank_ref[0],
            ),
        )

    return pl.pallas_call(
        kernel,
        grid_spec=pltpu.PrefetchScalarGridSpec(
            num_scalar_prefetch=1,
            grid=(sum(counts),),
            in_specs=[spec(first, count) for first, count in zip(firsts, counts)],
            out_specs=pl.BlockSpec((rows, width), lambda step, rank_ref: (0, step)),
        ),
        out_shape=jax.ShapeDtypeStruct((rows, width * sum(counts)), weights[0].dtype),
        cost_estimate=cost(0, 4 * rows * width * sum(counts)),
        name="pick_blocks",
    )(rank.reshape(1), *weights)


def spread_blocks(found, first, count, width):
    rows = found.shape[0] // PEERS

    def kernel(found_ref, out_ref):
        for peer in range(PEERS):
            out_ref[:, peer * width : (peer + 1) * width] = found_ref[
                peer * rows : (peer + 1) * rows, :
            ].astype(jnp.float32)

    return pl.pallas_call(
        kernel,
        grid=(count,),
        in_specs=[pl.BlockSpec((PEERS * rows, width), lambda block: (0, first + block))],
        out_specs=pl.BlockSpec((rows, PEERS * width), lambda block: (0, block)),
        out_shape=jax.ShapeDtypeStruct((rows, count * PEERS * width), jnp.float32),
        cost_estimate=cost(0, 6 * rows * count * PEERS * width),
        compiler_params=pltpu.CompilerParams(vmem_limit_bytes=VMEM_LIMIT),
        name="spread_blocks",
    )(found)


def spread_rows(found, width):
    rows = found.shape[0] // PEERS

    def kernel(found_ref, out_ref):
        out_ref[...] = found_ref[...].astype(jnp.float32)

    return pl.pallas_call(
        kernel,
        grid=(PEERS,),
        in_specs=[pl.BlockSpec((rows, width), lambda peer: (peer, 0))],
        out_specs=pl.BlockSpec((rows, width), lambda peer: (peer, 0)),
        out_shape=jax.ShapeDtypeStruct((PEERS * rows, width), jnp.float32),
        cost_estimate=cost(0, 6 * PEERS * rows * width),
        compiler_params=pltpu.CompilerParams(vmem_limit_bytes=VMEM_LIMIT),
        name="spread_rows",
    )(found)


PEERS = 4


def swap(value, mask):
    return lax.ppermute(value, "rep", [(peer, peer ^ mask) for peer in range(PEERS)])


def stack_rows(parts):
    rows, columns = parts[0].shape
    count = len(parts)

    def kernel(*refs):
        for i in range(count):

            @pl.when(pl.program_id(0) == i)
            def _():
                refs[-1][...] = refs[i][...]

    return pl.pallas_call(
        kernel,
        grid=(count,),
        in_specs=[pl.BlockSpec((rows, columns), lambda step: (0, 0))] * count,
        out_specs=pl.BlockSpec((rows, columns), lambda step: (step, 0)),
        out_shape=jax.ShapeDtypeStruct((count * rows, columns), parts[0].dtype),
        cost_estimate=cost(0, 4 * count * rows * columns),
        compiler_params=pltpu.CompilerParams(vmem_limit_bytes=VMEM_LIMIT),
        name="stack_rows",
    )(*parts)


def stack_columns(parts):
    orders = ((0, 1, 2, 3), (2, 3, 0, 1), (1, 0, 3, 2), (3, 2, 1, 0))
    rows, columns = parts[0].shape
    block = rows // PEERS

    def kernel(*refs):
        for i, order in enumerate(orders):

            @pl.when(pl.program_id(0) == i)
            def _():
                for j, source in enumerate(order):
                    refs[-1][j * block : (j + 1) * block, :] = refs[i][
                        source * block : (source + 1) * block, :
                    ]

    return pl.pallas_call(
        kernel,
        grid=(PEERS,),
        in_specs=[pl.BlockSpec((rows, columns), lambda step: (0, 0))] * PEERS,
        out_specs=pl.BlockSpec((rows, columns), lambda step: (0, step)),
        out_shape=jax.ShapeDtypeStruct((rows, PEERS * columns), parts[0].dtype),
        cost_estimate=cost(0, 4 * PEERS * rows * columns),
        compiler_params=pltpu.CompilerParams(vmem_limit_bytes=VMEM_LIMIT),
        name="stack_columns",
    )(*parts)


def narrow(total):
    return (total.astype(jnp.bfloat16),)


def plus(total, extra):
    return (total + extra.astype(jnp.float32),)


def narrow_plus(total, extra):
    return ((total + extra.astype(jnp.float32)).astype(jnp.bfloat16),)


def halves(total):
    rows = total.shape[0] // 2
    return (total[:rows].astype(jnp.bfloat16), total[rows:].astype(jnp.bfloat16))


def scaled(total, factor):
    return ((total * factor.astype(jnp.float32)).astype(jnp.bfloat16),)


def gate_and_slope(total):
    value, back = jax.vjp(smooth_gate, total)
    return (value.astype(jnp.bfloat16), back(jnp.ones_like(total))[0].astype(jnp.bfloat16))


def multiply(
    left, right, turned, finish=narrow, types=(jnp.bfloat16,), first=0, rows=None, extra=None, half=None
):
    rows = left.shape[0] if rows is None else rows
    depth = left.shape[1]
    breadth = right.shape[1] // (1 if half is None else 2)
    columns = right.shape[0] if turned else breadth
    width = min(512, columns)
    skip = 0 if half is None else half * breadth // (depth if turned else width)
    product = back_product if turned else matmul
    tall = rows // 2 if finish is halves else rows

    def kernel(*refs):
        left_ref, right_ref = refs[:2]
        outs = refs[-len(types) :]
        blocks = [ref[...] for ref in refs[2 : -len(types)]]
        for out, value in zip(outs, finish(product(left_ref[...], right_ref[...]), *blocks)):
            out[...] = value

    specs = [
        pl.BlockSpec((rows, depth), lambda step: (first // rows, 0)),
        pl.BlockSpec((width, depth), lambda step: (step, skip))
        if turned
        else pl.BlockSpec((depth, width), lambda step: (0, skip + step)),
    ]
    values = [left, right]
    if extra is not None:
        extra, start = extra
        specs.append(pl.BlockSpec((rows, width), lambda step: (start // rows, step)))
        values.append(extra)
    found = pl.pallas_call(
        kernel,
        grid=(columns // width,),
        in_specs=specs,
        out_specs=[pl.BlockSpec((tall, width), lambda step: (0, step))] * len(types),
        out_shape=[jax.ShapeDtypeStruct((tall, columns), kind) for kind in types],
        cost_estimate=cost(2 * rows * depth * columns, 2 * (rows * depth + depth * columns + rows * columns)),
        compiler_params=pltpu.CompilerParams(vmem_limit_bytes=VMEM_LIMIT),
        name="multiply",
    )(*values)
    return found[0] if len(types) == 1 else found


def weight_term(left, right, column_block=None):
    depth, rows = left.shape
    columns = right.shape[1] if column_block is None else right.shape[1] // PEERS
    height, width = min(1024, rows), min(512, columns)
    shift = columns // width
    chosen = jnp.zeros((1,), jnp.int32) if column_block is None else column_block.reshape(1)

    def kernel(chosen_ref, left_ref, right_ref, out_ref):
        out_ref[...] = outer_sum(left_ref[...], right_ref[...]).astype(jnp.bfloat16)

    return pl.pallas_call(
        kernel,
        grid_spec=pltpu.PrefetchScalarGridSpec(
            num_scalar_prefetch=1,
            grid=(columns // width, rows // height),
            in_specs=[
                pl.BlockSpec((depth, height), lambda j, i, chosen_ref: (0, i)),
                pl.BlockSpec(
                    (depth, width), lambda j, i, chosen_ref: (0, chosen_ref[0] * shift + j)
                ),
            ],
            out_specs=pl.BlockSpec((height, width), lambda j, i, chosen_ref: (i, j)),
        ),
        out_shape=jax.ShapeDtypeStruct((rows, columns), jnp.bfloat16),
        cost_estimate=cost(2 * rows * depth * columns, 2 * (rows * depth + depth * columns + rows * columns)),
        compiler_params=pltpu.CompilerParams(vmem_limit_bytes=VMEM_LIMIT),
        name="weight_term",
    )(chosen, left, right)


def multiply_rest(left, right, turned, got):
    (rows, columns), depth = got[0].shape, left.shape[1]
    width = min(512, columns)
    product = back_product if turned else matmul

    def kernel(left_ref, right_ref, got_ref, got_far_ref, own_ref, far_ref):
        total = product(left_ref[...], right_ref[...])
        own_ref[...] = total[:rows] + got_ref[...].astype(jnp.float32)
        far_ref[...] = (total[rows:] + got_far_ref[...].astype(jnp.float32)).astype(jnp.bfloat16)

    return pl.pallas_call(
        kernel,
        grid=(columns // width,),
        in_specs=[
            pl.BlockSpec((2 * rows, depth), lambda step: (0, 0)),
            pl.BlockSpec((width, depth), lambda step: (step, 0))
            if turned
            else pl.BlockSpec((depth, width), lambda step: (0, step)),
        ]
        + [pl.BlockSpec((rows, width), lambda step: (0, step))] * 2,
        out_specs=[pl.BlockSpec((rows, width), lambda step: (0, step))] * 2,
        out_shape=[
            jax.ShapeDtypeStruct((rows, columns), jnp.float32),
            jax.ShapeDtypeStruct((rows, columns), jnp.bfloat16),
        ],
        cost_estimate=cost(
            4 * rows * depth * columns, 2 * (2 * rows * depth + depth * columns + 5 * rows * columns)
        ),
        compiler_params=pltpu.CompilerParams(vmem_limit_bytes=VMEM_LIMIT),
        name="multiply_rest",
    )(left, right, *got)


class Order:
    def __init__(self):
        self.token = ()

    def run(self, work, first, *others):
        if self.token:
            first, self.token = lax.optimization_barrier((first, self.token))
        found = work(first, *others)
        self.token = tuple(jax.tree.leaves(found))
        return found

    def hold(self, value):
        value, self.token = lax.optimization_barrier((value, self.token))
        return value

    def tick(self, *rings):
        heads = [ring.pieces[-1] for ring in rings]
        heads, self.token = lax.optimization_barrier((heads, self.token))
        for ring, head in zip(rings, heads):
            ring.pieces[-1] = head
            if ring.sevenths < 7:
                ring.send()

    def wait(self, *values):
        self.token = self.token + tuple(jax.tree.leaves(values))


class GroupSum:
    def __init__(self, order, left, right, turned, half=None):
        self.order, self.left, self.right, self.turned = order, left, right, turned
        self.half = half
        self.rows = left.shape[0] // PEERS

    def near(self):
        rows = self.rows
        sent = self.order.run(
            lambda left: multiply(
                left,
                self.right,
                self.turned,
                halves,
                (jnp.bfloat16, jnp.bfloat16),
                first=2 * rows,
                rows=2 * rows,
            ),
            self.left,
        )
        self.got = [swap(part, 1) for part in sent]

    def rest(self):
        self.mine, self.sent = self.order.run(
            lambda left: multiply_rest(left, self.right, self.turned, self.got), self.left
        )
        self.crossed = swap(self.sent, 2)

    def send(self):
        self.near()
        self.rest()
        return self

def ring_member(place, size):
    place = place % size
    return jnp.where(place < size // 2, 2 * place, 2 * (size - 1 - place) + 1)


def ring_pairs(size, step):
    order = [2 * i for i in range(size // 2)] + [2 * i + 1 for i in reversed(range(size // 2))]
    return [(order[i], order[(i + step) % size]) for i in range(size)]


def after(value, earlier):
    return lax.optimization_barrier((value, earlier))[0]


class Gather:
    def __init__(self, value, size, step):
        self.size, self.step, self.pieces = size, step, [value]
        self.sevenths = 0

    def send(self):
        self.sevenths += 1
        while len(self.pieces) - 1 < self.sevenths * (self.size - 1) // 7:
            self.pieces.append(
                lax.ppermute(self.pieces[-1], "fsdp", ring_pairs(self.size, self.step))
            )

    def starts(self, place, rows):
        return jnp.stack(
            [ring_member(place - self.step * k, self.size) * rows for k in range(self.size)]
        ).astype(jnp.int32)


def lay_out(pieces, starts, widths):
    size = len(pieces)
    rows = pieces[0].shape[0]
    count = len(widths)
    edges = [sum(widths[:i]) for i in range(count)]

    def kernel(starts_ref, *refs):
        shards, outs, done = refs[:size], refs[size:-1], refs[-1]
        copies = []
        for i, shard in enumerate(shards):
            start = pl.multiple_of(starts_ref[i], rows)
            for j, out in enumerate(outs):
                copies.append(
                    pltpu.make_async_copy(
                        shard.at[:, edges[j] : edges[j] + widths[j]],
                        out.at[pl.ds(start, rows), :],
                        done.at[i, j],
                    )
                )
        for copy in copies:
            copy.start()
        for copy in copies:
            copy.wait()

    return pl.pallas_call(
        kernel,
        out_shape=[jax.ShapeDtypeStruct((size * rows, w), pieces[0].dtype) for w in widths],
        in_specs=[pl.BlockSpec(memory_space=pltpu.SMEM)]
        + [pl.BlockSpec(memory_space=pltpu.VMEM)] * size,
        out_specs=[pl.BlockSpec(memory_space=pl.ANY)] * count,
        scratch_shapes=[pltpu.SemaphoreType.DMA((size, count))],
        compiler_params=pltpu.CompilerParams(vmem_limit_bytes=VMEM_LIMIT),
        cost_estimate=cost(0, 4 * size * rows * sum(widths)),
        name="lay_out",
    )(starts, *pieces)


def ring_add(entries, spots, rows, got):
    flat = [value for values in entries for value in values]
    lengths = [sum(value.shape[1] for value in values) for values in entries]
    count = len(flat)

    def kernel(spots_ref, *refs):
        outs = refs[-len(entries) :]
        i = 0
        for entry, values in enumerate(entries):
            first = 0
            for value in values:
                place = slice(first, first + value.shape[1])
                block = refs[i][...]
                if got is not None:
                    here = refs[count + entry][:, place].astype(jnp.float32)
                    block = (here + block.astype(jnp.float32)).astype(jnp.bfloat16)
                outs[entry][:, place] = block
                first += value.shape[1]
                i += 1

    def spec(i):
        return pl.BlockSpec(
            (rows, flat[i].shape[1]), lambda step, spots_ref: (spots_ref[i], 0)
        )

    plain = [pl.BlockSpec((rows, length), lambda step, spots_ref: (0, 0)) for length in lengths]
    arrived = [] if got is None else list(got)
    return pl.pallas_call(
        kernel,
        grid_spec=pltpu.PrefetchScalarGridSpec(
            num_scalar_prefetch=1,
            grid=(1,),
            in_specs=[spec(i) for i in range(count)] + plain[: len(arrived)],
            out_specs=plain,
        ),
        out_shape=[jax.ShapeDtypeStruct((rows, length), jnp.bfloat16) for length in lengths],
        cost_estimate=cost(rows * sum(lengths), 6 * rows * sum(lengths)),
        compiler_params=pltpu.CompilerParams(vmem_limit_bytes=VMEM_LIMIT),
        name="ring_add",
    )(spots, *flat, *arrived)


class Scatter:
    def __init__(self, order, entries, size, place, rows):
        self.order, self.entries = order, entries
        self.size, self.place, self.rows, self.step = size, place, rows, 0
        self.values = [[value for value, _ in values] for values, _, _ in entries]
        self.sums = order.run(
            lambda first: ring_add(
                [[first] + self.values[0][1:]] + self.values[1:], self.spots(), self.rows, None
            ),
            self.values[0][0],
        )

    def spots(self):
        found = []
        for values, direction, block in self.entries:
            shard = ring_member(self.place - direction * (self.step + 1), self.size)
            found += [rows_of(shard) // self.rows + block for _, rows_of in values]
        return jnp.stack(found).astype(jnp.int32)

    def reach(self, seventh):
        while self.step < seventh * (self.size - 1) // 7:
            self.step += 1
            arrived = [
                lax.ppermute(value, "fsdp", ring_pairs(self.size, direction))
                for value, (_, direction, _) in zip(self.sums, self.entries)
            ]
            spots = self.spots()
            self.sums = self.order.run(
                lambda got: ring_add(self.values, spots, self.rows, got), arrived
            )


def exchange(value, size, between):
    value = value[None]
    member = lax.axis_index("fsdp")
    mask = 1
    while mask < size:
        other = between(lax.ppermute(value, "fsdp", [(i, i ^ mask) for i in range(size)]))
        low = (member & mask) == 0
        value = jnp.concatenate(
            [jnp.where(low, value, other), jnp.where(low, other, value)], axis=0
        )
        mask *= 2
    return value


class Everyone:
    def __init__(self, order, value, size):
        self.order, self.value = order, value
        self.hops = [("fsdp", size // 2 >> i, size) for i in range(size.bit_length() - 1)]
        self.hops += [("rep", 2, PEERS), ("rep", 1, PEERS)]
        self.send()

    def send(self):
        axis, mask, size = self.hops.pop(0)
        self.got = lax.ppermute(self.value, axis, [(i, i ^ mask) for i in range(size)])

    def hop(self, count=1):
        for _ in range(count):
            self.value = self.order.run(
                lambda got: jnp.concatenate([self.value, got], axis=0), self.got
            )
            if self.hops:
                self.send()


def body(
    image_tokens,
    text_tokens,
    text_lengths,
    timesteps,
    cotangent,
    mod_weight,
    qkv_weight,
    out_weight,
    query_weight,
    keyval_weight,
    merge_weight,
    cross_gain,
    up_weight,
    down_weight,
):
    images, length, width = image_tokens.shape
    text_count, text_width = text_tokens.shape[1:]
    group = lax.axis_size("fsdp")
    rank = lax.axis_index("rep")
    member = lax.axis_index("fsdp")
    heads = HEADS // PEERS
    head_width = width // HEADS
    part = width // PEERS
    score_scale = head_width ** (-0.5)
    shard_rows = mod_weight.shape[0]
    hidden = up_weight.shape[1]
    rows = images * length
    all_images = PEERS * images

    def own_part(value, blocks):
        count = value.shape[1] // (blocks * PEERS)
        return lax.dynamic_index_in_dim(
            value.reshape(value.shape[0], blocks, PEERS, count), rank, 2, keepdims=False
        ).reshape(value.shape[0], blocks * count)

    def ordered(found):
        stacked = jnp.stack(found)
        return [
            lax.dynamic_index_in_dim(stacked, rank ^ place, 0, keepdims=False)
            for place in range(PEERS)
        ]

    def columns_to_rows(value):
        blocks = value.reshape(PEERS, part, -1)
        found = [
            lax.dynamic_index_in_dim(blocks, rank ^ mask, 0, keepdims=False)
            for mask in range(PEERS)
        ]
        found = [found[0]] + [swap(found[mask], mask) for mask in range(1, PEERS)]
        return jnp.concatenate(ordered(found), axis=1)

    order = Order()
    aligned = hidden // (group * PEERS) % 128 == 0
    spot = jnp.where(member % 2 == 0, member // 2, group - 1 - member // 2)
    def flatten(value):
        return value.reshape(-1, value.shape[-1])

    def own_rows(value):
        return value.reshape(images, length, width)

    first_pick = order.run(lambda w: pick_blocks([w, out_weight], [3, 1], rank), qkv_weight)
    second_pick = order.run(
        lambda w: pick_blocks([w, keyval_weight, merge_weight], [1, 2, 1], rank), query_weight
    )
    first, second = Gather(first_pick, group, 1), Gather(second_pick, group, -1)
    order.tick(first, second)
    picks = [
        lambda w: pick_blocks([w], [group], rank) if aligned else own_part(w, group),
        lambda w: lax.dynamic_index_in_dim(
            w.reshape(PEERS, -1, width), rank, 0, keepdims=False
        ),
    ]
    sources = [up_weight, down_weight]
    picked = []

    def pick_between(value):
        if len(picked) < len(picks):
            i = len(picked)
            picked.append(order.run(picks[i], sources[i]))
        return after(value, order.token)

    small = exchange(
        jnp.concatenate([timesteps.astype(jnp.float32), cross_gain.astype(jnp.float32)]),
        group,
        pick_between,
    )
    while len(picked) < len(picks):
        pick_between(small)
    third_pick, fourth_pick = picked
    small = order.hold(small)
    order.tick(first, second)
    group_steps = small[:, :images].reshape(-1)
    gain_full = small[:, images:].reshape(-1)
    sequence = [0]
    while len(sequence) < group:
        sequence += [index + group // (2 * len(sequence)) for index in sequence]
    all_steps = small[:, :images][member ^ jnp.array(sequence, dtype=jnp.int32)].reshape(-1)
    all_steps = jnp.concatenate([all_steps, swap(all_steps, 2)])
    all_steps = jnp.concatenate([all_steps, swap(all_steps, 1)])
    length_far = swap(text_lengths, 2)
    length_all = jnp.concatenate(
        [text_lengths, length_far, swap(text_lengths, 1), swap(length_far, 1)]
    )

    half_width = width // 2
    column = member * shard_rows + jnp.arange(shard_rows, dtype=jnp.int32)
    place = jnp.where(column < half_width, column, column - half_width)
    frequency = jnp.exp(-math.log(10000.0) * place.astype(jnp.float32) / half_width)

    def conditions(steps):
        angles = steps.astype(jnp.float32)[:, None] * frequency[None, :]
        return jnp.where(column < half_width, jnp.sin(angles), jnp.cos(angles)).astype(
            jnp.bfloat16
        )

    terms = order.run(lambda steps: matmul(conditions(steps), mod_weight), group_steps)
    found = lax.all_to_all(
        terms.reshape(group, images, -1), "fsdp", split_axis=0, concat_axis=0, tiled=True
    )
    order.wait(all_steps, length_all)
    residual = image_tokens.astype(jnp.float32)
    grad_block = cotangent.astype(jnp.float32)

    def start(found):
        pieces = jnp.sum(found, axis=0).reshape(images, 6, 1, width)
        act = flatten(normed(residual) * (1.0 + pieces[:, 1]) + pieces[:, 0])
        return pieces, act.astype(jnp.bfloat16)

    pieces, act_one = order.run(start, found)
    shift_self, scale_self, gate_self = (pieces[:, 0], pieces[:, 1], pieces[:, 2])
    shift_mlp, scale_mlp, gate_mlp = (pieces[:, 3], pieces[:, 4], pieces[:, 5])
    norm_one = normed(residual)

    def send_rows(value):
        return [value, swap(value, 2), swap(value, 1)]

    def join_rows(parts):
        far = order.hold(parts[1])
        return order.run(
            lambda last: stack_rows([parts[0], far, parts[2], last]), swap(far, 1)
        )

    def send_columns(value):
        return [value, swap(value, 1), swap(value, 2)]

    def join_columns(parts):
        far = order.hold(parts[2])
        return order.run(
            lambda last: stack_columns([parts[0], parts[1], far, last]), swap(far, 1)
        )

    act_one = send_rows(act_one)
    text_all = send_rows(after(flatten(text_tokens), act_one[1]))
    order.tick(first, second)
    grad_three = order.run(lambda gate: flatten(gate * grad_block).astype(jnp.bfloat16), gate_mlp)
    order.tick(first, second)
    act_one = join_rows(act_one)
    order.tick(first, second)
    text_all = join_rows(text_all)
    order.tick(first, second)
    order.tick(first, second)
    third, fourth = Gather(third_pick, group, 1), Gather(fourth_pick, group, -1)
    order.tick(first, second, third, fourth)

    qkv_part, out_part = order.run(
        lambda last: lay_out(
            first.pieces[:-1] + [last], first.starts(spot, shard_rows), [3 * part, part]
        ),
        first.pieces[-1],
    )
    out_part = columns_to_rows(out_part)
    query_part, keyval_part, merge_part = order.run(
        lambda last: lay_out(
            second.pieces[:-1] + [last], second.starts(spot, shard_rows), [part, 2 * part, part]
        ),
        second.pieces[-1],
    )
    merge_part = columns_to_rows(merge_part)
    qkv_act = order.run(lambda a: multiply(a, qkv_part, False), act_one)
    order.tick(third, fourth)
    keyval = order.run(lambda a: multiply(a, keyval_part, False), text_all)
    mixed_flat, logsum_self = order.run(
        lambda a: attend_self(a, all_images, heads, score_scale), qkv_act
    )
    order.wait(out_part)
    branch_sum = GroupSum(order, mixed_flat, out_part, False)
    branch_sum.near()
    order.tick(third, fourth)
    branch_sum.rest()
    order.wait(merge_part)
    order.tick(third, fourth)

    def finish_self(crossed):
        branch_one = own_rows(branch_sum.mine + crossed.astype(jnp.float32))
        hidden_one = residual + gate_self * branch_one
        return (
            branch_one,
            hidden_one,
            flatten(normed(hidden_one) * gain_full).astype(jnp.bfloat16),
        )

    branch_one, hidden_one, act_two = order.run(finish_self, branch_sum.crossed)
    norm_two = normed(hidden_one)
    act_two = send_rows(act_two)
    grad_three = send_rows(after(grad_three, act_two[1]))
    order.tick(third, fourth)
    act_two = join_rows(act_two)
    cross_queries = order.run(lambda a: multiply(a, query_part, False), act_two)
    cross_flat, logsum_cross = order.run(
        lambda a: attend_cross(a, keyval, length_all, all_images, heads, score_scale),
        cross_queries,
    )
    branch_sum = GroupSum(order, cross_flat, merge_part, False)
    branch_sum.near()
    order.tick(third, fourth)
    branch_sum.rest()
    order.tick(third, fourth)

    def finish_cross(crossed):
        hidden_two = hidden_one + own_rows(branch_sum.mine + crossed.astype(jnp.float32))
        act = flatten(normed(hidden_two) * (1.0 + scale_mlp) + shift_mlp)
        return hidden_two, act.astype(jnp.bfloat16)

    hidden_two, act_three = order.run(finish_cross, branch_sum.crossed)
    norm_three = normed(hidden_two)
    act_three = send_rows(act_three)
    mixed_parts = send_columns(after(mixed_flat, act_three[1]))
    order.tick(third, fourth)
    act_three = join_rows(act_three)
    grad_three = join_rows(grad_three)
    cross_parts = send_columns(after(cross_flat, mixed_parts[2]))

    (up_part,) = order.run(
        lambda last: lay_out(
            third.pieces[:-1] + [last], third.starts(spot, shard_rows), [hidden // PEERS]
        ),
        third.pieces[-1],
    )
    activated, slope = order.run(
        lambda a: multiply(a, up_part, False, gate_and_slope, (jnp.bfloat16, jnp.bfloat16)),
        act_three,
    )
    (down_part,) = order.run(
        lambda last: lay_out(
            fourth.pieces[:-1] + [last], fourth.starts(spot, shard_rows), [width]
        ),
        fourth.pieces[-1],
    )
    mixed_all = join_columns(mixed_parts)

    def shard_start(shard):
        return shard * shard_rows

    def swapped_start(shard):
        begin = shard * shard_rows
        return ((begin // part) ^ rank) * part + begin % part

    def ring(values):
        return Scatter(order, [(values, 1, 0), (values, -1, 1)], group, spot, shard_rows // 2)

    grad_pre = order.run(
        lambda a: multiply(a, down_part, True, scaled, extra=(slope, 0)), grad_three
    )
    branch_sum = GroupSum(order, grad_pre, up_part, True).send()
    down_term = order.run(lambda a: weight_term(a, grad_three), activated)
    up_term = order.run(lambda a: weight_term(a, grad_pre), act_three)
    mlp_ring = Scatter(
        order,
        [([(down_term, shard_start)], 1, 0), ([(up_term, shard_start)], -1, 0)],
        group,
        spot,
        shard_rows,
    )

    def finish_mlp_back(crossed):
        grad_act = own_rows(branch_sum.mine + crossed.astype(jnp.float32))
        grad_two = grad_block + normed_back(hidden_two, grad_act * (1.0 + scale_mlp))
        return (
            jnp.sum(grad_act, axis=1),
            jnp.sum(grad_act * norm_three, axis=1),
            grad_two,
            flatten(grad_two).astype(jnp.bfloat16),
        )

    grad_shift_mlp, grad_scale_mlp, grad_two, grad_merge = order.run(
        finish_mlp_back, branch_sum.crossed
    )
    grad_merge = send_rows(grad_merge)
    cross_all_heads = join_columns(cross_parts)
    mlp_ring.reach(1)
    grad_merge = join_rows(grad_merge)

    grad_mixed = order.run(lambda a: multiply(a, merge_part, True), grad_merge)
    grad_query, grad_keyval = order.run(
        lambda a: attend_cross_back(
            cross_queries, keyval, length_all, logsum_cross, a, all_images, heads, score_scale
        ),
        grad_mixed,
    )
    branch_sum = GroupSum(order, grad_query, query_part, True)
    branch_sum.near()
    mlp_ring.reach(2)
    branch_sum.rest()
    query_term = order.run(lambda a: weight_term(a, grad_query), act_two)
    keyval_term = order.run(lambda a: weight_term(a, grad_keyval), text_all)
    merge_term = order.run(lambda a: weight_term(a, grad_merge, rank), cross_all_heads)
    cross_ring = ring(
        [(query_term, shard_start), (keyval_term, shard_start), (merge_term, swapped_start)]
    )
    mlp_ring.reach(3)

    def finish_cross_back(crossed):
        grad_act = own_rows(branch_sum.mine + crossed.astype(jnp.float32))
        grad_one = grad_two + normed_back(hidden_one, grad_act * gain_full)
        return (
            jnp.sum(grad_act * norm_two, axis=1),
            jnp.sum(grad_one * branch_one, axis=1),
            grad_one,
            flatten(gate_self * grad_one).astype(jnp.bfloat16),
        )

    gain_term, grad_gate_self, grad_one, grad_out = order.run(
        finish_cross_back, branch_sum.crossed
    )
    grad_out = send_rows(grad_out)
    mlp_ring.reach(4)
    cross_ring.reach(1)
    grad_out = join_rows(grad_out)

    grad_mixed = order.run(lambda a: multiply(a, out_part, True), grad_out)
    grad_qkv = order.run(
        lambda a: attend_self_back(qkv_act, logsum_self, a, all_images, heads, score_scale),
        grad_mixed,
    )
    branch_sum = GroupSum(order, grad_qkv, qkv_part, True)
    branch_sum.near()
    mlp_ring.reach(5)
    cross_ring.reach(2)
    branch_sum.rest()
    qkv_term = order.run(lambda a: weight_term(a, grad_qkv), act_one)
    out_term = order.run(lambda a: weight_term(a, grad_out, rank), mixed_all)
    self_ring = ring([(qkv_term, shard_start), (out_term, swapped_start)])
    mlp_ring.reach(6)
    cross_ring.reach(3)

    def finish_self_back(crossed):
        grad_act = own_rows(branch_sum.mine + crossed.astype(jnp.float32))
        image_grad = grad_one + normed_back(residual, grad_act * (1.0 + scale_self))
        return (
            jnp.sum(grad_act, axis=1),
            jnp.sum(grad_act * norm_one, axis=1),
            image_grad.astype(jnp.bfloat16),
        )

    grad_shift_self, grad_scale_self, image_grad = order.run(finish_self_back, branch_sum.crossed)

    cross_ring.reach(4)
    self_ring.reach(1)
    mlp_sum = GroupSum(order, activated, down_part, False)
    mlp_sum.near()
    mlp_ring.reach(7)
    down_all, up_all = [
        lax.all_gather(found, "rep", axis=0, tiled=True) for found in mlp_ring.sums
    ]
    mlp_sum.rest()
    cross_ring.reach(5)
    self_ring.reach(2)

    def finish_mlp(crossed):
        branch_three = own_rows(mlp_sum.mine + crossed.astype(jnp.float32))
        block_out = (hidden_two + gate_mlp * branch_three).astype(jnp.bfloat16)
        vectors = jnp.concatenate(
            [
                grad_shift_self,
                grad_scale_self,
                grad_gate_self,
                grad_shift_mlp,
                grad_scale_mlp,
                jnp.sum(grad_block * branch_three, axis=1),
                gain_term,
            ],
            axis=1,
        )
        return block_out, vectors.astype(jnp.bfloat16)

    block_out, vectors = order.run(finish_mlp, mlp_sum.crossed)
    everyone = Everyone(order, vectors, group)
    cross_ring.reach(6)
    self_ring.reach(3)
    everyone.hop()
    text_sum = GroupSum(order, grad_keyval, keyval_part, True)
    text_sum.near()
    cross_ring.reach(7)
    cross_all = lax.all_gather(jnp.concatenate(cross_ring.sums, axis=0), "rep", axis=0, tiled=True)
    self_ring.reach(4)
    text_sum.rest()
    everyone.hop()
    self_ring.reach(5)
    everyone.hop()
    down_grad = order.run(lambda a: spread_rows(a, width), down_all)
    text_grad = order.run(
        lambda crossed: (text_sum.mine + crossed.astype(jnp.float32))
        .astype(jnp.bfloat16)
        .reshape(text_tokens.shape),
        text_sum.crossed,
    )
    self_ring.reach(6)
    everyone.hop(len(everyone.hops))
    if aligned:
        up_grad = order.run(
            lambda a: spread_blocks(a, 0, group, hidden // (group * PEERS)), up_all
        )
    else:
        up_grad = (
            up_all.reshape(PEERS, shard_rows, group, -1)
            .transpose(1, 2, 0, 3)
            .reshape(shard_rows, hidden)
            .astype(jnp.float32)
        )
    self_ring.reach(7)
    self_all = lax.all_gather(
        jnp.concatenate(self_ring.sums, axis=0), "rep", axis=0, tiled=True
    )
    everyone.hop(1 + len(everyone.hops))

    def finish_modulation(found):
        return (
            outer_sum(conditions(all_steps), found[:, : 6 * width]),
            jnp.sum(
                lax.dynamic_slice_in_dim(
                    found, 6 * width + member * shard_rows, shard_rows, 1
                ).astype(jnp.float32),
                axis=0,
            ),
        )

    mod_grad, gain_grad = order.run(finish_modulation, everyone.value)
    query_grad = order.run(lambda a: spread_blocks(a, 0, 1, part), cross_all)
    keyval_grad = order.run(lambda a: spread_blocks(a, 1, 2, part), cross_all)
    merge_grad = order.run(lambda a: spread_blocks(a, 3, 1, part), cross_all)
    return (
        block_out,
        image_grad,
        text_grad,
        mod_grad,
        order.run(lambda a: spread_blocks(a, 0, 3, part), self_all),
        order.run(lambda a: spread_blocks(a, 3, 1, part), self_all),
        query_grad,
        keyval_grad,
        merge_grad,
        gain_grad,
        up_grad,
        down_grad,
    )


def solution(mesh):
    placed = (
        P(("rep", "fsdp"), None, None),
        P(("rep", "fsdp"), None, None),
        P(("rep", "fsdp")),
        P(("rep", "fsdp")),
        P(("rep", "fsdp"), None, None),
        P("fsdp", None),
        P("fsdp", None),
        P("fsdp", None),
        P("fsdp", None),
        P("fsdp", None),
        P("fsdp", None),
        P("fsdp"),
        P("fsdp", None),
        P("fsdp", None),
    )
    return jax.shard_map(
        body,
        mesh=mesh,
        in_specs=placed,
        out_specs=(
            P(("rep", "fsdp"), None, None),
            P(("rep", "fsdp"), None, None),
            P(("rep", "fsdp"), None, None),
            P("fsdp", None),
            P("fsdp", None),
            P("fsdp", None),
            P("fsdp", None),
            P("fsdp", None),
            P("fsdp", None),
            P("fsdp"),
            P("fsdp", None),
            P("fsdp", None),
        ),
        check_vma=False,
    )
```

time: 1270 us -> 1080 us (0.85)
  Pallas kernels: 100 us -> 366 us
  matrix products: 206 us -> 10.9 us
  waiting for transfers between devices: 582 us -> 454 us
  local copies, waits for them, and re-layouts: 113 us -> 49.1 us
  starting transfers between devices: 162 us -> 128 us
  other arithmetic: 75.1 us -> 46.7 us
    pallas_call x10 -> x72, Pallas kernels: 65.6 us -> 331 us  [the longest x14 95.2 us: multiply(): pl.pallas_call(kernel, grid=(columns // width,), in_specs=specs, out_spec...]
    ppermute x113 -> x78, waiting for transfers between devices: 401 us -> 311 us  [the longest x28 181 us: send(): lax.ppermute(self.pieces[-1], 'fsdp', ring_pairs(self.size, self.step))]
    dot_general x15 -> x0, matrix products: 74.7 us -> none  [back_product(): lax.dot_general(left, right, (((1,), (1,)), ((), ())), preferred_element_...]
    dot_general x14 -> x1, matrix products: 71.6 us -> 3.79 us  [matmul(): return jnp.dot(left, right, preferred_element_type=jnp.float32)]
    dot_general x8 -> x1, matrix products: 59.5 us -> 7.07 us  [outer_sum(): lax.dot_general(left, right, (((0,), (0,)), ((), ())), preferred_element_...]
    ppermute x56 -> x59, waiting for transfers between devices: 173 us -> 128 us  [swap(): lax.ppermute(value, 'rep', [(peer, peer ^ mask) for peer in range(PEERS)])]
    ppermute x113 -> x78, starting transfers between devices: 125 us -> 81.7 us  [the longest x42 43.5 us: reach(): lax.ppermute(value, 'fsdp', ring_pairs(self.size, direction))]
    dynamic_slice x16 -> x0, local copies, waits for them, and re-layouts: 42.5 us -> none  [the longest x7 24 us: piece(): lax.dynamic_slice_in_dim(v, start, half, 0)]
  transfers between devices with their start and end apart: 173 -> 142, of which waited for: 76 -> 72; matrix products, arithmetic and copies ran while one was open for 27% -> 6% of each run, Pallas kernels for 7% -> 29%
where the time goes in v3:
time: 1080 us; the launch traced here: 1070 us
  waiting for transfers between devices  454 us (42%)
  Pallas kernels  366 us (34%)
  starting transfers between devices  128 us (12%)
  local copies, waits for them, and re-layouts  49.1 us (5%)
  other arithmetic  46.7 us (4%)
  between operations  17.2 us (2%)
  matrix products  10.9 us (1%)
    ppermute x28, waiting for transfers between devices, send(): lax.ppermute(self.pieces[-1], 'fsdp', ring_pairs(self.size, self.step))  181 us
    ppermute x59, waiting for transfers between devices, swap(): lax.ppermute(value, 'rep', [(peer, peer ^ mask) for peer in range(PEERS)])  128 us
    ppermute x42, waiting for transfers between devices, reach(): lax.ppermute(value, 'fsdp', ring_pairs(self.size, direction))  106 us
    pallas_call x14, Pallas kernels, multiply(): pl.pallas_call(kernel, grid=(columns // width,), in_specs=specs, out_spec...  95.2 us
    pallas_call x24, Pallas kernels, ring_add(): pl.pallas_call(kernel, grid_spec=pltpu.PrefetchScalarGridSpec(num_scalar_...  68.5 us
    pallas_call x7, Pallas kernels, weight_term(): pl.pallas_call(kernel, grid_spec=pltpu.PrefetchScalarGridSpec(num_scalar_...  57.7 us
    ppermute x42, starting transfers between devices, reach(): lax.ppermute(value, 'fsdp', ring_pairs(self.size, direction))  43.5 us
    pallas_call x7, Pallas kernels, multiply_rest(): pl.pallas_call(kernel, grid=(columns // width,), in_specs=[pl.BlockSpec((...  42.6 us
  transfers between devices with their start and end apart: 142, of which 72 were waited for; matrix products, arithmetic and copies ran while one was open for 6% of the time, Pallas kernels for 29%

profile of v3, /device:TPU:0, one launch (start us, length us, event | category | flops | bytes accessed | tf_op | source)
XLA Modules:
  0.0 1071.5 jit_solution(16219769351227756000)
XLA Ops:
  29.7 15.2 %collective-permute-done.1 = f32[2,257]{1,0:T(2,128)S(1)} collective-permute-done((f32[2,257]{1,0:T(2,128)S(1)}, f32[2,257]{1,0:T(2,128)S(1)}, u32[]{:S(2)}, u32[]{:S(2)}) %collective-permute-start.1) | collective-permute-done | bytes 2088 | tf_op jit(solution)/shard_map/ppermute | solution.py:723
  80.1 17.8 %collective-permute-done.14.refs_2_ = bf16[256,2048]{1,0:T(8,128)(2,1)} collective-permute-done((bf16[256,2048]{1,0:T(8,128)(2,1)S(1)}, bf16[256,2048]{1,0:T(8,128)(2,1)}, u32[]{:S(2)}, u32[]{:S(2)}) %collective-permute-start.14) | collective-permute-done | bytes 1048608 | tf_op jit(solution)/shard_map/ppermute | solution.py:598
  104.8 19.4 %collective-permute-done.16.refs_3_ = bf16[256,2048]{1,0:T(8,128)(2,1)S(1)} collective-permute-done((bf16[256,2048]{1,0:T(8,128)(2,1)}, bf16[256,2048]{1,0:T(8,128)(2,1)S(1)}, u32[]{:S(2)}, u32[]{:S(2)}) %collective-permute-start.16) | collective-permute-done | bytes 1048608 | tf_op jit(solution)/shard_map/ppermute | solution.py:598
  130.4 18.2 %collective-permute-done.18.refs_4_ = bf16[256,2048]{1,0:T(8,128)(2,1)S(1)} collective-permute-done((bf16[256,2048]{1,0:T(8,128)(2,1)S(1)}, bf16[256,2048]{1,0:T(8,128)(2,1)S(1)}, u32[]{:S(2)}, u32[]{:S(2)}) %collective-permute-start.18) | collective-permute-done | bytes 1048608 | tf_op jit(solution)/shard_map/ppermute | solution.py:598
  156.1 16.1 %collective-permute-done.20.refs_5_ = bf16[256,2048]{1,0:T(8,128)(2,1)S(1)} collective-permute-done((bf16[256,2048]{1,0:T(8,128)(2,1)S(1)}, bf16[256,2048]{1,0:T(8,128)(2,1)S(1)}, u32[]{:S(2)}, u32[]{:S(2)}) %collective-permute-start.20) | collective-permute-done | bytes 1048608 | tf_op jit(solution)/shard_map/ppermute | solution.py:598
  175.4 20.0 %collective-permute-done.25.refs_6_ = bf16[256,2048]{1,0:T(8,128)(2,1)} collective-permute-done((bf16[256,2048]{1,0:T(8,128)(2,1)S(1)}, bf16[256,2048]{1,0:T(8,128)(2,1)}, u32[]{:S(2)}, u32[]{:S(2)}) %collective-permute-start.25) | collective-permute-done | bytes 1048608 | tf_op jit(solution)/shard_map/ppermute | solution.py:598
  199.3 17.5 %collective-permute-done.27.refs_7_ = bf16[256,2048]{1,0:T(8,128)(2,1)} collective-permute-done((bf16[256,2048]{1,0:T(8,128)(2,1)}, bf16[256,2048]{1,0:T(8,128)(2,1)}, u32[]{:S(2)}, u32[]{:S(2)}) %collective-permute-start.27) | collective-permute-done | bytes 1048608 | tf_op jit(solution)/shard_map/ppermute | solution.py:598
  238.8 10.0 multiply.63.qkv_ref
  276.6 21.3 %collective-permute-done.33 = bf16[256,2048]{1,0:T(8,128)(2,1)S(1)} collective-permute-done((bf16[256,2048]{1,0:T(8,128)(2,1)S(1)}, bf16[256,2048]{1,0:T(8,128)(2,1)S(1)}, u32[]{:S(2)}, u32[]{:S(2)}) %collective-permute-start.33) | collective-permute-done | bytes 1048608 | tf_op jit(solution)/shard_map/ppermute | solution.py:330
  305.5 21.4 %collective-permute-done.34.refs_1_ = bf16[256,2048]{1,0:T(8,128)(2,1)S(1)} collective-permute-done((bf16[256,2048]{1,0:T(8,128)(2,1)S(1)}, bf16[256,2048]{1,0:T(8,128)(2,1)S(1)}, u32[]{:S(2)}, u32[]{:S(2)}) %collective-permute-start.34) | collective-permute-done | bytes 1048608 | tf_op jit(solution)/shard_map/ppermute | solution.py:330
  327.6 9.8 collective-permute-done.39
  338.4 9.6 collective-permute-done.38
  365.9 8.7 collective-permute-done.50.refs_3_
  385.8 13.1 %collective-permute-done.52.refs_4_ = bf16[256,2048]{1,0:T(8,128)(2,1)S(1)} collective-permute-done((bf16[256,2048]{1,0:T(8,128)(2,1)}, bf16[256,2048]{1,0:T(8,128)(2,1)S(1)}, u32[]{:S(2)}, u32[]{:S(2)}) %collective-permute-start.52) | collective-permute-done | bytes 1048608 | tf_op jit(solution)/shard_map/ppermute | solution.py:598
  407.5 14.8 %collective-permute-done.54.refs_5_ = bf16[256,2048]{1,0:T(8,128)(2,1)S(1)} collective-permute-done((bf16[256,2048]{1,0:T(8,128)(2,1)S(1)}, bf16[256,2048]{1,0:T(8,128)(2,1)S(1)}, u32[]{:S(2)}, u32[]{:S(2)}) %collective-permute-start.54) | collective-permute-done | bytes 1048608 | tf_op jit(solution)/shard_map/ppermute | solution.py:598
  430.7 14.8 %collective-permute-done.56.refs_6_ = bf16[256,2048]{1,0:T(8,128)(2,1)} collective-permute-done((bf16[256,2048]{1,0:T(8,128)(2,1)S(1)}, bf16[256,2048]{1,0:T(8,128)(2,1)}, u32[]{:S(2)}, u32[]{:S(2)}) %collective-permute-start.56) | collective-permute-done | bytes 1048608 | tf_op jit(solution)/shard_map/ppermute | solution.py:598
  456.2 10.6 collective-permute-done.58.refs_7_
  475.8 18.1 %multiply.68 = (bf16[1024,2048]{1,0:T(8,128)(2,1)S(1)}, bf16[1024,2048]{1,0:T(8,128)(2,1)}) custom-call(bf16[1024,2048]{1,0:T(8,128)(2,1)} %stack_rows.10.refs_0_.left_ref, bf16[2048,2048]{1,0:T(8,128)(2,1)} %lay_out.6.refs_1_.right_ref), custom_call_target="tpu_custom_call" | custom-call | flops 8589934592 | bytes 16777216 | tf_op jit(solution)/shard_map/multiply/pallas_call | solution.py:439
  508.6 13.0 %multiply.69.refs_0_.left_ref.right_ref = bf16[1024,2048]{1,0:T(8,128)(2,1)S(1)} custom-call(bf16[1024,2048]{1,0:T(8,128)(2,1)} %stack_rows.11.refs_0_.right_ref, bf16[2048,2048]{1,0:T(8,128)(2,1)} %lay_out.7.refs_1_.right_ref, bf16[1024,2048]{1,0:T(8,128)(2,1)} %get-tuple-element.311.refs_2_), custom_call_target="tpu_custom_call" | custom-call | flops 8589934592 | bytes 16777216 | tf_op jit(solution)/shard_map/multiply/pallas_call | solution.py:439
  523.6 8.6 multiply.70
  547.1 13.8 %weight_term.7.refs_0_ = bf16[2048,2048]{1,0:T(8,128)(2,1)} custom-call(s32[1]{0:T(128)} %constant.1029.clone.1.chosen_ref, bf16[1024,2048]{1,0:T(8,128)(2,1)S(1)} %copy-done.76, bf16[1024,2048]{1,0:T(8,128)(2,1)} %stack_rows.11.refs_0_.right_ref), custom_call_target="tpu_custom_call" | custom-call | flops 8589934592 | bytes 16777216 | tf_op jit(solution)/shard_map/weight_term/pallas_call | solution.py:462
  560.8 14.0 %weight_term.8.refs_1_ = bf16[2048,2048]{1,0:T(8,128)(2,1)} custom-call(s32[1]{0:T(128)} %constant.1029.clone.1.chosen_ref, bf16[1024,2048]{1,0:T(8,128)(2,1)S(1)} %copy-done.20, bf16[1024,2048]{1,0:T(8,128)(2,1)} %copy-done.77), custom_call_target="tpu_custom_call" | custom-call | flops 8589934592 | bytes 16777216 | tf_op jit(solution)/shard_map/weight_term/pallas_call | solution.py:462
  595.3 15.9 %collective-permute-done.68.refs_2_ = bf16[256,2048]{1,0:T(8,128)(2,1)} collective-permute-done((bf16[256,2048]{1,0:T(8,128)(2,1)}, bf16[256,2048]{1,0:T(8,128)(2,1)}, u32[]{:S(2)}, u32[]{:S(2)}) %collective-permute-start.68) | collective-permute-done | bytes 1048608 | tf_op jit(solution)/shard_map/ppermute | solution.py:709
  690.9 13.1 %collective-permute-done.83.refs_2_ = bf16[256,2048]{1,0:T(8,128)(2,1)S(1)} collective-permute-done((bf16[256,2048]{1,0:T(8,128)(2,1)}, bf16[256,2048]{1,0:T(8,128)(2,1)S(1)}, u32[]{:S(2)}, u32[]{:S(2)}) %collective-permute-start.83) | collective-permute-done | bytes 1048608 | tf_op jit(solution)/shard_map/ppermute | solution.py:709
  780.5 12.0 %weight_term.12.refs_0_.refs_2_ = bf16[2048,1536]{1,0:T(8,128)(2,1)} custom-call(s32[1]{0:T(128)} %constant.1029.clone.1.chosen_ref, bf16[1024,2048]{1,0:T(8,128)(2,1)} %stack_rows.7.refs_0_.left_ref, bf16[1024,1536]{1,0:T(8,128)(2,1)S(1)} %copy-done.29), custom_call_target="tpu_custom_call" | custom-call | flops 6442450944 | bytes 13631488 | tf_op jit(solution)/shard_map/weight_term/pallas_call | solution.py:462
  811.8 32.7 %collective-permute-done.105.refs_6_ = bf16[128,2048]{1,0:T(8,128)(2,1)S(1)} collective-permute-done((bf16[128,2048]{1,0:T(8,128)(2,1)S(1)}, bf16[128,2048]{1,0:T(8,128)(2,1)S(1)}, u32[]{:S(2)}, u32[]{:S(2)}) %collective-permute-start.105) | collective-permute-done | bytes 524320 | tf_op jit(solution)/shard_map/ppermute | solution.py:709
  880.3 8.3 multiply_rest.12
  889.2 10.4 collective-permute-done.113.refs_6_
  909.6 13.2 %collective-permute-done.110 = bf16[256,2048]{1,0:T(8,128)(2,1)S(1)} collective-permute-done((bf16[256,2048]{1,0:T(8,128)(2,1)S(1)}, bf16[256,2048]{1,0:T(8,128)(2,1)S(1)}, u32[]{:S(2)}, u32[]{:S(2)}) %collective-permute-start.110) | collective-permute-done | bytes 1048608 | tf_op jit(solution)/shard_map/ppermute | solution.py:330
  952.2 9.5 collective-permute-done.119.refs_4_
  988.1 10.1 collective-permute-done.126
  1042.6 15.1 %all-gather.9.cloned.1.call-done.found_ref = bf16[1024,2048]{1,0:T(8,128)(2,1)} async-done(((bf16[256,2048]{1,0:T(8,128)(2,1)}), bf16[1024,2048]{1,0:T(8,128)(2,1)}) %all-gather.9.cloned.1.call-update) | async-done | bytes 4194320 | tf_op jit(solution)/shard_map/all_gather | solution.py:1173
  (672 shorter events, 588.2 us)
Async XLA Ops:
  7.2 55.8 %collective-permute-start.5 = (s32[1]{0:T(128)}, s32[1]{0:T(128)}, u32[]{:S(2)}, u32[]{:S(2)}) collective-permute-start(s32[1]{0:T(128)} %param.17), channel_id=1, source_target_pairs={{0,16},{8,24},{16,0},{24,8},{1,17},{9,25},{17,1},{25,9},{2,18},{10... | collective-permute-start | bytes 20 | tf_op jit(solution)/shard_map/ppermute | solution.py:330
  10.2 52.9 %collective-permute-start.6 = (s32[1]{0:T(128)}, s32[1]{0:T(128)}, u32[]{:S(2)}, u32[]{:S(2)}) collective-permute-start(s32[1]{0:T(128)} %param.17), channel_id=1, source_target_pairs={{0,8},{8,0},{16,24},{24,16},{1,9},{9,1},{17,25},{25,17},{2,10},{10... | collective-permute-start | bytes 20 | tf_op jit(solution)/shard_map/ppermute | solution.py:330
  19.3 52.7 %collective-permute-start.12 = (bf16[256,2048]{1,0:T(8,128)(2,1)}, bf16[256,2048]{1,0:T(8,128)(2,1)S(1)}, u32[]{:S(2)}, u32[]{:S(2)}) collective-permute-start(bf16[256,2048]{1,0:T(8,128)(2,1)} %pick_blocks.5.refs_0_), channel_id=1, source_target_pairs={{0,1},{2,0},{4,2},{6,4},{7,6},{5,7},{3,5},{1,3},{8,9},{10,8},{12,1... | collective-permute-start | bytes 3145736 | tf_op jit(solution)/shard_map/ppermute | solution.py:598
  19.9 52.2 %collective-permute-start.11 = (bf16[256,2048]{1,0:T(8,128)(2,1)S(1)}, bf16[256,2048]{1,0:T(8,128)(2,1)}, u32[]{:S(2)}, u32[]{:S(2)}) collective-permute-start(bf16[256,2048]{1,0:T(8,128)(2,1)S(1)} %copy-done.23), channel_id=1, source_target_pairs={{0,2},{2,4},{4,6},{6,7},{7,5},{5,3},{3,1},{1,0},{8,10},{10,12},{12... | collective-permute-start | bytes 3145736 | tf_op jit(solution)/shard_map/ppermute | solution.py:598
  60.2 922.2 %all-gather.5.cloned.1.call-start = ((), (), s32[]{:S(2)}) async-start(), calls=%async_computation.1 | async-start | bytes 5242880 | tf_op jit(solution)/shard_map/all_gather | solution.py:1115
  274.5 30.3 %collective-permute-start.46 = (bf16[256,2048]{1,0:T(8,128)(2,1)S(1)}, bf16[256,2048]{1,0:T(8,128)(2,1)S(1)}, u32[]{:S(2)}, u32[]{:S(2)}) collective-permute-start(bf16[256,2048]{1,0:T(8,128)(2,1)S(1)} %copy-done.21), channel_id=1, source_target_pairs={{0,2},{2,4},{4,6},{6,7},{7,5},{5,3},{3,1},{1,0},{8,10},{10,12},{12... | collective-permute-start | bytes 3145736 | tf_op jit(solution)/shard_map/ppermute | solution.py:598
  275.2 29.8 %collective-permute-start.47 = (bf16[256,2048]{1,0:T(8,128)(2,1)S(1)}, bf16[256,2048]{1,0:T(8,128)(2,1)S(1)}, u32[]{:S(2)}, u32[]{:S(2)}) collective-permute-start(bf16[256,2048]{1,0:T(8,128)(2,1)S(1)} %dynamic-slice_bitcast_fusion.refs_0_), channel_id=1, source_target_pairs={{0,1},{2,0},{4,2},{6,4},{7,6},{5,7},{3,5},{1,3},{8,9},{10,8},{12,1... | collective-permute-start | bytes 3145736 | tf_op jit(solution)/shard_map/ppermute | solution.py:598
  303.0 34.4 %collective-permute-start.39 = (bf16[512,512]{1,0:T(8,128)(2,1)S(1)}, bf16[512,512]{1,0:T(8,128)(2,1)S(1)}, u32[]{:S(2)}, u32[]{:S(2)}) collective-permute-start(bf16[512,512]{1,0:T(8,128)(2,1)S(1)} %get-tuple-element.491), channel_id=1, source_target_pairs={{0,24},{8,16},{16,8},{24,0},{1,25},{9,17},{17,9},{25,1},{2,26},{10... | collective-permute-start | bytes 1572872 | tf_op jit(solution)/shard_map/ppermute | solution.py:330
  303.7 44.2 %collective-permute-start.38 = (bf16[512,512]{1,0:T(8,128)(2,1)S(1)}, bf16[512,512]{1,0:T(8,128)(2,1)S(1)}, u32[]{:S(2)}, u32[]{:S(2)}) collective-permute-start(bf16[512,512]{1,0:T(8,128)(2,1)S(1)} %get-tuple-element.492), channel_id=1, source_target_pairs={{0,16},{8,24},{16,0},{24,8},{1,17},{9,25},{17,1},{25,9},{2,18},{10... | collective-permute-start | bytes 1572872 | tf_op jit(solution)/shard_map/ppermute | solution.py:330
  304.9 43.1 %collective-permute-start.37 = (bf16[512,512]{1,0:T(8,128)(2,1)S(1)}, bf16[512,512]{1,0:T(8,128)(2,1)S(1)}, u32[]{:S(2)}, u32[]{:S(2)}) collective-permute-start(bf16[512,512]{1,0:T(8,128)(2,1)S(1)} %get-tuple-element.493), channel_id=1, source_target_pairs={{0,8},{8,0},{16,24},{24,16},{1,9},{9,1},{17,25},{25,17},{2,10},{10... | collective-permute-start | bytes 1572872 | tf_op jit(solution)/shard_map/ppermute | solution.py:330
  305.0 43.7 %collective-permute-start.48 = (bf16[256,2048]{1,0:T(8,128)(2,1)S(1)}, bf16[256,2048]{1,0:T(8,128)(2,1)}, u32[]{:S(2)}, u32[]{:S(2)}) collective-permute-start(bf16[256,2048]{1,0:T(8,128)(2,1)S(1)} %collective-permute-done.46.refs_1_), channel_id=1, source_target_pairs={{0,2},{2,4},{4,6},{6,7},{7,5},{5,3},{3,1},{1,0},{8,10},{10,12},{12... | collective-permute-start | bytes 3145736 | tf_op jit(solution)/shard_map/ppermute | solution.py:598
  454.5 47.3 %collective-permute-start.64 = (bf16[1024,512]{1,0:T(8,128)(2,1)S(1)}, bf16[1024,512]{1,0:T(8,128)(2,1)S(1)}, u32[]{:S(2)}, u32[]{:S(2)}) collective-permute-start(bf16[1024,512]{1,0:T(8,128)(2,1)S(1)} %get-tuple-element.309.refs_0_.left_ref), channel_id=1, source_target_pairs={{0,16},{8,24},{16,0},{24,8},{1,17},{9,25},{17,1},{25,9},{2,18},{10... | collective-permute-start | bytes 3145736 | tf_op jit(solution)/shard_map/ppermute | solution.py:330
  532.8 52.4 %collective-permute-start.71 = (bf16[1024,512]{1,0:T(8,128)(2,1)}, bf16[1024,512]{1,0:T(8,128)(2,1)}, u32[]{:S(2)}, u32[]{:S(2)}) collective-permute-start(bf16[1024,512]{1,0:T(8,128)(2,1)} %copy-done.24), channel_id=1, source_target_pairs={{0,16},{8,24},{16,0},{24,8},{1,17},{9,25},{17,1},{25,9},{2,18},{10... | collective-permute-start | bytes 3145736 | tf_op jit(solution)/shard_map/ppermute | solution.py:330
  544.8 36.4 %collective-permute-start.72 = (bf16[256,2048]{1,0:T(8,128)(2,1)S(1)}, bf16[256,2048]{1,0:T(8,128)(2,1)S(1)}, u32[]{:S(2)}, u32[]{:S(2)}) collective-permute-start(bf16[256,2048]{1,0:T(8,128)(2,1)S(1)} %get-tuple-element.320), channel_id=1, source_target_pairs={{0,16},{8,24},{16,0},{24,8},{1,17},{9,25},{17,1},{25,9},{2,18},{10... | collective-permute-start | bytes 3145736 | tf_op jit(solution)/shard_map/ppermute | solution.py:330
  587.8 28.5 %collective-permute-start.76 = (bf16[256,2048]{1,0:T(8,128)(2,1)}, bf16[256,2048]{1,0:T(8,128)(2,1)}, u32[]{:S(2)}, u32[]{:S(2)}) collective-permute-start(bf16[256,2048]{1,0:T(8,128)(2,1)} %get-tuple-element.478.refs_0_), channel_id=1, source_target_pairs={{0,16},{8,24},{16,0},{24,8},{1,17},{9,25},{17,1},{25,9},{2,18},{10... | collective-permute-start | bytes 3145736 | tf_op jit(solution)/shard_map/ppermute | solution.py:330
  687.0 29.3 %collective-permute-start.88 = (bf16[256,2048]{1,0:T(8,128)(2,1)}, bf16[256,2048]{1,0:T(8,128)(2,1)}, u32[]{:S(2)}, u32[]{:S(2)}) collective-permute-start(bf16[256,2048]{1,0:T(8,128)(2,1)} %fusion.20.refs_0_), channel_id=1, source_target_pairs={{0,16},{8,24},{16,0},{24,8},{1,17},{9,25},{17,1},{25,9},{2,18},{10... | collective-permute-start | bytes 3145736 | tf_op jit(solution)/shard_map/ppermute | solution.py:330
  716.9 30.5 %collective-permute-start.86 = (bf16[256,2048]{1,0:T(8,128)(2,1)S(1)}, bf16[256,2048]{1,0:T(8,128)(2,1)S(1)}, u32[]{:S(2)}, u32[]{:S(2)}) collective-permute-start(bf16[256,2048]{1,0:T(8,128)(2,1)S(1)} %get-tuple-element.360), channel_id=1, source_target_pairs={{0,2},{2,4},{4,6},{6,7},{7,5},{5,3},{3,1},{1,0},{8,10},{10,12},{12... | collective-permute-start | bytes 3145736 | tf_op jit(solution)/shard_map/ppermute | solution.py:709
  718.2 31.0 %collective-permute-start.87 = (bf16[256,2048]{1,0:T(8,128)(2,1)}, bf16[256,2048]{1,0:T(8,128)(2,1)}, u32[]{:S(2)}, u32[]{:S(2)}) collective-permute-start(bf16[256,2048]{1,0:T(8,128)(2,1)} %get-tuple-element.361), channel_id=1, source_target_pairs={{0,1},{2,0},{4,2},{6,4},{7,6},{5,7},{3,5},{1,3},{8,9},{10,8},{12,1... | collective-permute-start | bytes 3145736 | tf_op jit(solution)/shard_map/ppermute | solution.py:709
  754.4 44.4 %collective-permute-start.93 = (bf16[256,2048]{1,0:T(8,128)(2,1)}, bf16[256,2048]{1,0:T(8,128)(2,1)}, u32[]{:S(2)}, u32[]{:S(2)}) collective-permute-start(bf16[256,2048]{1,0:T(8,128)(2,1)} %get-tuple-element.373), channel_id=1, source_target_pairs={{0,2},{2,4},{4,6},{6,7},{7,5},{5,3},{3,1},{1,0},{8,10},{10,12},{12... | collective-permute-start | bytes 3145736 | tf_op jit(solution)/shard_map/ppermute | solution.py:709
  761.2 38.7 %collective-permute-start.94 = (bf16[256,2048]{1,0:T(8,128)(2,1)}, bf16[256,2048]{1,0:T(8,128)(2,1)}, u32[]{:S(2)}, u32[]{:S(2)}) collective-permute-start(bf16[256,2048]{1,0:T(8,128)(2,1)} %get-tuple-element.374), channel_id=1, source_target_pairs={{0,1},{2,0},{4,2},{6,4},{7,6},{5,7},{3,5},{1,3},{8,9},{10,8},{12,1... | collective-permute-start | bytes 3145736 | tf_op jit(solution)/shard_map/ppermute | solution.py:709
  774.6 33.8 %collective-permute-start.107 = (bf16[256,2048]{1,0:T(8,128)(2,1)}, bf16[256,2048]{1,0:T(8,128)(2,1)}, u32[]{:S(2)}, u32[]{:S(2)}) collective-permute-start(bf16[256,2048]{1,0:T(8,128)(2,1)} %get-tuple-element.381), channel_id=1, source_target_pairs={{0,16},{8,24},{16,0},{24,8},{1,17},{9,25},{17,1},{25,9},{2,18},{10... | collective-permute-start | bytes 3145736 | tf_op jit(solution)/shard_map/ppermute | solution.py:330
  798.8 51.5 %collective-permute-start.101 = (bf16[128,2048]{1,0:T(8,128)(2,1)S(1)}, bf16[128,2048]{1,0:T(8,128)(2,1)S(1)}, u32[]{:S(2)}, u32[]{:S(2)}) collective-permute-start(bf16[128,2048]{1,0:T(8,128)(2,1)S(1)} %get-tuple-element.385), channel_id=1, source_target_pairs={{0,2},{2,4},{4,6},{6,7},{7,5},{5,3},{3,1},{1,0},{8,10},{10,12},{12... | collective-permute-start | bytes 1572872 | tf_op jit(solution)/shard_map/ppermute | solution.py:709
  803.2 62.6 %collective-permute-start.99 = (bf16[256,2048]{1,0:T(8,128)(2,1)S(1)}, bf16[256,2048]{1,0:T(8,128)(2,1)S(1)}, u32[]{:S(2)}, u32[]{:S(2)}) collective-permute-start(bf16[256,2048]{1,0:T(8,128)(2,1)S(1)} %get-tuple-element.389), channel_id=1, source_target_pairs={{0,2},{2,4},{4,6},{6,7},{7,5},{5,3},{3,1},{1,0},{8,10},{10,12},{12... | collective-permute-start | bytes 3145736 | tf_op jit(solution)/shard_map/ppermute | solution.py:709
  804.3 61.4 %collective-permute-start.100 = (bf16[256,2048]{1,0:T(8,128)(2,1)S(1)}, bf16[256,2048]{1,0:T(8,128)(2,1)S(1)}, u32[]{:S(2)}, u32[]{:S(2)}) collective-permute-start(bf16[256,2048]{1,0:T(8,128)(2,1)S(1)} %get-tuple-element.390), channel_id=1, source_target_pairs={{0,1},{2,0},{4,2},{6,4},{7,6},{5,7},{3,5},{1,3},{8,9},{10,8},{12,1... | collective-permute-start | bytes 3145736 | tf_op jit(solution)/shard_map/ppermute | solution.py:709
  807.2 37.3 %collective-permute-start.105 = (bf16[128,2048]{1,0:T(8,128)(2,1)S(1)}, bf16[128,2048]{1,0:T(8,128)(2,1)S(1)}, u32[]{:S(2)}, u32[]{:S(2)}) collective-permute-start(bf16[128,2048]{1,0:T(8,128)(2,1)S(1)} %get-tuple-element.393), channel_id=1, source_target_pairs={{0,2},{2,4},{4,6},{6,7},{7,5},{5,3},{3,1},{1,0},{8,10},{10,12},{12... | collective-permute-start | bytes 1572872 | tf_op jit(solution)/shard_map/ppermute | solution.py:709
  808.4 40.0 %collective-permute-start.106 = (bf16[128,2048]{1,0:T(8,128)(2,1)S(1)}, bf16[128,2048]{1,0:T(8,128)(2,1)S(1)}, u32[]{:S(2)}, u32[]{:S(2)}) collective-permute-start(bf16[128,2048]{1,0:T(8,128)(2,1)S(1)} %get-tuple-element.394), channel_id=1, source_target_pairs={{0,1},{2,0},{4,2},{6,4},{7,6},{5,7},{3,5},{1,3},{8,9},{10,8},{12,1... | collective-permute-start | bytes 1572872 | tf_op jit(solution)/shard_map/ppermute | solution.py:709
  870.4 143.6 %all-gather.7.cloned.1.call-start = ((), (), s32[]{:S(2)}) async-start(), calls=%async_computation.2 | async-start | bytes 5242880 | tf_op jit(solution)/shard_map/all_gather | solution.py:1115
  871.2 164.0 %all-gather.11.cloned.1.call-start = ((), (), s32[]{:S(2)}) async-start(), calls=%async_computation.4 | async-start | bytes 5242880 | tf_op jit(solution)/shard_map/all_gather | solution.py:1146
  874.5 30.0 %collective-permute-start.111 = (bf16[128,2048]{1,0:T(8,128)(2,1)S(1)}, bf16[128,2048]{1,0:T(8,128)(2,1)S(1)}, u32[]{:S(2)}, u32[]{:S(2)}) collective-permute-start(bf16[128,2048]{1,0:T(8,128)(2,1)S(1)} %copy-done.67), channel_id=1, source_target_pairs={{0,2},{2,4},{4,6},{6,7},{7,5},{5,3},{3,1},{1,0},{8,10},{10,12},{12... | collective-permute-start | bytes 1572872 | tf_op jit(solution)/shard_map/ppermute | solution.py:709
  874.6 29.9 %collective-permute-start.112 = (bf16[128,2048]{1,0:T(8,128)(2,1)S(1)}, bf16[128,2048]{1,0:T(8,128)(2,1)S(1)}, u32[]{:S(2)}, u32[]{:S(2)}) collective-permute-start(bf16[128,2048]{1,0:T(8,128)(2,1)S(1)} %copy-done.65), channel_id=1, source_target_pairs={{0,1},{2,0},{4,2},{6,4},{7,6},{5,7},{3,5},{1,3},{8,9},{10,8},{12,1... | collective-permute-start | bytes 1572872 | tf_op jit(solution)/shard_map/ppermute | solution.py:709
  888.6 34.2 %collective-permute-start.110 = (bf16[256,2048]{1,0:T(8,128)(2,1)S(1)}, bf16[256,2048]{1,0:T(8,128)(2,1)S(1)}, u32[]{:S(2)}, u32[]{:S(2)}) collective-permute-start(bf16[256,2048]{1,0:T(8,128)(2,1)S(1)} %get-tuple-element.413), channel_id=1, source_target_pairs={{0,16},{8,24},{16,0},{24,8},{1,17},{9,25},{17,1},{25,9},{2,18},{10... | collective-permute-start | bytes 3145736 | tf_op jit(solution)/shard_map/ppermute | solution.py:330
  949.2 108.6 %all-gather.9.cloned.1.call-start = ((), (), s32[]{:S(2)}) async-start(), calls=%async_computation.3 | async-start | bytes 5242880 | tf_op jit(solution)/shard_map/all_gather | solution.py:1173
  (232 other events, 3013.6 us)
Sparse Core Ops, SparseCore 0:
  870.5 41.0 all-gather.4
  913.7 37.5 all-gather.6
  953.4 46.4 all-gather.10
  1024.3 33.4 all-gather.8

commit v4 on v3

--- a/solution.py
+++ b/solution.py
@@ -305,6 +305,35 @@
     )(found)
 
 
+def spread_peers(found, rank, first, count, width):
+    rows = found[0].shape[0]
+
+    def kernel(rank_ref, *refs):
+        for peer in range(PEERS):
+            for mask in range(PEERS):
+
+                @pl.when((rank_ref[0] ^ mask) == peer)
+                def _():
+                    refs[-1][:, peer * width : (peer + 1) * width] = refs[mask][...].astype(
+                        jnp.float32
+                    )
+
+    return pl.pallas_call(
+        kernel,
+        grid_spec=pltpu.PrefetchScalarGridSpec(
+            num_scalar_prefetch=1,
+            grid=(count,),
+            in_specs=[pl.BlockSpec((rows, width), lambda block, rank_ref: (0, first + block))]
+            * PEERS,
+            out_specs=pl.BlockSpec((rows, PEERS * width), lambda block, rank_ref: (0, block)),
+        ),
+        out_shape=jax.ShapeDtypeStruct((rows, count * PEERS * width), jnp.float32),
+        cost_estimate=cost(0, 6 * rows * count * PEERS * width),
+        compiler_params=pltpu.CompilerParams(vmem_limit_bytes=VMEM_LIMIT),
+        name="spread_peers",
+    )(rank.reshape(1), *found)
+
+
 def spread_rows(found, width):
     rows = found.shape[0] // PEERS
 
@@ -335,18 +364,32 @@
     count = len(parts)
 
     def kernel(*refs):
-        for i in range(count):
-
-            @pl.when(pl.program_id(0) == i)
-            def _():
-                refs[-1][...] = refs[i][...]
+        ins, out, held, arrived, left = refs[:count], refs[count], refs[-3], refs[-2], refs[-1]
+        fetches = [
+            pltpu.make_async_copy(ins[i], held.at[i], arrived.at[i]) for i in range(count)
+        ]
+        stores = [
+            pltpu.make_async_copy(held.at[i], out.at[i * rows : (i + 1) * rows, :], left.at[i])
+            for i in range(count)
+        ]
+        for fetch in fetches:
+            fetch.start()
+        for fetch, store in zip(fetches, stores):
+            fetch.wait()
+            store.start()
+        for store in stores:
+            store.wait()
 
     return pl.pallas_call(
         kernel,
-        grid=(count,),
-        in_specs=[pl.BlockSpec((rows, columns), lambda step: (0, 0))] * count,
-        out_specs=pl.BlockSpec((rows, columns), lambda step: (step, 0)),
+        in_specs=[pl.BlockSpec(memory_space=pl.ANY)] * count,
+        out_specs=pl.BlockSpec(memory_space=pl.ANY),
         out_shape=jax.ShapeDtypeStruct((count * rows, columns), parts[0].dtype),
+        scratch_shapes=[
+            pltpu.VMEM((count, rows, columns), parts[0].dtype),
+            pltpu.SemaphoreType.DMA((count,)),
+            pltpu.SemaphoreType.DMA((count,)),
+        ],
         cost_estimate=cost(0, 4 * count * rows * columns),
         compiler_params=pltpu.CompilerParams(vmem_limit_bytes=VMEM_LIMIT),
         name="stack_rows",
@@ -449,15 +492,17 @@
     return found[0] if len(types) == 1 else found
 
 
-def weight_term(left, right, column_block=None):
+def weight_term(left, right, rank=None, into=None, first=0, total=None):
     depth, rows = left.shape
-    columns = right.shape[1] if column_block is None else right.shape[1] // PEERS
-    height, width = min(1024, rows), min(512, columns)
+    columns = right.shape[1] if rank is None else right.shape[1] // PEERS
+    height = min(1024, rows) if rank is None else rows // PEERS
+    width = min(512, columns)
     shift = columns // width
-    chosen = jnp.zeros((1,), jnp.int32) if column_block is None else column_block.reshape(1)
-
-    def kernel(chosen_ref, left_ref, right_ref, out_ref):
-        out_ref[...] = outer_sum(left_ref[...], right_ref[...]).astype(jnp.bfloat16)
+    chosen = jnp.zeros((1,), jnp.int32) if rank is None else rank.reshape(1)
+    total = columns if total is None else total
+
+    def kernel(chosen_ref, left_ref, right_ref, *refs):
+        refs[-1][...] = outer_sum(left_ref[...], right_ref[...]).astype(jnp.bfloat16)
 
     return pl.pallas_call(
         kernel,
@@ -465,18 +510,27 @@
             num_scalar_prefetch=1,
             grid=(columns // width, rows // height),
             in_specs=[
-                pl.BlockSpec((depth, height), lambda j, i, chosen_ref: (0, i)),
+                pl.BlockSpec(
+                    (depth, height),
+                    lambda j, i, chosen_ref: (0, i if rank is None else i ^ chosen_ref[0]),
+                ),
                 pl.BlockSpec(
                     (depth, width), lambda j, i, chosen_ref: (0, chosen_ref[0] * shift + j)
                 ),
-            ],
-            out_specs=pl.BlockSpec((height, width), lambda j, i, chosen_ref: (i, j)),
+            ]
+            + [pl.BlockSpec(memory_space=pl.ANY)] * (into is not None),
+            out_specs=pl.BlockSpec(
+                (height, width), lambda j, i, chosen_ref: (i, first // width + j)
+            ),
         ),
-        out_shape=jax.ShapeDtypeStruct((rows, columns), jnp.bfloat16),
-        cost_estimate=cost(2 * rows * depth * columns, 2 * (rows * depth + depth * columns + rows * columns)),
+        out_shape=jax.ShapeDtypeStruct((rows, total), jnp.bfloat16),
+        input_output_aliases={} if into is None else {3: 0},
+        cost_estimate=cost(
+            2 * rows * depth * columns, 2 * (rows * depth + depth * columns + rows * columns)
+        ),
         compiler_params=pltpu.CompilerParams(vmem_limit_bytes=VMEM_LIMIT),
         name="weight_term",
-    )(chosen, left, right)
+    )(chosen, left, right, *([] if into is None else [into]))
 
 
 def multiply_rest(left, right, turned, got):
@@ -539,6 +593,10 @@
         self.token = self.token + tuple(jax.tree.leaves(values))
 
 
+class State:
+    pass
+
+
 class GroupSum:
     def __init__(self, order, left, right, turned, half=None):
         self.order, self.left, self.right, self.turned = order, left, right, turned
@@ -641,69 +699,59 @@
     )(starts, *pieces)
 
 
-def ring_add(entries, spots, rows, got):
-    flat = [value for values in entries for value in values]
-    lengths = [sum(value.shape[1] for value in values) for values in entries]
-    count = len(flat)
+def ring_add(values, spots, rows, got):
+    count = len(values)
+    columns = values[0].shape[1]
+    width = min(1024, columns)
 
     def kernel(spots_ref, *refs):
-        outs = refs[-len(entries) :]
-        i = 0
-        for entry, values in enumerate(entries):
-            first = 0
-            for value in values:
-                place = slice(first, first + value.shape[1])
-                block = refs[i][...]
-                if got is not None:
-                    here = refs[count + entry][:, place].astype(jnp.float32)
-                    block = (here + block.astype(jnp.float32)).astype(jnp.bfloat16)
-                outs[entry][:, place] = block
-                first += value.shape[1]
-                i += 1
+        for i in range(count):
+            block = refs[i][...]
+            refs[-count + i][...] = block if got is None else refs[count + i][...] + block
 
     def spec(i):
-        return pl.BlockSpec(
-            (rows, flat[i].shape[1]), lambda step, spots_ref: (spots_ref[i], 0)
-        )
-
-    plain = [pl.BlockSpec((rows, length), lambda step, spots_ref: (0, 0)) for length in lengths]
+        return pl.BlockSpec((rows, width), lambda step, spots_ref: (spots_ref[i], step))
+
+    plain = [pl.BlockSpec((rows, width), lambda step, spots_ref: (0, step))] * count
     arrived = [] if got is None else list(got)
     return pl.pallas_call(
         kernel,
         grid_spec=pltpu.PrefetchScalarGridSpec(
             num_scalar_prefetch=1,
-            grid=(1,),
+            grid=(columns // width,),
             in_specs=[spec(i) for i in range(count)] + plain[: len(arrived)],
             out_specs=plain,
         ),
-        out_shape=[jax.ShapeDtypeStruct((rows, length), jnp.bfloat16) for length in lengths],
-        cost_estimate=cost(rows * sum(lengths), 6 * rows * sum(lengths)),
+        out_shape=[jax.ShapeDtypeStruct((rows, columns), jnp.bfloat16)] * count,
+        cost_estimate=cost(rows * columns * count, 6 * rows * columns * count),
         compiler_params=pltpu.CompilerParams(vmem_limit_bytes=VMEM_LIMIT),
         name="ring_add",
-    )(spots, *flat, *arrived)
+    )(spots, *values, *arrived)
 
 
 class Scatter:
-    def __init__(self, order, entries, size, place, rows):
+    def __init__(self, order, entries, size, place, rows, shard_rows):
         self.order, self.entries = order, entries
         self.size, self.place, self.rows, self.step = size, place, rows, 0
-        self.values = [[value for value, _ in values] for values, _, _ in entries]
+        self.sevenths, self.blocks = 0, shard_rows // rows
+        self.values = [value for value, _, _ in entries]
         self.sums = order.run(
-            lambda first: ring_add(
-                [[first] + self.values[0][1:]] + self.values[1:], self.spots(), self.rows, None
-            ),
-            self.values[0][0],
+            lambda first: ring_add([first] + self.values[1:], self.spots(), self.rows, None),
+            self.values[0],
         )
 
     def spots(self):
-        found = []
-        for values, direction, block in self.entries:
-            shard = ring_member(self.place - direction * (self.step + 1), self.size)
-            found += [rows_of(shard) // self.rows + block for _, rows_of in values]
-        return jnp.stack(found).astype(jnp.int32)
-
-    def reach(self, seventh):
-        while self.step < seventh * (self.size - 1) // 7:
+        return jnp.stack(
+            [
+                ring_member(self.place - direction * (self.step + 1), self.size) * self.blocks
+                + block
+                for _, direction, block in self.entries
+            ]
+        ).astype(jnp.int32)
+
+    def reach(self):
+        self.sevenths += 1
+        while self.step < self.sevenths * (self.size - 1) // 7:
             self.step += 1
             arrived = [
                 lax.ppermute(value, "fsdp", ring_pairs(self.size, direction))
@@ -713,20 +761,30 @@
             self.sums = self.order.run(
                 lambda got: ring_add(self.values, spots, self.rows, got), arrived
             )
-
-
-def exchange(value, size, between):
-    value = value[None]
-    member = lax.axis_index("fsdp")
-    mask = 1
-    while mask < size:
-        other = between(lax.ppermute(value, "fsdp", [(i, i ^ mask) for i in range(size)]))
-        low = (member & mask) == 0
-        value = jnp.concatenate(
-            [jnp.where(low, value, other), jnp.where(low, other, value)], axis=0
-        )
-        mask *= 2
-    return value
+        return self.sevenths == 7
+
+
+class Exchange:
+    def __init__(self, order, value, size):
+        self.order, self.value, self.size, self.mask = order, value[None], size, 1
+        self.send()
+
+    def send(self):
+        pairs = [(i, i ^ self.mask) for i in range(self.size)]
+        self.got = lax.ppermute(self.value, "fsdp", pairs)
+
+    def hop(self):
+        low = (lax.axis_index("fsdp") & self.mask) == 0
+
+        def join(got):
+            return jnp.concatenate(
+                [jnp.where(low, self.value, got), jnp.where(low, got, self.value)], axis=0
+            )
+
+        self.value = self.order.run(join, self.got)
+        self.mask *= 2
+        if self.mask < self.size:
+            self.send()
 
 
 class Everyone:
@@ -734,19 +792,35 @@
         self.order, self.value = order, value
         self.hops = [("fsdp", size // 2 >> i, size) for i in range(size.bit_length() - 1)]
         self.hops += [("rep", 2, PEERS), ("rep", 1, PEERS)]
+        self.left = len(self.hops)
         self.send()
 
     def send(self):
         axis, mask, size = self.hops.pop(0)
         self.got = lax.ppermute(self.value, axis, [(i, i ^ mask) for i in range(size)])
 
-    def hop(self, count=1):
-        for _ in range(count):
+    def hop(self):
+        if self.left:
             self.value = self.order.run(
                 lambda got: jnp.concatenate([self.value, got], axis=0), self.got
             )
+            self.left -= 1
             if self.hops:
                 self.send()
+
+
+PLAN = (
+    "p1", "p2", "a0", "r", "p3", "p4", "A", "e", "A", "e", "A", "e", "terms", "A", "start", "xa",
+    "A", "ja", "st", "xt", "A", "jt", "sg", "A", "ab", "lay1", "lay2", "qkv", "B", "kv", "B",
+    "self", "wo", "near1", "rest1", "wm", "B", "x1", "fin1", "y2", "B", "join2", "sm", "cq",
+    "cross", "near2", "B", "rest2", "x2", "B", "fin2", "y3", "B", "join3", "sc", "jm", "jg",
+    "lay3", "up", "lay4", "pre", "near3", "rest3", "dterm", "uterm", "F0", "x3", "fin3", "jc",
+    "near6", "y4", "F", "join4", "mm4", "cback", "near4", "F", "rest4", "qterm", "kterm", "mterm",
+    "C0", "x4", "F", "fin4", "rest6", "y5", "F", "C", "join5", "mm5", "sback", "near5", "F", "C",
+    "rest5", "qkvterm", "oterm", "S0", "x5", "F", "C", "fin5", "C", "S", "F", "C", "S", "x6",
+    "fin6", "C", "S", "h", "near7", "C", "S", "rest7", "h", "S", "h", "dout", "fin7", "S", "h",
+    "uout", "S", "h", "mod", "cout", "sout",
+)
 
 
 def body(
@@ -810,50 +884,6 @@
     def own_rows(value):
         return value.reshape(images, length, width)
 
-    first_pick = order.run(lambda w: pick_blocks([w, out_weight], [3, 1], rank), qkv_weight)
-    second_pick = order.run(
-        lambda w: pick_blocks([w, keyval_weight, merge_weight], [1, 2, 1], rank), query_weight
-    )
-    first, second = Gather(first_pick, group, 1), Gather(second_pick, group, -1)
-    order.tick(first, second)
-    picks = [
-        lambda w: pick_blocks([w], [group], rank) if aligned else own_part(w, group),
-        lambda w: lax.dynamic_index_in_dim(
-            w.reshape(PEERS, -1, width), rank, 0, keepdims=False
-        ),
-    ]
-    sources = [up_weight, down_weight]
-    picked = []
-
-    def pick_between(value):
-        if len(picked) < len(picks):
-            i = len(picked)
-            picked.append(order.run(picks[i], sources[i]))
-        return after(value, order.token)
-
-    small = exchange(
-        jnp.concatenate([timesteps.astype(jnp.float32), cross_gain.astype(jnp.float32)]),
-        group,
-        pick_between,
-    )
-    while len(picked) < len(picks):
-        pick_between(small)
-    third_pick, fourth_pick = picked
-    small = order.hold(small)
-    order.tick(first, second)
-    group_steps = small[:, :images].reshape(-1)
-    gain_full = small[:, images:].reshape(-1)
-    sequence = [0]
-    while len(sequence) < group:
-        sequence += [index + group // (2 * len(sequence)) for index in sequence]
-    all_steps = small[:, :images][member ^ jnp.array(sequence, dtype=jnp.int32)].reshape(-1)
-    all_steps = jnp.concatenate([all_steps, swap(all_steps, 2)])
-    all_steps = jnp.concatenate([all_steps, swap(all_steps, 1)])
-    length_far = swap(text_lengths, 2)
-    length_all = jnp.concatenate(
-        [text_lengths, length_far, swap(text_lengths, 1), swap(length_far, 1)]
-    )
-
     half_width = width // 2
     column = member * shard_rows + jnp.arange(shard_rows, dtype=jnp.int32)
     place = jnp.where(column < half_width, column, column - half_width)
@@ -865,22 +895,8 @@
             jnp.bfloat16
         )
 
-    terms = order.run(lambda steps: matmul(conditions(steps), mod_weight), group_steps)
-    found = lax.all_to_all(
-        terms.reshape(group, images, -1), "fsdp", split_axis=0, concat_axis=0, tiled=True
-    )
-    order.wait(all_steps, length_all)
     residual = image_tokens.astype(jnp.float32)
     grad_block = cotangent.astype(jnp.float32)
-
-    def start(found):
-        pieces = jnp.sum(found, axis=0).reshape(images, 6, 1, width)
-        act = flatten(normed(residual) * (1.0 + pieces[:, 1]) + pieces[:, 0])
-        return pieces, act.astype(jnp.bfloat16)
-
-    pieces, act_one = order.run(start, found)
-    shift_self, scale_self, gate_self = (pieces[:, 0], pieces[:, 1], pieces[:, 2])
-    shift_mlp, scale_mlp, gate_mlp = (pieces[:, 3], pieces[:, 4], pieces[:, 5])
     norm_one = normed(residual)
 
     def send_rows(value):
@@ -901,308 +917,530 @@
             lambda last: stack_columns([parts[0], parts[1], far, last]), swap(far, 1)
         )
 
-    act_one = send_rows(act_one)
-    text_all = send_rows(after(flatten(text_tokens), act_one[1]))
-    order.tick(first, second)
-    grad_three = order.run(lambda gate: flatten(gate * grad_block).astype(jnp.bfloat16), gate_mlp)
-    order.tick(first, second)
-    act_one = join_rows(act_one)
-    order.tick(first, second)
-    text_all = join_rows(text_all)
-    order.tick(first, second)
-    order.tick(first, second)
-    third, fourth = Gather(third_pick, group, 1), Gather(fourth_pick, group, -1)
-    order.tick(first, second, third, fourth)
-
-    qkv_part, out_part = order.run(
-        lambda last: lay_out(
-            first.pieces[:-1] + [last], first.starts(spot, shard_rows), [3 * part, part]
-        ),
-        first.pieces[-1],
-    )
-    out_part = columns_to_rows(out_part)
-    query_part, keyval_part, merge_part = order.run(
-        lambda last: lay_out(
-            second.pieces[:-1] + [last], second.starts(spot, shard_rows), [part, 2 * part, part]
-        ),
-        second.pieces[-1],
-    )
-    merge_part = columns_to_rows(merge_part)
-    qkv_act = order.run(lambda a: multiply(a, qkv_part, False), act_one)
-    order.tick(third, fourth)
-    keyval = order.run(lambda a: multiply(a, keyval_part, False), text_all)
-    mixed_flat, logsum_self = order.run(
-        lambda a: attend_self(a, all_images, heads, score_scale), qkv_act
-    )
-    order.wait(out_part)
-    branch_sum = GroupSum(order, mixed_flat, out_part, False)
-    branch_sum.near()
-    order.tick(third, fourth)
-    branch_sum.rest()
-    order.wait(merge_part)
-    order.tick(third, fourth)
-
-    def finish_self(crossed):
-        branch_one = own_rows(branch_sum.mine + crossed.astype(jnp.float32))
-        hidden_one = residual + gate_self * branch_one
-        return (
-            branch_one,
-            hidden_one,
-            flatten(normed(hidden_one) * gain_full).astype(jnp.bfloat16),
-        )
-
-    branch_one, hidden_one, act_two = order.run(finish_self, branch_sum.crossed)
-    norm_two = normed(hidden_one)
-    act_two = send_rows(act_two)
-    grad_three = send_rows(after(grad_three, act_two[1]))
-    order.tick(third, fourth)
-    act_two = join_rows(act_two)
-    cross_queries = order.run(lambda a: multiply(a, query_part, False), act_two)
-    cross_flat, logsum_cross = order.run(
-        lambda a: attend_cross(a, keyval, length_all, all_images, heads, score_scale),
-        cross_queries,
-    )
-    branch_sum = GroupSum(order, cross_flat, merge_part, False)
-    branch_sum.near()
-    order.tick(third, fourth)
-    branch_sum.rest()
-    order.tick(third, fourth)
-
-    def finish_cross(crossed):
-        hidden_two = hidden_one + own_rows(branch_sum.mine + crossed.astype(jnp.float32))
-        act = flatten(normed(hidden_two) * (1.0 + scale_mlp) + shift_mlp)
-        return hidden_two, act.astype(jnp.bfloat16)
-
-    hidden_two, act_three = order.run(finish_cross, branch_sum.crossed)
-    norm_three = normed(hidden_two)
-    act_three = send_rows(act_three)
-    mixed_parts = send_columns(after(mixed_flat, act_three[1]))
-    order.tick(third, fourth)
-    act_three = join_rows(act_three)
-    grad_three = join_rows(grad_three)
-    cross_parts = send_columns(after(cross_flat, mixed_parts[2]))
-
-    (up_part,) = order.run(
-        lambda last: lay_out(
-            third.pieces[:-1] + [last], third.starts(spot, shard_rows), [hidden // PEERS]
-        ),
-        third.pieces[-1],
-    )
-    activated, slope = order.run(
-        lambda a: multiply(a, up_part, False, gate_and_slope, (jnp.bfloat16, jnp.bfloat16)),
-        act_three,
-    )
-    (down_part,) = order.run(
-        lambda last: lay_out(
-            fourth.pieces[:-1] + [last], fourth.starts(spot, shard_rows), [width]
-        ),
-        fourth.pieces[-1],
-    )
-    mixed_all = join_columns(mixed_parts)
-
-    def shard_start(shard):
-        return shard * shard_rows
-
-    def swapped_start(shard):
-        begin = shard * shard_rows
-        return ((begin // part) ^ rank) * part + begin % part
-
-    def ring(values):
-        return Scatter(order, [(values, 1, 0), (values, -1, 1)], group, spot, shard_rows // 2)
-
-    grad_pre = order.run(
-        lambda a: multiply(a, down_part, True, scaled, extra=(slope, 0)), grad_three
-    )
-    branch_sum = GroupSum(order, grad_pre, up_part, True).send()
-    down_term = order.run(lambda a: weight_term(a, grad_three), activated)
-    up_term = order.run(lambda a: weight_term(a, grad_pre), act_three)
-    mlp_ring = Scatter(
-        order,
-        [([(down_term, shard_start)], 1, 0), ([(up_term, shard_start)], -1, 0)],
-        group,
-        spot,
-        shard_rows,
-    )
-
-    def finish_mlp_back(crossed):
-        grad_act = own_rows(branch_sum.mine + crossed.astype(jnp.float32))
-        grad_two = grad_block + normed_back(hidden_two, grad_act * (1.0 + scale_mlp))
-        return (
-            jnp.sum(grad_act, axis=1),
-            jnp.sum(grad_act * norm_three, axis=1),
-            grad_two,
-            flatten(grad_two).astype(jnp.bfloat16),
-        )
-
-    grad_shift_mlp, grad_scale_mlp, grad_two, grad_merge = order.run(
-        finish_mlp_back, branch_sum.crossed
-    )
-    grad_merge = send_rows(grad_merge)
-    cross_all_heads = join_columns(cross_parts)
-    mlp_ring.reach(1)
-    grad_merge = join_rows(grad_merge)
-
-    grad_mixed = order.run(lambda a: multiply(a, merge_part, True), grad_merge)
-    grad_query, grad_keyval = order.run(
-        lambda a: attend_cross_back(
-            cross_queries, keyval, length_all, logsum_cross, a, all_images, heads, score_scale
-        ),
-        grad_mixed,
-    )
-    branch_sum = GroupSum(order, grad_query, query_part, True)
-    branch_sum.near()
-    mlp_ring.reach(2)
-    branch_sum.rest()
-    query_term = order.run(lambda a: weight_term(a, grad_query), act_two)
-    keyval_term = order.run(lambda a: weight_term(a, grad_keyval), text_all)
-    merge_term = order.run(lambda a: weight_term(a, grad_merge, rank), cross_all_heads)
-    cross_ring = ring(
-        [(query_term, shard_start), (keyval_term, shard_start), (merge_term, swapped_start)]
-    )
-    mlp_ring.reach(3)
-
-    def finish_cross_back(crossed):
-        grad_act = own_rows(branch_sum.mine + crossed.astype(jnp.float32))
-        grad_one = grad_two + normed_back(hidden_one, grad_act * gain_full)
-        return (
-            jnp.sum(grad_act * norm_two, axis=1),
-            jnp.sum(grad_one * branch_one, axis=1),
-            grad_one,
-            flatten(gate_self * grad_one).astype(jnp.bfloat16),
-        )
-
-    gain_term, grad_gate_self, grad_one, grad_out = order.run(
-        finish_cross_back, branch_sum.crossed
-    )
-    grad_out = send_rows(grad_out)
-    mlp_ring.reach(4)
-    cross_ring.reach(1)
-    grad_out = join_rows(grad_out)
-
-    grad_mixed = order.run(lambda a: multiply(a, out_part, True), grad_out)
-    grad_qkv = order.run(
-        lambda a: attend_self_back(qkv_act, logsum_self, a, all_images, heads, score_scale),
-        grad_mixed,
-    )
-    branch_sum = GroupSum(order, grad_qkv, qkv_part, True)
-    branch_sum.near()
-    mlp_ring.reach(5)
-    cross_ring.reach(2)
-    branch_sum.rest()
-    qkv_term = order.run(lambda a: weight_term(a, grad_qkv), act_one)
-    out_term = order.run(lambda a: weight_term(a, grad_out, rank), mixed_all)
-    self_ring = ring([(qkv_term, shard_start), (out_term, swapped_start)])
-    mlp_ring.reach(6)
-    cross_ring.reach(3)
-
-    def finish_self_back(crossed):
-        grad_act = own_rows(branch_sum.mine + crossed.astype(jnp.float32))
-        image_grad = grad_one + normed_back(residual, grad_act * (1.0 + scale_self))
-        return (
-            jnp.sum(grad_act, axis=1),
-            jnp.sum(grad_act * norm_one, axis=1),
-            image_grad.astype(jnp.bfloat16),
-        )
-
-    grad_shift_self, grad_scale_self, image_grad = order.run(finish_self_back, branch_sum.crossed)
-
-    cross_ring.reach(4)
-    self_ring.reach(1)
-    mlp_sum = GroupSum(order, activated, down_part, False)
-    mlp_sum.near()
-    mlp_ring.reach(7)
-    down_all, up_all = [
-        lax.all_gather(found, "rep", axis=0, tiled=True) for found in mlp_ring.sums
-    ]
-    mlp_sum.rest()
-    cross_ring.reach(5)
-    self_ring.reach(2)
-
-    def finish_mlp(crossed):
-        branch_three = own_rows(mlp_sum.mine + crossed.astype(jnp.float32))
-        block_out = (hidden_two + gate_mlp * branch_three).astype(jnp.bfloat16)
-        vectors = jnp.concatenate(
-            [
-                grad_shift_self,
-                grad_scale_self,
-                grad_gate_self,
-                grad_shift_mlp,
-                grad_scale_mlp,
-                jnp.sum(grad_block * branch_three, axis=1),
-                gain_term,
-            ],
-            axis=1,
-        )
-        return block_out, vectors.astype(jnp.bfloat16)
-
-    block_out, vectors = order.run(finish_mlp, mlp_sum.crossed)
-    everyone = Everyone(order, vectors, group)
-    cross_ring.reach(6)
-    self_ring.reach(3)
-    everyone.hop()
-    text_sum = GroupSum(order, grad_keyval, keyval_part, True)
-    text_sum.near()
-    cross_ring.reach(7)
-    cross_all = lax.all_gather(jnp.concatenate(cross_ring.sums, axis=0), "rep", axis=0, tiled=True)
-    self_ring.reach(4)
-    text_sum.rest()
-    everyone.hop()
-    self_ring.reach(5)
-    everyone.hop()
-    down_grad = order.run(lambda a: spread_rows(a, width), down_all)
-    text_grad = order.run(
-        lambda crossed: (text_sum.mine + crossed.astype(jnp.float32))
-        .astype(jnp.bfloat16)
-        .reshape(text_tokens.shape),
-        text_sum.crossed,
-    )
-    self_ring.reach(6)
-    everyone.hop(len(everyone.hops))
-    if aligned:
-        up_grad = order.run(
-            lambda a: spread_blocks(a, 0, group, hidden // (group * PEERS)), up_all
-        )
-    else:
-        up_grad = (
-            up_all.reshape(PEERS, shard_rows, group, -1)
-            .transpose(1, 2, 0, 3)
-            .reshape(shard_rows, hidden)
-            .astype(jnp.float32)
-        )
-    self_ring.reach(7)
-    self_all = lax.all_gather(
-        jnp.concatenate(self_ring.sums, axis=0), "rep", axis=0, tiled=True
-    )
-    everyone.hop(1 + len(everyone.hops))
-
-    def finish_modulation(found):
-        return (
-            outer_sum(conditions(all_steps), found[:, : 6 * width]),
-            jnp.sum(
-                lax.dynamic_slice_in_dim(
-                    found, 6 * width + member * shard_rows, shard_rows, 1
-                ).astype(jnp.float32),
-                axis=0,
+    v = State()
+    mine = jnp.concatenate([timesteps, text_lengths]).astype(jnp.float32)
+    mine = [mine, swap(mine, 2), swap(mine, 1)]
+
+    def p1():
+        v.pick1 = order.run(lambda w: pick_blocks([w, out_weight], [3, 1], rank), qkv_weight)
+
+    def p2():
+        v.pick2 = order.run(
+            lambda w: pick_blocks([w, keyval_weight, merge_weight], [1, 2, 1], rank),
+            query_weight,
+        )
+
+    def p3():
+        v.pick3 = order.run(
+            lambda w: pick_blocks([w], [group], rank) if aligned else own_part(w, group),
+            up_weight,
+        )
+
+    def p4():
+        v.pick4 = order.run(
+            lambda w: lax.dynamic_index_in_dim(
+                w.reshape(PEERS, -1, width), rank, 0, keepdims=False
             ),
-        )
-
-    mod_grad, gain_grad = order.run(finish_modulation, everyone.value)
-    query_grad = order.run(lambda a: spread_blocks(a, 0, 1, part), cross_all)
-    keyval_grad = order.run(lambda a: spread_blocks(a, 1, 2, part), cross_all)
-    merge_grad = order.run(lambda a: spread_blocks(a, 3, 1, part), cross_all)
+            down_weight,
+        )
+
+    def a0():
+        v.first, v.second = Gather(v.pick1, group, 1), Gather(v.pick2, group, -1)
+        order.tick(v.first, v.second)
+
+    def ab():
+        v.third, v.fourth = Gather(v.pick3, group, 1), Gather(v.pick4, group, -1)
+        order.tick(v.first, v.second, v.third, v.fourth)
+
+    def r():
+        far = order.hold(mine[1])
+        found = order.run(
+            lambda last: jnp.stack([mine[0], far, mine[2], last]), swap(far, 1)
+        )
+        v.length_all = found[:, images:].reshape(-1).astype(jnp.int32)
+        v.exchange = Exchange(
+            order,
+            jnp.concatenate([found[:, :images].reshape(-1), cross_gain.astype(jnp.float32)]),
+            group,
+        )
+
+    def e():
+        v.exchange.hop()
+
+    def terms():
+        while v.exchange.mask < group:
+            e()
+        small = v.exchange.value
+        v.gain_full = small[:, all_images:].reshape(-1)
+        sequence = [0]
+        while len(sequence) < group:
+            sequence += [index + group // (2 * len(sequence)) for index in sequence]
+        steps = small[:, :all_images][member ^ jnp.array(sequence, dtype=jnp.int32)]
+        v.all_steps = steps.reshape(group, PEERS, images).transpose(1, 0, 2).reshape(-1)
+        found = order.run(
+            lambda steps: matmul(conditions(steps), mod_weight), small[:, :images].reshape(-1)
+        )
+        v.terms = lax.all_to_all(
+            found.reshape(group, images, -1), "fsdp", split_axis=0, concat_axis=0, tiled=True
+        )
+
+    def start():
+        def work(found):
+            pieces = jnp.sum(found, axis=0).reshape(images, 6, 1, width)
+            act = flatten(normed(residual) * (1.0 + pieces[:, 1]) + pieces[:, 0])
+            grad_three = flatten(pieces[:, 5] * grad_block)
+            return pieces, act.astype(jnp.bfloat16), grad_three.astype(jnp.bfloat16)
+
+        pieces, act_one, v.grad_three = order.run(work, v.terms)
+        v.shift_self, v.scale_self, v.gate_self = (pieces[:, 0], pieces[:, 1], pieces[:, 2])
+        v.shift_mlp, v.scale_mlp, v.gate_mlp = (pieces[:, 3], pieces[:, 4], pieces[:, 5])
+        v.act_one = send_rows(act_one)
+
+    def ja():
+        v.act_one = join_rows(v.act_one)
+
+    def st():
+        v.text_all = send_rows(order.hold(flatten(text_tokens)))
+
+    def jt():
+        v.text_all = join_rows(v.text_all)
+
+    def sg():
+        v.grad_three = send_rows(order.hold(v.grad_three))
+
+    def jg():
+        v.grad_three = join_rows(v.grad_three)
+
+    def lay1():
+        v.qkv_part, out_part = order.run(
+            lambda last: lay_out(
+                v.first.pieces[:-1] + [last], v.first.starts(spot, shard_rows), [3 * part, part]
+            ),
+            v.first.pieces[-1],
+        )
+        v.out_part = columns_to_rows(out_part)
+
+    def lay2():
+        v.query_part, v.keyval_part, merge_part = order.run(
+            lambda last: lay_out(
+                v.second.pieces[:-1] + [last],
+                v.second.starts(spot, shard_rows),
+                [part, 2 * part, part],
+            ),
+            v.second.pieces[-1],
+        )
+        v.merge_part = columns_to_rows(merge_part)
+
+    def qkv():
+        v.qkv_act = order.run(lambda a: multiply(a, v.qkv_part, False), v.act_one)
+
+    def kv():
+        v.keyval = order.run(lambda a: multiply(a, v.keyval_part, False), v.text_all)
+
+    def self_attend():
+        v.mixed_flat, v.logsum_self = order.run(
+            lambda a: attend_self(a, all_images, heads, score_scale), v.qkv_act
+        )
+
+    def near1():
+        v.sum1 = GroupSum(order, v.mixed_flat, v.out_part, False)
+        v.sum1.near()
+
+    def fin1():
+        def finish(crossed):
+            branch_one = own_rows(v.sum1.mine + crossed.astype(jnp.float32))
+            hidden_one = residual + v.gate_self * branch_one
+            return (
+                branch_one,
+                hidden_one,
+                flatten(normed(hidden_one) * v.gain_full).astype(jnp.bfloat16),
+            )
+
+        v.branch_one, v.hidden_one, act_two = order.run(finish, v.sum1.crossed)
+        v.norm_two = normed(v.hidden_one)
+        v.act_two = send_rows(act_two)
+
+    def join2():
+        v.act_two = join_rows(v.act_two)
+
+    def cq():
+        v.cross_queries = order.run(lambda a: multiply(a, v.query_part, False), v.act_two)
+
+    def cross():
+        v.cross_flat, v.logsum_cross = order.run(
+            lambda a: attend_cross(a, v.keyval, v.length_all, all_images, heads, score_scale),
+            v.cross_queries,
+        )
+
+    def near2():
+        v.sum2 = GroupSum(order, v.cross_flat, v.merge_part, False)
+        v.sum2.near()
+
+    def fin2():
+        def finish(crossed):
+            hidden_two = v.hidden_one + own_rows(v.sum2.mine + crossed.astype(jnp.float32))
+            act = flatten(normed(hidden_two) * (1.0 + v.scale_mlp) + v.shift_mlp)
+            return hidden_two, act.astype(jnp.bfloat16)
+
+        v.hidden_two, act_three = order.run(finish, v.sum2.crossed)
+        v.norm_three = normed(v.hidden_two)
+        v.act_three = send_rows(act_three)
+
+    def join3():
+        v.act_three = join_rows(v.act_three)
+
+    def sm():
+        v.mixed_parts = send_columns(order.hold(v.mixed_flat))
+
+    def jm():
+        v.mixed_all = join_columns(v.mixed_parts)
+
+    def sc():
+        v.cross_parts = send_columns(order.hold(v.cross_flat))
+
+    def jc():
+        v.cross_all = join_columns(v.cross_parts)
+
+    def lay3():
+        (v.up_part,) = order.run(
+            lambda last: lay_out(
+                v.third.pieces[:-1] + [last], v.third.starts(spot, shard_rows), [hidden // PEERS]
+            ),
+            v.third.pieces[-1],
+        )
+
+    def up():
+        v.activated, v.slope = order.run(
+            lambda a: multiply(a, v.up_part, False, gate_and_slope, (jnp.bfloat16, jnp.bfloat16)),
+            v.act_three,
+        )
+
+    def lay4():
+        (v.down_part,) = order.run(
+            lambda last: lay_out(
+                v.fourth.pieces[:-1] + [last], v.fourth.starts(spot, shard_rows), [width]
+            ),
+            v.fourth.pieces[-1],
+        )
+
+    def pre():
+        v.grad_pre = order.run(
+            lambda a: multiply(a, v.down_part, True, scaled, extra=(v.slope, 0)), v.grad_three
+        )
+
+    def ring(value):
+        halves = [(value, 1, 0), (value, -1, 1)]
+        return Scatter(order, halves, group, spot, shard_rows // 2, shard_rows)
+
+    def near3():
+        v.sum3 = GroupSum(order, v.grad_pre, v.up_part, True)
+        v.sum3.near()
+
+    def dterm():
+        v.down_term = order.run(lambda a: weight_term(a, v.grad_three), v.activated)
+
+    def uterm():
+        v.up_term = order.run(lambda a: weight_term(a, v.grad_pre), v.act_three)
+
+    def mlp_start():
+        v.mlp_ring = Scatter(
+            order,
+            [(v.down_term, 1, 0), (v.up_term, -1, 0)],
+            group,
+            spot,
+            shard_rows,
+            shard_rows,
+        )
+
+    def mlp_step():
+        if v.mlp_ring.reach():
+            v.down_all, v.up_all = [over_ranks(found) for found in v.mlp_ring.sums]
+
+    def over_ranks(found):
+        return lax.all_gather(found, "rep", axis=0, tiled=True)
+
+    def fin3():
+        def finish(crossed):
+            grad_act = own_rows(v.sum3.mine + crossed.astype(jnp.float32))
+            grad_two = grad_block + normed_back(v.hidden_two, grad_act * (1.0 + v.scale_mlp))
+            return (
+                jnp.sum(grad_act, axis=1),
+                jnp.sum(grad_act * v.norm_three, axis=1),
+                grad_two,
+                flatten(grad_two).astype(jnp.bfloat16),
+            )
+
+        v.grad_shift_mlp, v.grad_scale_mlp, v.grad_two, grad_merge = order.run(
+            finish, v.sum3.crossed
+        )
+        v.grad_merge = send_rows(grad_merge)
+
+    def join4():
+        v.grad_merge = join_rows(v.grad_merge)
+
+    def mm4():
+        v.grad_mixed = order.run(lambda a: multiply(a, v.merge_part, True), v.grad_merge)
+
+    def cback():
+        v.grad_query, v.grad_keyval = order.run(
+            lambda a: attend_cross_back(
+                v.cross_queries,
+                v.keyval,
+                v.length_all,
+                v.logsum_cross,
+                a,
+                all_images,
+                heads,
+                score_scale,
+            ),
+            v.grad_mixed,
+        )
+
+    def near4():
+        v.sum4 = GroupSum(order, v.grad_query, v.query_part, True)
+        v.sum4.near()
+
+    def qterm():
+        v.cross_term = order.run(
+            lambda a: weight_term(a, v.grad_query, first=0, total=4 * part), v.act_two
+        )
+
+    def kterm():
+        v.cross_term = order.run(
+            lambda a, into: weight_term(a, v.grad_keyval, None, into, part, 4 * part),
+            v.text_all,
+            v.cross_term,
+        )
+
+    def mterm():
+        v.cross_term = order.run(
+            lambda a, into: weight_term(a, v.grad_merge, rank, into, 3 * part, 4 * part),
+            v.cross_all,
+            v.cross_term,
+        )
+
+    def cross_start():
+        v.cross_ring = ring(v.cross_term)
+
+    def cross_step():
+        if v.cross_ring.reach():
+            v.cross_found = over_ranks(jnp.concatenate(v.cross_ring.sums, axis=0))
+
+    def fin4():
+        def finish(crossed):
+            grad_act = own_rows(v.sum4.mine + crossed.astype(jnp.float32))
+            grad_one = v.grad_two + normed_back(v.hidden_one, grad_act * v.gain_full)
+            return (
+                jnp.sum(grad_act * v.norm_two, axis=1),
+                jnp.sum(grad_one * v.branch_one, axis=1),
+                grad_one,
+                flatten(v.gate_self * grad_one).astype(jnp.bfloat16),
+            )
+
+        v.gain_term, v.grad_gate_self, v.grad_one, grad_out = order.run(finish, v.sum4.crossed)
+        v.grad_out = send_rows(grad_out)
+
+    def join5():
+        v.grad_out = join_rows(v.grad_out)
+
+    def mm5():
+        v.grad_mixed = order.run(lambda a: multiply(a, v.out_part, True), v.grad_out)
+
+    def sback():
+        v.grad_qkv = order.run(
+            lambda a: attend_self_back(
+                v.qkv_act, v.logsum_self, a, all_images, heads, score_scale
+            ),
+            v.grad_mixed,
+        )
+
+    def near5():
+        v.sum5 = GroupSum(order, v.grad_qkv, v.qkv_part, True)
+        v.sum5.near()
+
+    def qkvterm():
+        v.self_term = order.run(
+            lambda a: weight_term(a, v.grad_qkv, first=0, total=4 * part), v.act_one
+        )
+
+    def oterm():
+        v.self_term = order.run(
+            lambda a, into: weight_term(a, v.grad_out, rank, into, 3 * part, 4 * part),
+            v.mixed_all,
+            v.self_term,
+        )
+
+    def self_start():
+        v.self_ring = ring(v.self_term)
+
+    def self_step():
+        if v.self_ring.reach():
+            own = jnp.concatenate(v.self_ring.sums, axis=0)
+            far = swap(own, 2)
+            v.self_found = [own, swap(own, 1), far, swap(far, 1)]
+
+    def fin5():
+        def finish(crossed):
+            grad_act = own_rows(v.sum5.mine + crossed.astype(jnp.float32))
+            image_grad = v.grad_one + normed_back(residual, grad_act * (1.0 + v.scale_self))
+            return (
+                jnp.sum(grad_act, axis=1),
+                jnp.sum(grad_act * norm_one, axis=1),
+                image_grad.astype(jnp.bfloat16),
+            )
+
+        v.grad_shift_self, v.grad_scale_self, v.image_grad = order.run(finish, v.sum5.crossed)
+
+    def near6():
+        v.sum6 = GroupSum(order, v.activated, v.down_part, False)
+        v.sum6.near()
+
+    def fin6():
+        def finish(crossed):
+            branch_three = own_rows(v.sum6.mine + crossed.astype(jnp.float32))
+            block_out = (v.hidden_two + v.gate_mlp * branch_three).astype(jnp.bfloat16)
+            vectors = jnp.concatenate(
+                [
+                    v.grad_shift_self,
+                    v.grad_scale_self,
+                    v.grad_gate_self,
+                    v.grad_shift_mlp,
+                    v.grad_scale_mlp,
+                    jnp.sum(grad_block * branch_three, axis=1),
+                    v.gain_term,
+                ],
+                axis=1,
+            )
+            return block_out, vectors.astype(jnp.bfloat16)
+
+        v.block_out, vectors = order.run(finish, v.sum6.crossed)
+        v.everyone = Everyone(order, vectors, group)
+
+    def hop():
+        v.everyone.hop()
+
+    def near7():
+        v.sum7 = GroupSum(order, v.grad_keyval, v.keyval_part, True)
+        v.sum7.near()
+
+    def fin7():
+        v.text_grad = order.run(
+            lambda crossed: (v.sum7.mine + crossed.astype(jnp.float32))
+            .astype(jnp.bfloat16)
+            .reshape(text_tokens.shape),
+            v.sum7.crossed,
+        )
+
+    def down_out():
+        v.down_grad = order.run(lambda a: spread_rows(a, width), v.down_all)
+
+    def up_out():
+        if aligned:
+            v.up_grad = order.run(
+                lambda a: spread_blocks(a, 0, group, hidden // (group * PEERS)), v.up_all
+            )
+        else:
+            v.up_grad = (
+                v.up_all.reshape(PEERS, shard_rows, group, -1)
+                .transpose(1, 2, 0, 3)
+                .reshape(shard_rows, hidden)
+                .astype(jnp.float32)
+            )
+
+    def mod_out():
+        while v.everyone.left:
+            hop()
+
+        def finish(found):
+            return (
+                outer_sum(conditions(v.all_steps), found[:, : 6 * width]),
+                jnp.sum(
+                    lax.dynamic_slice_in_dim(
+                        found, 6 * width + member * shard_rows, shard_rows, 1
+                    ).astype(jnp.float32),
+                    axis=0,
+                ),
+            )
+
+        v.mod_grad, v.gain_grad = order.run(finish, v.everyone.value)
+
+    def cross_out():
+        v.query_grad, v.keyval_grad, v.merge_grad = [
+            order.run(lambda a: spread_blocks(a, start, count, part), v.cross_found)
+            for start, count in ((0, 1), (1, 2), (3, 1))
+        ]
+
+    def self_out():
+        v.qkv_grad, v.out_grad = [
+            order.run(
+                lambda last: spread_peers(
+                    v.self_found[:-1] + [last], rank, start, count, part
+                ),
+                v.self_found[-1],
+            )
+            for start, count in ((0, 3), (3, 1))
+        ]
+
+    work = {
+        "A": lambda: order.tick(v.first, v.second),
+        "B": lambda: order.tick(v.third, v.fourth),
+        "xa": lambda: order.wait(v.act_one[1]),
+        "xt": lambda: order.wait(v.text_all[1]),
+        "F0": mlp_start,
+        "F": mlp_step,
+        "C0": cross_start,
+        "C": cross_step,
+        "S0": self_start,
+        "S": self_step,
+        "h": hop,
+        "self": self_attend,
+        "wo": lambda: order.wait(v.out_part),
+        "wm": lambda: order.wait(v.merge_part),
+        "dout": down_out,
+        "uout": up_out,
+        "mod": mod_out,
+        "cout": cross_out,
+        "sout": self_out,
+        "x1": lambda: order.wait(v.sum1.crossed),
+        "x2": lambda: order.wait(v.sum2.crossed),
+        "x3": lambda: order.wait(v.sum3.crossed),
+        "x4": lambda: order.wait(v.sum4.crossed),
+        "x5": lambda: order.wait(v.sum5.crossed),
+        "x6": lambda: order.wait(v.sum6.crossed),
+        "y2": lambda: order.wait(v.act_two[1]),
+        "y3": lambda: order.wait(v.act_three[1]),
+        "y4": lambda: order.wait(v.grad_merge[1]),
+        "y5": lambda: order.wait(v.grad_out[1]),
+        "rest1": lambda: v.sum1.rest(),
+        "rest2": lambda: v.sum2.rest(),
+        "rest3": lambda: v.sum3.rest(),
+        "rest4": lambda: v.sum4.rest(),
+        "rest5": lambda: v.sum5.rest(),
+        "rest6": lambda: v.sum6.rest(),
+        "rest7": lambda: v.sum7.rest(),
+    }
+    for step in (
+        (p1, p2, p3, p4, a0, ab, r, e, terms, start, ja, st, jt, sg, jg)
+        + (lay1, lay2, qkv, kv, near1, fin1, join2, cq, cross, near2, fin2, join3, sm, jm, sc, jc)
+        + (lay3, up, lay4, pre, near3, dterm, uterm, fin3, join4, mm4, cback, near4, qterm, kterm)
+        + (mterm, fin4, join5, mm5, sback, near5, qkvterm, oterm, fin5, near6, fin6, near7, fin7)
+    ):
+        work[step.__name__] = step
+    for name in PLAN:
+        work[name]()
     return (
-        block_out,
-        image_grad,
-        text_grad,
-        mod_grad,
-        order.run(lambda a: spread_blocks(a, 0, 3, part), self_all),
-        order.run(lambda a: spread_blocks(a, 3, 1, part), self_all),
-        query_grad,
-        keyval_grad,
-        merge_grad,
-        gain_grad,
-        up_grad,
-        down_grad,
+        v.block_out,
+        v.image_grad,
+        v.text_grad,
+        v.mod_grad,
+        v.qkv_grad,
+        v.out_grad,
+        v.query_grad,
+        v.keyval_grad,
+        v.merge_grad,
+        v.gain_grad,
+        v.up_grad,
+        v.down_grad,
     )
 
 

time: 1080 us -> 1050 us (0.972)
  waiting for transfers between devices: 454 us -> 428 us
    ppermute x28, waiting for transfers between devices: 181 us -> 102 us  [send(): lax.ppermute(self.pieces[-1], 'fsdp', ring_pairs(self.size, self.step))]
    ppermute x59 -> x60, waiting for transfers between devices: 128 us -> 151 us  [swap(): lax.ppermute(value, 'rep', [(peer, peer ^ mask) for peer in range(PEERS)])]
    all_to_all x1, waiting for transfers between devices: 0.01 us -> 18.8 us  [terms(): lax.all_to_all(found.reshape(group, images, -1), 'fsdp', split_axis=0, co...]
    ppermute x3, waiting for transfers between devices: 17.2 us -> 33.4 us  [send(): self.got = lax.ppermute(self.value, 'fsdp', pairs)]
    all_gather x4 -> x3, waiting for transfers between devices: 15.1 us -> 0.02 us  [over_ranks(): return lax.all_gather(found, 'rep', axis=0, tiled=True)]
    ppermute x59 -> x60, starting transfers between devices: 40.7 us -> 28.7 us  [swap(): lax.ppermute(value, 'rep', [(peer, peer ^ mask) for peer in range(PEERS)])]
    pallas_call x7 -> x9, Pallas kernels: 18.6 us -> 22.1 us  [the longest x7 15.5 us: stack_rows(): pl.pallas_call(kernel, in_specs=[pl.BlockSpec(memory_space=pl.ANY)] * cou...]
    unnamed x252 -> x268, local copies, waits for them, and re-layouts: 39.6 us -> 40 us
  transfers between devices with their start and end apart: 142 -> 142, of which waited for: 72 -> 64; matrix products, arithmetic and copies ran while one was open for 6% -> 6% of each run, Pallas kernels for 29% -> 26%
where the time goes in v4:
time: 1050 us; the launch traced here: 1030 us
  waiting for transfers between devices  428 us (41%)
  Pallas kernels  359 us (34%)
  starting transfers between devices  122 us (12%)
  local copies, waits for them, and re-layouts  52.6 us (5%)
  other arithmetic  43.6 us (4%)
  between operations  17.1 us (2%)
  matrix products  11.7 us (1%)
    ppermute x60, waiting for transfers between devices, swap(): lax.ppermute(value, 'rep', [(peer, peer ^ mask) for peer in range(PEERS)])  151 us
    ppermute x42, waiting for transfers between devices, reach(): lax.ppermute(value, 'fsdp', ring_pairs(self.size, direction))  107 us
    ppermute x28, waiting for transfers between devices, send(): lax.ppermute(self.pieces[-1], 'fsdp', ring_pairs(self.size, self.step))  102 us
    pallas_call x14, Pallas kernels, multiply(): pl.pallas_call(kernel, grid=(columns // width,), in_specs=specs, out_spec...  94.6 us
    pallas_call x24, Pallas kernels, ring_add(): pl.pallas_call(kernel, grid_spec=pltpu.PrefetchScalarGridSpec(num_scalar_...  60.1 us
    pallas_call x7, Pallas kernels, weight_term(): pl.pallas_call(kernel, grid_spec=pltpu.PrefetchScalarGridSpec(num_scalar_...  58.7 us
    ppermute x42, starting transfers between devices, reach(): lax.ppermute(value, 'fsdp', ring_pairs(self.size, direction))  44.7 us
    pallas_call x7, Pallas kernels, multiply_rest(): pl.pallas_call(kernel, grid=(columns // width,), in_specs=[pl.BlockSpec((...  42.2 us
  transfers between devices with their start and end apart: 142, of which 64 were waited for; matrix products, arithmetic and copies ran while one was open for 6% of the time, Pallas kernels for 26%

profile of v4, /device:TPU:0, one launch (start us, length us, event | category | flops | bytes accessed | tf_op | source)
XLA Modules:
  0.0 1033.9 jit_solution(18005134128934292982)
XLA Ops:
  31.9 9.3 collective-permute-done.3
  43.7 21.3 %collective-permute-done.4 = f32[2,260]{1,0:T(2,128)S(1)} collective-permute-done((f32[2,260]{1,0:T(2,128)S(1)}, f32[2,260]{1,0:T(2,128)S(1)}, u32[]{:S(2)}, u32[]{:S(2)}) %collective-permute-start.4) | collective-permute-done | bytes 2112 | tf_op jit(solution)/shard_map/ppermute | solution.py:774
  84.2 18.8 %all-to-all-done = f32[8,1,12288]{2,1,0:T(1,128)S(1)} async-done(((f32[8,1,12288]{2,1,0:T(1,128)}), f32[8,1,12288]{2,1,0:T(1,128)S(1)}, u32[]{:S(2)}, u32[]{:S(2)}) %all-to-all-start) | async-done | bytes 393248 | tf_op jit(solution)/shard_map/all_to_all | solution.py:983
  111.6 16.4 %collective-permute-done.16.refs_4_ = bf16[256,2048]{1,0:T(8,128)(2,1)S(1)} collective-permute-done((bf16[256,2048]{1,0:T(8,128)(2,1)}, bf16[256,2048]{1,0:T(8,128)(2,1)S(1)}, u32[]{:S(2)}, u32[]{:S(2)}) %collective-permute-start.16) | collective-permute-done | bytes 1048608 | tf_op jit(solution)/shard_map/ppermute | solution.py:656
  131.8 19.3 %collective-permute-done.18.refs_5_ = bf16[256,2048]{1,0:T(8,128)(2,1)S(1)} collective-permute-done((bf16[256,2048]{1,0:T(8,128)(2,1)S(1)}, bf16[256,2048]{1,0:T(8,128)(2,1)S(1)}, u32[]{:S(2)}, u32[]{:S(2)}) %collective-permute-start.18) | collective-permute-done | bytes 1048608 | tf_op jit(solution)/shard_map/ppermute | solution.py:656
  165.7 8.5 collective-permute-done.20.refs_6_
  176.4 14.8 %collective-permute-done.23.refs_7_ = bf16[256,2048]{1,0:T(8,128)(2,1)} collective-permute-done((bf16[256,2048]{1,0:T(8,128)(2,1)}, bf16[256,2048]{1,0:T(8,128)(2,1)}, u32[]{:S(2)}, u32[]{:S(2)}) %collective-permute-start.23) | collective-permute-done | bytes 1048608 | tf_op jit(solution)/shard_map/ppermute | solution.py:656
  207.5 10.0 multiply.63.qkv_ref
  222.2 9.0 collective-permute-done.25
  242.8 17.0 %collective-permute-done.44.refs_1_ = bf16[256,2048]{1,0:T(8,128)(2,1)S(1)} collective-permute-done((bf16[256,2048]{1,0:T(8,128)(2,1)S(1)}, bf16[256,2048]{1,0:T(8,128)(2,1)S(1)}, u32[]{:S(2)}, u32[]{:S(2)}) %collective-permute-start.44) | collective-permute-done | bytes 1048608 | tf_op jit(solution)/shard_map/ppermute | solution.py:656
  276.0 8.5 collective-permute-done.46.refs_2_
  308.4 9.4 collective-permute-done.36
  355.2 16.0 %collective-permute-done.52.refs_5_ = bf16[256,2048]{1,0:T(8,128)(2,1)} collective-permute-done((bf16[256,2048]{1,0:T(8,128)(2,1)}, bf16[256,2048]{1,0:T(8,128)(2,1)}, u32[]{:S(2)}, u32[]{:S(2)}) %collective-permute-start.52) | collective-permute-done | bytes 1048608 | tf_op jit(solution)/shard_map/ppermute | solution.py:656
  375.8 20.8 %collective-permute-done.40 = bf16[256,2048]{1,0:T(8,128)(2,1)S(1)} collective-permute-done((bf16[256,2048]{1,0:T(8,128)(2,1)S(1)}, bf16[256,2048]{1,0:T(8,128)(2,1)S(1)}, u32[]{:S(2)}, u32[]{:S(2)}) %collective-permute-start.40) | collective-permute-done | bytes 1048608 | tf_op jit(solution)/shard_map/ppermute | solution.py:359
  404.9 14.1 %collective-permute-done.58.refs_1_ = bf16[256,2048]{1,0:T(8,128)(2,1)S(1)} collective-permute-done((bf16[256,2048]{1,0:T(8,128)(2,1)S(1)}, bf16[256,2048]{1,0:T(8,128)(2,1)S(1)}, u32[]{:S(2)}, u32[]{:S(2)}) %collective-permute-start.58) | collective-permute-done | bytes 1048608 | tf_op jit(solution)/shard_map/ppermute | solution.py:359
  419.5 20.4 %collective-permute-done.41.refs_1_ = bf16[256,2048]{1,0:T(8,128)(2,1)} collective-permute-done((bf16[256,2048]{1,0:T(8,128)(2,1)S(1)}, bf16[256,2048]{1,0:T(8,128)(2,1)}, u32[]{:S(2)}, u32[]{:S(2)}) %collective-permute-start.41) | collective-permute-done | bytes 1048608 | tf_op jit(solution)/shard_map/ppermute | solution.py:359
  456.4 18.3 %multiply.68 = (bf16[1024,2048]{1,0:T(8,128)(2,1)S(1)}, bf16[1024,2048]{1,0:T(8,128)(2,1)}) custom-call(bf16[1024,2048]{1,0:T(8,128)(2,1)} %stack_rows.10.refs_0_.left_ref, bf16[2048,2048]{1,0:T(8,128)(2,1)} %lay_out.6.refs_1_.right_ref), custom_call_target="tpu_custom_call" | custom-call | flops 8589934592 | bytes 16777216 | tf_op jit(solution)/shard_map/multiply/pallas_call | solution.py:482
  482.1 13.0 %multiply.69.refs_0_.left_ref.right_ref = bf16[1024,2048]{1,0:T(8,128)(2,1)S(1)} custom-call(bf16[1024,2048]{1,0:T(8,128)(2,1)} %stack_rows.11.refs_0_.right_ref, bf16[2048,2048]{1,0:T(8,128)(2,1)} %lay_out.7.refs_1_.right_ref, bf16[1024,2048]{1,0:T(8,128)(2,1)} %get-tuple-element.306.refs_2_), custom_call_target="tpu_custom_call" | custom-call | flops 8589934592 | bytes 16777216 | tf_op jit(solution)/shard_map/multiply/pallas_call | solution.py:482
  497.2 7.8 multiply.70
  509.3 8.7 multiply_rest.9
  518.6 13.9 %weight_term.7.refs_0_ = bf16[2048,2048]{1,0:T(8,128)(2,1)} custom-call(s32[1]{0:T(128)} %constant.347.clone.1.chosen_ref, bf16[1024,2048]{1,0:T(8,128)(2,1)S(1)} %copy-done.82, bf16[1024,2048]{1,0:T(8,128)(2,1)} %stack_rows.11.refs_0_.right_ref), custom_call_target="tpu_custom_call" | custom-call | flops 8589934592 | bytes 16777216 | tf_op jit(solution)/shard_map/weight_term/pallas_call | solution.py:507
  532.5 13.7 %weight_term.8.refs_1_ = bf16[2048,2048]{1,0:T(8,128)(2,1)} custom-call(s32[1]{0:T(128)} %constant.347.clone.1.chosen_ref, bf16[1024,2048]{1,0:T(8,128)(2,1)S(1)} %copy-done.12, bf16[1024,2048]{1,0:T(8,128)(2,1)} %copy-done.83), custom_call_target="tpu_custom_call" | custom-call | flops 8589934592 | bytes 16777216 | tf_op jit(solution)/shard_map/weight_term/pallas_call | solution.py:507
  574.7 9.5 collective-permute-done.68.refs_2_
  668.6 7.9 multiply_rest.11
  710.1 8.0 attend_self_back.1.refs_0_.left_ref.right_ref
  732.8 7.9 collective-permute-done.92.refs_2_
  756.1 12.2 %weight_term.12.refs_0_ = bf16[2048,2048]{1,0:T(8,128)(2,1)} custom-call(s32[1]{0:T(128)} %constant.347.clone.1.chosen_ref, bf16[1024,2048]{1,0:T(8,128)(2,1)} %stack_rows.7.refs_0_.left_ref, bf16[1024,1536]{1,0:T(8,128)(2,1)S(1)} %copy-done.20), custom_call_target="tpu_custom_call" | custom-call | flops 6442450944 | bytes 13631488 | tf_op jit(solution)/shard_map/weight_term/pallas_call | solution.py:507
  787.9 32.8 %collective-permute-done.105.refs_2_ = bf16[128,2048]{1,0:T(8,128)(2,1)S(1)} collective-permute-done((bf16[128,2048]{1,0:T(8,128)(2,1)S(1)}, bf16[128,2048]{1,0:T(8,128)(2,1)S(1)}, u32[]{:S(2)}, u32[]{:S(2)}) %collective-permute-start.105) | collective-permute-done | bytes 524320 | tf_op jit(solution)/shard_map/ppermute | solution.py:757
  851.0 16.8 %collective-permute-done.109.refs_2_ = bf16[128,2048]{1,0:T(8,128)(2,1)S(1)} collective-permute-done((bf16[128,2048]{1,0:T(8,128)(2,1)S(1)}, bf16[128,2048]{1,0:T(8,128)(2,1)S(1)}, u32[]{:S(2)}, u32[]{:S(2)}) %collective-permute-start.109) | collective-permute-done | bytes 524320 | tf_op jit(solution)/shard_map/ppermute | solution.py:757
  951.1 10.8 %collective-permute-done.129 = bf16[8,14336]{1,0:T(8,128)(2,1)S(1)} collective-permute-done((bf16[8,14336]{1,0:T(8,128)(2,1)S(1)}, bf16[8,14336]{1,0:T(8,128)(2,1)S(1)}, u32[]{:S(2)}, u32[]{:S(2)}) %collective-permute-start.129) | collective-permute-done | bytes 229408 | tf_op jit(solution)/shard_map/ppermute | solution.py:800
  973.6 19.3 %collective-permute-done.136.refs_2_ = bf16[256,2048]{1,0:T(8,128)(2,1)S(1)} collective-permute-done((bf16[256,2048]{1,0:T(8,128)(2,1)S(1)}, bf16[256,2048]{1,0:T(8,128)(2,1)S(1)}, u32[]{:S(2)}, u32[]{:S(2)}) %collective-permute-start.136) | collective-permute-done | bytes 1048608 | tf_op jit(solution)/shard_map/ppermute | solution.py:359
  1005.2 7.9 fusion.23
  (684 shorter events, 574.7 us)
Async XLA Ops:
  41.2 28.8 %collective-permute-start.12 = (bf16[256,2048]{1,0:T(8,128)(2,1)S(1)}, bf16[256,2048]{1,0:T(8,128)(2,1)}, u32[]{:S(2)}, u32[]{:S(2)}) collective-permute-start(bf16[256,2048]{1,0:T(8,128)(2,1)S(1)} %collective-permute-done.10.refs_1_), channel_id=1, source_target_pairs={{0,1},{2,0},{4,2},{6,4},{7,6},{5,7},{3,5},{1,3},{8,9},{10,8},{12,1... | collective-permute-start | bytes 3145736 | tf_op jit(solution)/shard_map/ppermute | solution.py:656
  69.9 33.9 %collective-permute-start.14 = (bf16[256,2048]{1,0:T(8,128)(2,1)}, bf16[256,2048]{1,0:T(8,128)(2,1)}, u32[]{:S(2)}, u32[]{:S(2)}) collective-permute-start(bf16[256,2048]{1,0:T(8,128)(2,1)} %collective-permute-done.12.refs_2_), channel_id=1, source_target_pairs={{0,1},{2,0},{4,2},{6,4},{7,6},{5,7},{3,5},{1,3},{8,9},{10,8},{12,1... | collective-permute-start | bytes 3145736 | tf_op jit(solution)/shard_map/ppermute | solution.py:656
  72.9 31.0 %collective-permute-start.13 = (bf16[256,2048]{1,0:T(8,128)(2,1)}, bf16[256,2048]{1,0:T(8,128)(2,1)}, u32[]{:S(2)}, u32[]{:S(2)}) collective-permute-start(bf16[256,2048]{1,0:T(8,128)(2,1)} %collective-permute-done.11.refs_2_), channel_id=1, source_target_pairs={{0,2},{2,4},{4,6},{6,7},{7,5},{5,3},{3,1},{1,0},{8,10},{10,12},{12... | collective-permute-start | bytes 3145736 | tf_op jit(solution)/shard_map/ppermute | solution.py:656
  82.6 854.1 %all-gather.4.cloned.1.call-start = ((), (), s32[]{:S(2)}) async-start(), calls=%async_computation.1 | async-start | bytes 5242880 | tf_op jit(solution)/shard_map/all_gather | solution.py:1160
  274.2 31.8 %collective-permute-start.37 = (bf16[512,512]{1,0:T(8,128)(2,1)}, bf16[512,512]{1,0:T(8,128)(2,1)S(1)}, u32[]{:S(2)}, u32[]{:S(2)}) collective-permute-start(bf16[512,512]{1,0:T(8,128)(2,1)} %get-tuple-element.485), channel_id=1, source_target_pairs={{0,24},{8,16},{16,8},{24,0},{1,25},{9,17},{17,9},{25,1},{2,26},{10... | collective-permute-start | bytes 1572872 | tf_op jit(solution)/shard_map/ppermute | solution.py:359
  274.5 43.2 %collective-permute-start.36 = (bf16[512,512]{1,0:T(8,128)(2,1)}, bf16[512,512]{1,0:T(8,128)(2,1)}, u32[]{:S(2)}, u32[]{:S(2)}) collective-permute-start(bf16[512,512]{1,0:T(8,128)(2,1)} %get-tuple-element.486), channel_id=1, source_target_pairs={{0,16},{8,24},{16,0},{24,8},{1,17},{9,25},{17,1},{25,9},{2,18},{10... | collective-permute-start | bytes 1572872 | tf_op jit(solution)/shard_map/ppermute | solution.py:359
  284.5 33.4 %collective-permute-start.35 = (bf16[512,512]{1,0:T(8,128)(2,1)S(1)}, bf16[512,512]{1,0:T(8,128)(2,1)S(1)}, u32[]{:S(2)}, u32[]{:S(2)}) collective-permute-start(bf16[512,512]{1,0:T(8,128)(2,1)S(1)} %get-tuple-element.487), channel_id=1, source_target_pairs={{0,8},{8,0},{16,24},{24,16},{1,9},{9,1},{17,25},{25,17},{2,10},{10... | collective-permute-start | bytes 1572872 | tf_op jit(solution)/shard_map/ppermute | solution.py:359
  289.1 30.9 %collective-permute-start.48 = (bf16[256,2048]{1,0:T(8,128)(2,1)S(1)}, bf16[256,2048]{1,0:T(8,128)(2,1)}, u32[]{:S(2)}, u32[]{:S(2)}) collective-permute-start(bf16[256,2048]{1,0:T(8,128)(2,1)S(1)} %collective-permute-done.46.refs_2_), channel_id=1, source_target_pairs={{0,2},{2,4},{4,6},{6,7},{7,5},{5,3},{3,1},{1,0},{8,10},{10,12},{12... | collective-permute-start | bytes 3145736 | tf_op jit(solution)/shard_map/ppermute | solution.py:656
  353.2 43.4 %collective-permute-start.40 = (bf16[256,2048]{1,0:T(8,128)(2,1)S(1)}, bf16[256,2048]{1,0:T(8,128)(2,1)S(1)}, u32[]{:S(2)}, u32[]{:S(2)}) collective-permute-start(bf16[256,2048]{1,0:T(8,128)(2,1)S(1)} %get-tuple-element.283), channel_id=1, source_target_pairs={{0,16},{8,24},{16,0},{24,8},{1,17},{9,25},{17,1},{25,9},{2,18},{10... | collective-permute-start | bytes 3145736 | tf_op jit(solution)/shard_map/ppermute | solution.py:359
  354.7 64.4 %collective-permute-start.58 = (bf16[256,2048]{1,0:T(8,128)(2,1)S(1)}, bf16[256,2048]{1,0:T(8,128)(2,1)S(1)}, u32[]{:S(2)}, u32[]{:S(2)}) collective-permute-start(bf16[256,2048]{1,0:T(8,128)(2,1)S(1)} %copy-done.18), channel_id=1, source_target_pairs={{0,16},{8,24},{16,0},{24,8},{1,17},{9,25},{17,1},{25,9},{2,18},{10... | collective-permute-start | bytes 3145736 | tf_op jit(solution)/shard_map/ppermute | solution.py:359
  371.2 31.1 %collective-permute-start.59 = (bf16[1024,512]{1,0:T(8,128)(2,1)S(1)}, bf16[1024,512]{1,0:T(8,128)(2,1)S(1)}, u32[]{:S(2)}, u32[]{:S(2)}) collective-permute-start(bf16[1024,512]{1,0:T(8,128)(2,1)S(1)} %get-tuple-element.300.refs_0_.left_ref), channel_id=1, source_target_pairs={{0,8},{8,0},{16,24},{24,16},{1,9},{9,1},{17,25},{25,17},{2,10},{10... | collective-permute-start | bytes 3145736 | tf_op jit(solution)/shard_map/ppermute | solution.py:359
  399.6 40.3 %collective-permute-start.41 = (bf16[256,2048]{1,0:T(8,128)(2,1)S(1)}, bf16[256,2048]{1,0:T(8,128)(2,1)}, u32[]{:S(2)}, u32[]{:S(2)}) collective-permute-start(bf16[256,2048]{1,0:T(8,128)(2,1)S(1)} %fusion.19.refs_0_), channel_id=1, source_target_pairs={{0,16},{8,24},{16,0},{24,8},{1,17},{9,25},{17,1},{25,9},{2,18},{10... | collective-permute-start | bytes 3145736 | tf_op jit(solution)/shard_map/ppermute | solution.py:359
  400.2 39.7 %collective-permute-start.56 = (bf16[256,2048]{1,0:T(8,128)(2,1)}, bf16[256,2048]{1,0:T(8,128)(2,1)}, u32[]{:S(2)}, u32[]{:S(2)}) collective-permute-start(bf16[256,2048]{1,0:T(8,128)(2,1)} %collective-permute-done.54.refs_6_), channel_id=1, source_target_pairs={{0,2},{2,4},{4,6},{6,7},{7,5},{5,3},{3,1},{1,0},{8,10},{10,12},{12... | collective-permute-start | bytes 3145736 | tf_op jit(solution)/shard_map/ppermute | solution.py:656
  401.6 38.8 %collective-permute-start.57 = (bf16[256,2048]{1,0:T(8,128)(2,1)}, bf16[256,2048]{1,0:T(8,128)(2,1)}, u32[]{:S(2)}, u32[]{:S(2)}) collective-permute-start(bf16[256,2048]{1,0:T(8,128)(2,1)} %collective-permute-done.55.refs_6_), channel_id=1, source_target_pairs={{0,1},{2,0},{4,2},{6,4},{7,6},{5,7},{3,5},{1,3},{8,9},{10,8},{12,1... | collective-permute-start | bytes 3145736 | tf_op jit(solution)/shard_map/ppermute | solution.py:656
  505.6 52.8 %collective-permute-start.71 = (bf16[1024,512]{1,0:T(8,128)(2,1)}, bf16[1024,512]{1,0:T(8,128)(2,1)}, u32[]{:S(2)}, u32[]{:S(2)}) collective-permute-start(bf16[1024,512]{1,0:T(8,128)(2,1)} %get-tuple-element.321.refs_0_.left_ref), channel_id=1, source_target_pairs={{0,16},{8,24},{16,0},{24,8},{1,17},{9,25},{17,1},{25,9},{2,18},{10... | collective-permute-start | bytes 3145736 | tf_op jit(solution)/shard_map/ppermute | solution.py:359
  518.0 35.5 %collective-permute-start.66 = (bf16[256,2048]{1,0:T(8,128)(2,1)}, bf16[256,2048]{1,0:T(8,128)(2,1)S(1)}, u32[]{:S(2)}, u32[]{:S(2)}) collective-permute-start(bf16[256,2048]{1,0:T(8,128)(2,1)} %get-tuple-element.314), channel_id=1, source_target_pairs={{0,16},{8,24},{16,0},{24,8},{1,17},{9,25},{17,1},{25,9},{2,18},{10... | collective-permute-start | bytes 3145736 | tf_op jit(solution)/shard_map/ppermute | solution.py:359
  626.3 35.5 %collective-permute-start.82 = (bf16[256,2048]{1,0:T(8,128)(2,1)}, bf16[256,2048]{1,0:T(8,128)(2,1)S(1)}, u32[]{:S(2)}, u32[]{:S(2)}) collective-permute-start(bf16[256,2048]{1,0:T(8,128)(2,1)} %copy-done.60), channel_id=1, source_target_pairs={{0,8},{8,0},{16,24},{24,16},{1,9},{9,1},{17,25},{25,17},{2,10},{10... | collective-permute-start | bytes 3145736 | tf_op jit(solution)/shard_map/ppermute | solution.py:359
  626.3 37.5 %collective-permute-start.83 = (bf16[256,2048]{1,0:T(8,128)(2,1)}, bf16[256,2048]{1,0:T(8,128)(2,1)S(1)}, u32[]{:S(2)}, u32[]{:S(2)}) collective-permute-start(bf16[256,2048]{1,0:T(8,128)(2,1)} %copy-done.59), channel_id=1, source_target_pairs={{0,8},{8,0},{16,24},{24,16},{1,9},{9,1},{17,25},{25,17},{2,10},{10... | collective-permute-start | bytes 3145736 | tf_op jit(solution)/shard_map/ppermute | solution.py:359
  662.7 31.6 %collective-permute-start.86 = (bf16[128,2048]{1,0:T(8,128)(2,1)}, bf16[128,2048]{1,0:T(8,128)(2,1)}, u32[]{:S(2)}, u32[]{:S(2)}) collective-permute-start(bf16[128,2048]{1,0:T(8,128)(2,1)} %get-tuple-element.348), channel_id=1, source_target_pairs={{0,2},{2,4},{4,6},{6,7},{7,5},{5,3},{3,1},{1,0},{8,10},{10,12},{12... | collective-permute-start | bytes 1572872 | tf_op jit(solution)/shard_map/ppermute | solution.py:757
  664.8 30.3 %collective-permute-start.87 = (bf16[128,2048]{1,0:T(8,128)(2,1)}, bf16[128,2048]{1,0:T(8,128)(2,1)}, u32[]{:S(2)}, u32[]{:S(2)}) collective-permute-start(bf16[128,2048]{1,0:T(8,128)(2,1)} %get-tuple-element.349), channel_id=1, source_target_pairs={{0,1},{2,0},{4,2},{6,4},{7,6},{5,7},{3,5},{1,3},{8,9},{10,8},{12,1... | collective-permute-start | bytes 1572872 | tf_op jit(solution)/shard_map/ppermute | solution.py:757
  731.3 44.1 %collective-permute-start.102 = (bf16[256,2048]{1,0:T(8,128)(2,1)}, bf16[256,2048]{1,0:T(8,128)(2,1)}, u32[]{:S(2)}, u32[]{:S(2)}) collective-permute-start(bf16[256,2048]{1,0:T(8,128)(2,1)} %get-tuple-element.373), channel_id=1, source_target_pairs={{0,2},{2,4},{4,6},{6,7},{7,5},{5,3},{3,1},{1,0},{8,10},{10,12},{12... | collective-permute-start | bytes 3145736 | tf_op jit(solution)/shard_map/ppermute | solution.py:757
  740.8 35.8 %collective-permute-start.103 = (bf16[256,2048]{1,0:T(8,128)(2,1)}, bf16[256,2048]{1,0:T(8,128)(2,1)}, u32[]{:S(2)}, u32[]{:S(2)}) collective-permute-start(bf16[256,2048]{1,0:T(8,128)(2,1)} %get-tuple-element.374), channel_id=1, source_target_pairs={{0,1},{2,0},{4,2},{6,4},{7,6},{5,7},{3,5},{1,3},{8,9},{10,8},{12,1... | collective-permute-start | bytes 3145736 | tf_op jit(solution)/shard_map/ppermute | solution.py:757
  752.1 29.5 %collective-permute-start.100 = (bf16[128,2048]{1,0:T(8,128)(2,1)}, bf16[128,2048]{1,0:T(8,128)(2,1)S(1)}, u32[]{:S(2)}, u32[]{:S(2)}) collective-permute-start(bf16[128,2048]{1,0:T(8,128)(2,1)} %copy-done.66), channel_id=1, source_target_pairs={{0,2},{2,4},{4,6},{6,7},{7,5},{5,3},{3,1},{1,0},{8,10},{10,12},{12... | collective-permute-start | bytes 1572872 | tf_op jit(solution)/shard_map/ppermute | solution.py:757
  753.2 29.3 %collective-permute-start.101 = (bf16[128,2048]{1,0:T(8,128)(2,1)}, bf16[128,2048]{1,0:T(8,128)(2,1)S(1)}, u32[]{:S(2)}, u32[]{:S(2)}) collective-permute-start(bf16[128,2048]{1,0:T(8,128)(2,1)} %copy-done.65), channel_id=1, source_target_pairs={{0,1},{2,0},{4,2},{6,4},{7,6},{5,7},{3,5},{1,3},{8,9},{10,8},{12,1... | collective-permute-start | bytes 1572872 | tf_op jit(solution)/shard_map/ppermute | solution.py:757
  775.4 59.0 %collective-permute-start.98 = (bf16[128,2048]{1,0:T(8,128)(2,1)S(1)}, bf16[128,2048]{1,0:T(8,128)(2,1)S(1)}, u32[]{:S(2)}, u32[]{:S(2)}) collective-permute-start(bf16[128,2048]{1,0:T(8,128)(2,1)S(1)} %get-tuple-element.385), channel_id=1, source_target_pairs={{0,2},{2,4},{4,6},{6,7},{7,5},{5,3},{3,1},{1,0},{8,10},{10,12},{12... | collective-permute-start | bytes 1572872 | tf_op jit(solution)/shard_map/ppermute | solution.py:757
  776.6 57.8 %collective-permute-start.99 = (bf16[128,2048]{1,0:T(8,128)(2,1)S(1)}, bf16[128,2048]{1,0:T(8,128)(2,1)S(1)}, u32[]{:S(2)}, u32[]{:S(2)}) collective-permute-start(bf16[128,2048]{1,0:T(8,128)(2,1)S(1)} %get-tuple-element.386), channel_id=1, source_target_pairs={{0,1},{2,0},{4,2},{6,4},{7,6},{5,7},{3,5},{1,3},{8,9},{10,8},{12,1... | collective-permute-start | bytes 1572872 | tf_op jit(solution)/shard_map/ppermute | solution.py:757
  780.4 55.9 %collective-permute-start.111 = (bf16[256,2048]{1,0:T(8,128)(2,1)S(1)}, bf16[256,2048]{1,0:T(8,128)(2,1)S(1)}, u32[]{:S(2)}, u32[]{:S(2)}) collective-permute-start(bf16[256,2048]{1,0:T(8,128)(2,1)S(1)} %get-tuple-element.389), channel_id=1, source_target_pairs={{0,2},{2,4},{4,6},{6,7},{7,5},{5,3},{3,1},{1,0},{8,10},{10,12},{12... | collective-permute-start | bytes 3145736 | tf_op jit(solution)/shard_map/ppermute | solution.py:757
  781.6 54.8 %collective-permute-start.112 = (bf16[256,2048]{1,0:T(8,128)(2,1)S(1)}, bf16[256,2048]{1,0:T(8,128)(2,1)S(1)}, u32[]{:S(2)}, u32[]{:S(2)}) collective-permute-start(bf16[256,2048]{1,0:T(8,128)(2,1)S(1)} %get-tuple-element.390), channel_id=1, source_target_pairs={{0,1},{2,0},{4,2},{6,4},{7,6},{5,7},{3,5},{1,3},{8,9},{10,8},{12,1... | collective-permute-start | bytes 3145736 | tf_op jit(solution)/shard_map/ppermute | solution.py:757
  784.4 36.3 %collective-permute-start.105 = (bf16[128,2048]{1,0:T(8,128)(2,1)S(1)}, bf16[128,2048]{1,0:T(8,128)(2,1)S(1)}, u32[]{:S(2)}, u32[]{:S(2)}) collective-permute-start(bf16[128,2048]{1,0:T(8,128)(2,1)S(1)} %get-tuple-element.393), channel_id=1, source_target_pairs={{0,2},{2,4},{4,6},{6,7},{7,5},{5,3},{3,1},{1,0},{8,10},{10,12},{12... | collective-permute-start | bytes 1572872 | tf_op jit(solution)/shard_map/ppermute | solution.py:757
  840.7 123.0 %all-gather.6.cloned.1.call-start = ((), (), s32[]{:S(2)}) async-start(), calls=%async_computation.2 | async-start | bytes 5242880 | tf_op jit(solution)/shard_map/all_gather | solution.py:1160
  841.4 171.7 %all-gather.8.cloned.1.call-start = ((), (), s32[]{:S(2)}) async-start(), calls=%async_computation.3 | async-start | bytes 5242880 | tf_op jit(solution)/shard_map/all_gather | solution.py:1160
  843.8 40.1 %collective-permute-start.84 = (bf16[256,2048]{1,0:T(8,128)(2,1)S(1)}, bf16[256,2048]{1,0:T(8,128)(2,1)S(1)}, u32[]{:S(2)}, u32[]{:S(2)}) collective-permute-start(bf16[256,2048]{1,0:T(8,128)(2,1)S(1)} %copy-done.58), channel_id=1, source_target_pairs={{0,16},{8,24},{16,0},{24,8},{1,17},{9,25},{17,1},{25,9},{2,18},{10... | collective-permute-start | bytes 3145736 | tf_op jit(solution)/shard_map/ppermute | solution.py:359
  (240 other events, 3212.5 us)
Sparse Core Ops, SparseCore 0:
  840.8 48.3 all-gather.3
  891.3 33.9 all-gather.5
  928.0 38.8 all-gather.7

commit v5 on v4

--- a/solution.py
+++ b/solution.py
@@ -572,22 +572,22 @@
 
     def run(self, work, first, *others):
         if self.token:
-            first, self.token = lax.optimization_barrier((first, self.token))
+            first = after(first, self.token)
         found = work(first, *others)
         self.token = tuple(jax.tree.leaves(found))
         return found
 
     def hold(self, value):
-        value, self.token = lax.optimization_barrier((value, self.token))
-        return value
+        return after(value, self.token)
 
     def tick(self, *rings):
         heads = [ring.pieces[-1] for ring in rings]
-        heads, self.token = lax.optimization_barrier((heads, self.token))
-        for ring, head in zip(rings, heads):
+        after_work = after(heads, self.token)
+        for ring, head in zip(rings, after_work):
             ring.pieces[-1] = head
             if ring.sevenths < 7:
                 ring.send()
+        self.wait(*heads)
 
     def wait(self, *values):
         self.token = self.token + tuple(jax.tree.leaves(values))
@@ -811,14 +811,14 @@
 
 PLAN = (
     "p1", "p2", "a0", "r", "p3", "p4", "A", "e", "A", "e", "A", "e", "terms", "A", "start", "xa",
-    "A", "ja", "st", "xt", "A", "jt", "sg", "A", "ab", "lay1", "lay2", "qkv", "B", "kv", "B",
-    "self", "wo", "near1", "rest1", "wm", "B", "x1", "fin1", "y2", "B", "join2", "sm", "cq",
-    "cross", "near2", "B", "rest2", "x2", "B", "fin2", "y3", "B", "join3", "sc", "jm", "jg",
-    "lay3", "up", "lay4", "pre", "near3", "rest3", "dterm", "uterm", "F0", "x3", "fin3", "jc",
-    "near6", "y4", "F", "join4", "mm4", "cback", "near4", "F", "rest4", "qterm", "kterm", "mterm",
-    "C0", "x4", "F", "fin4", "rest6", "y5", "F", "C", "join5", "mm5", "sback", "near5", "F", "C",
-    "rest5", "qkvterm", "oterm", "S0", "x5", "F", "C", "fin5", "C", "S", "F", "C", "S", "x6",
-    "fin6", "C", "S", "h", "near7", "C", "S", "rest7", "h", "S", "h", "dout", "fin7", "S", "h",
+    "A", "ja", "st", "xt", "A", "jt", "sg", "A", "ab", "lay1", "qkv", "lay2", "B", "kv", "self",
+    "wo", "near1", "rest1", "B", "wm", "B", "x1", "fin1", "B", "y2", "join2", "sm", "cq", "cross",
+    "near2", "B", "rest2", "B", "x2", "fin2", "B", "y3", "join3", "sc", "lay3", "up", "jg",
+    "lay4", "pre", "near3", "rest3", "dterm", "uterm", "F0", "x3", "fin3", "jc", "near6", "F",
+    "y4", "join4", "mm4", "cback", "near4", "F", "rest4", "qterm", "kterm", "mterm", "C0", "F",
+    "x4", "fin4", "near7", "C", "F", "y5", "join5", "mm5", "sback", "near5", "F", "C", "rest5",
+    "qkvterm", "jm", "oterm", "S0", "F", "C", "x5", "fin5", "rest6", "S", "C", "F", "S", "C",
+    "x6", "fin6", "S", "C", "h", "S", "C", "h", "rest7", "S", "h", "dout", "S", "h", "fin7",
     "uout", "S", "h", "mod", "cout", "sout",
 )
 

time: 1050 us -> 1020 us (0.971)
  waiting for transfers between devices: 428 us -> 404 us
    ppermute x60, waiting for transfers between devices: 151 us -> 71.4 us  [swap(): lax.ppermute(value, 'rep', [(peer, peer ^ mask) for peer in range(PEERS)])]
    ppermute x28, waiting for transfers between devices: 102 us -> 154 us  [send(): lax.ppermute(self.pieces[-1], 'fsdp', ring_pairs(self.size, self.step))]
    ppermute x3, waiting for transfers between devices: 33.4 us -> 44.8 us  [send(): self.got = lax.ppermute(self.value, 'fsdp', pairs)]
    all_to_all x1, waiting for transfers between devices: 18.8 us -> 7.57 us  [terms(): lax.all_to_all(found.reshape(group, images, -1), 'fsdp', split_axis=0, co...]
    unnamed x268 -> x260, local copies, waits for them, and re-layouts: 40 us -> 36.3 us
  transfers between devices with their start and end apart: 142 -> 142, of which waited for: 64 -> 75; matrix products, arithmetic and copies ran while one was open for 6% -> 6% of each run, Pallas kernels for 26% -> 30%
where the time goes in v5:
time: 1020 us; the launch traced here: 1010 us
  waiting for transfers between devices  404 us (40%)
  Pallas kernels  361 us (35%)
  starting transfers between devices  120 us (12%)
  local copies, waits for them, and re-layouts  52 us (5%)
  other arithmetic  39.9 us (4%)
  between operations  17.1 us (2%)
  matrix products  11.7 us (1%)
    ppermute x28, waiting for transfers between devices, send(): lax.ppermute(self.pieces[-1], 'fsdp', ring_pairs(self.size, self.step))  154 us
    ppermute x42, waiting for transfers between devices, reach(): lax.ppermute(value, 'fsdp', ring_pairs(self.size, direction))  111 us
    pallas_call x14, Pallas kernels, multiply(): pl.pallas_call(kernel, grid=(columns // width,), in_specs=specs, out_spec...  95.6 us
    ppermute x60, waiting for transfers between devices, swap(): lax.ppermute(value, 'rep', [(peer, peer ^ mask) for peer in range(PEERS)])  71.4 us
    pallas_call x24, Pallas kernels, ring_add(): pl.pallas_call(kernel, grid_spec=pltpu.PrefetchScalarGridSpec(num_scalar_...  59.7 us
    pallas_call x7, Pallas kernels, weight_term(): pl.pallas_call(kernel, grid_spec=pltpu.PrefetchScalarGridSpec(num_scalar_...  58.4 us
    ppermute x3, waiting for transfers between devices, send(): self.got = lax.ppermute(self.value, 'fsdp', pairs)  44.8 us
    ppermute x42, starting transfers between devices, reach(): lax.ppermute(value, 'fsdp', ring_pairs(self.size, direction))  44.3 us
  transfers between devices with their start and end apart: 142, of which 75 were waited for; matrix products, arithmetic and copies ran while one was open for 6% of the time, Pallas kernels for 30%

profile of v5, /device:TPU:0, one launch (start us, length us, event | category | flops | bytes accessed | tf_op | source)
XLA Modules:
  0.0 1005.5 jit_solution(7488234899479764514)
XLA Ops:
  29.1 10.5 %collective-permute-done.4.refs_1_ = bf16[256,2048]{1,0:T(8,128)(2,1)} collective-permute-done((bf16[256,2048]{1,0:T(8,128)(2,1)S(1)}, bf16[256,2048]{1,0:T(8,128)(2,1)}, u32[]{:S(2)}, u32[]{:S(2)}) %collective-permute-start.4) | collective-permute-done | bytes 1048608 | tf_op jit(solution)/shard_map/ppermute | solution.py:656
  43.8 21.5 %collective-permute-done.3 = f32[1,260]{1,0:T(1,128)S(1)} collective-permute-done((f32[1,260]{1,0:T(1,128)S(1)}, f32[1,260]{1,0:T(1,128)S(1)}, u32[]{:S(2)}, u32[]{:S(2)}) %collective-permute-start.3) | collective-permute-done | bytes 1072 | tf_op jit(solution)/shard_map/ppermute | solution.py:774
  70.0 20.5 %collective-permute-done.6 = f32[2,260]{1,0:T(2,128)S(1)} collective-permute-done((f32[2,260]{1,0:T(2,128)S(1)}, f32[2,260]{1,0:T(2,128)S(1)}, u32[]{:S(2)}, u32[]{:S(2)}) %collective-permute-start.6) | collective-permute-done | bytes 2112 | tf_op jit(solution)/shard_map/ppermute | solution.py:774
  106.4 11.8 %collective-permute-done.12.refs_4_ = bf16[256,2048]{1,0:T(8,128)(2,1)} collective-permute-done((bf16[256,2048]{1,0:T(8,128)(2,1)}, bf16[256,2048]{1,0:T(8,128)(2,1)}, u32[]{:S(2)}, u32[]{:S(2)}) %collective-permute-start.12) | collective-permute-done | bytes 1048608 | tf_op jit(solution)/shard_map/ppermute | solution.py:656
  134.9 9.6 collective-permute-done.14.refs_1_
  155.6 18.5 %collective-permute-done.19.refs_6_ = bf16[256,2048]{1,0:T(8,128)(2,1)} collective-permute-done((bf16[256,2048]{1,0:T(8,128)(2,1)S(1)}, bf16[256,2048]{1,0:T(8,128)(2,1)}, u32[]{:S(2)}, u32[]{:S(2)}) %collective-permute-start.19) | collective-permute-done | bytes 1048608 | tf_op jit(solution)/shard_map/ppermute | solution.py:656
  184.6 14.1 %collective-permute-done.22.refs_7_ = bf16[256,2048]{1,0:T(8,128)(2,1)} collective-permute-done((bf16[256,2048]{1,0:T(8,128)(2,1)}, bf16[256,2048]{1,0:T(8,128)(2,1)}, u32[]{:S(2)}, u32[]{:S(2)}) %collective-permute-start.22) | collective-permute-done | bytes 1048608 | tf_op jit(solution)/shard_map/ppermute | solution.py:656
  212.0 10.2 %multiply.63.qkv_ref = bf16[1024,1536]{1,0:T(8,128)(2,1)S(1)} custom-call(bf16[1024,2048]{1,0:T(8,128)(2,1)} %stack_rows.7.refs_0_.left_ref, bf16[2048,1536]{1,0:T(8,128)(2,1)} %get-tuple-element.297.refs_1_.right_ref), custom_call_target="tpu_custom_call" | custom-call | flops 6442450944 | bytes 13631488 | tf_op jit(solution)/shard_map/multiply/pallas_call | solution.py:482
  262.2 15.2 %collective-permute-done.34.refs_2_ = bf16[256,2048]{1,0:T(8,128)(2,1)S(1)} collective-permute-done((bf16[256,2048]{1,0:T(8,128)(2,1)}, bf16[256,2048]{1,0:T(8,128)(2,1)S(1)}, u32[]{:S(2)}, u32[]{:S(2)}) %collective-permute-start.34) | collective-permute-done | bytes 1048608 | tf_op jit(solution)/shard_map/ppermute | solution.py:656
  283.7 18.4 %collective-permute-done.39.refs_3_ = bf16[256,2048]{1,0:T(8,128)(2,1)S(1)} collective-permute-done((bf16[256,2048]{1,0:T(8,128)(2,1)S(1)}, bf16[256,2048]{1,0:T(8,128)(2,1)S(1)}, u32[]{:S(2)}, u32[]{:S(2)}) %collective-permute-start.39) | collective-permute-done | bytes 1048608 | tf_op jit(solution)/shard_map/ppermute | solution.py:656
  308.0 17.3 %collective-permute-done.42.refs_4_ = bf16[256,2048]{1,0:T(8,128)(2,1)} collective-permute-done((bf16[256,2048]{1,0:T(8,128)(2,1)S(1)}, bf16[256,2048]{1,0:T(8,128)(2,1)}, u32[]{:S(2)}, u32[]{:S(2)}) %collective-permute-start.42) | collective-permute-done | bytes 1048608 | tf_op jit(solution)/shard_map/ppermute | solution.py:656
  362.0 16.3 %collective-permute-done.51.refs_6_ = bf16[256,2048]{1,0:T(8,128)(2,1)S(1)} collective-permute-done((bf16[256,2048]{1,0:T(8,128)(2,1)}, bf16[256,2048]{1,0:T(8,128)(2,1)S(1)}, u32[]{:S(2)}, u32[]{:S(2)}) %collective-permute-start.51) | collective-permute-done | bytes 1048608 | tf_op jit(solution)/shard_map/ppermute | solution.py:656
  389.2 12.7 %collective-permute-done.54.refs_7_ = bf16[256,2048]{1,0:T(8,128)(2,1)S(1)} collective-permute-done((bf16[256,2048]{1,0:T(8,128)(2,1)S(1)}, bf16[256,2048]{1,0:T(8,128)(2,1)S(1)}, u32[]{:S(2)}, u32[]{:S(2)}) %collective-permute-start.54) | collective-permute-done | bytes 1048608 | tf_op jit(solution)/shard_map/ppermute | solution.py:656
  422.9 18.1 %multiply.68 = (bf16[1024,2048]{1,0:T(8,128)(2,1)S(1)}, bf16[1024,2048]{1,0:T(8,128)(2,1)}) custom-call(bf16[1024,2048]{1,0:T(8,128)(2,1)} %stack_rows.10.refs_0_.left_ref, bf16[2048,2048]{1,0:T(8,128)(2,1)} %lay_out.6.refs_1_.right_ref), custom_call_target="tpu_custom_call" | custom-call | flops 8589934592 | bytes 16777216 | tf_op jit(solution)/shard_map/multiply/pallas_call | solution.py:482
  454.9 13.0 %multiply.69.refs_0_.left_ref.right_ref = bf16[1024,2048]{1,0:T(8,128)(2,1)S(1)} custom-call(bf16[1024,2048]{1,0:T(8,128)(2,1)} %stack_rows.11.refs_0_.right_ref, bf16[2048,2048]{1,0:T(8,128)(2,1)} %lay_out.7.refs_1_.right_ref, bf16[1024,2048]{1,0:T(8,128)(2,1)} %get-tuple-element.350.refs_2_), custom_call_target="tpu_custom_call" | custom-call | flops 8589934592 | bytes 16777216 | tf_op jit(solution)/shard_map/multiply/pallas_call | solution.py:482
  469.9 7.8 multiply.70
  481.9 8.8 multiply_rest.9
  492.1 13.8 %weight_term.7.refs_0_ = bf16[2048,2048]{1,0:T(8,128)(2,1)} custom-call(s32[1]{0:T(128)} %constant.347.clone.1.chosen_ref, bf16[1024,2048]{1,0:T(8,128)(2,1)S(1)} %copy-done.74, bf16[1024,2048]{1,0:T(8,128)(2,1)} %stack_rows.11.refs_0_.right_ref), custom_call_target="tpu_custom_call" | custom-call | flops 8589934592 | bytes 16777216 | tf_op jit(solution)/shard_map/weight_term/pallas_call | solution.py:507
  505.8 13.7 %weight_term.8.refs_1_ = bf16[2048,2048]{1,0:T(8,128)(2,1)} custom-call(s32[1]{0:T(128)} %constant.347.clone.1.chosen_ref, bf16[1024,2048]{1,0:T(8,128)(2,1)S(1)} %copy-done.11, bf16[1024,2048]{1,0:T(8,128)(2,1)} %copy-done.75), custom_call_target="tpu_custom_call" | custom-call | flops 8589934592 | bytes 16777216 | tf_op jit(solution)/shard_map/weight_term/pallas_call | solution.py:507
  542.7 7.8 multiply.71
  550.5 9.6 collective-permute-done.65.refs_2_
  643.0 17.8 %collective-permute-done.82.refs_2_ = bf16[128,2048]{1,0:T(8,128)(2,1)} collective-permute-done((bf16[128,2048]{1,0:T(8,128)(2,1)}, bf16[128,2048]{1,0:T(8,128)(2,1)}, u32[]{:S(2)}, u32[]{:S(2)}) %collective-permute-start.82) | collective-permute-done | bytes 524320 | tf_op jit(solution)/shard_map/ppermute | solution.py:757
  678.5 8.0 attend_self_back.1.refs_0_.left_ref.right_ref
  700.8 7.6 collective-permute-done.86.refs_2_
  714.9 7.6 multiply_rest.11
  722.5 12.0 %weight_term.12.refs_0_ = bf16[2048,2048]{1,0:T(8,128)(2,1)} custom-call(s32[1]{0:T(128)} %constant.347.clone.1.chosen_ref, bf16[1024,2048]{1,0:T(8,128)(2,1)} %stack_rows.7.refs_0_.left_ref, bf16[1024,1536]{1,0:T(8,128)(2,1)S(1)} %copy-done.22), custom_call_target="tpu_custom_call" | custom-call | flops 6442450944 | bytes 13631488 | tf_op jit(solution)/shard_map/weight_term/pallas_call | solution.py:507
  776.6 7.9 multiply_rest.12
  785.8 21.8 %collective-permute-done.106.refs_3_ = bf16[128,2048]{1,0:T(8,128)(2,1)S(1)} collective-permute-done((bf16[128,2048]{1,0:T(8,128)(2,1)S(1)}, bf16[128,2048]{1,0:T(8,128)(2,1)S(1)}, u32[]{:S(2)}, u32[]{:S(2)}) %collective-permute-start.106) | collective-permute-done | bytes 524320 | tf_op jit(solution)/shard_map/ppermute | solution.py:757
  824.1 18.3 %collective-permute-done.109.refs_2_ = bf16[128,2048]{1,0:T(8,128)(2,1)S(1)} collective-permute-done((bf16[128,2048]{1,0:T(8,128)(2,1)S(1)}, bf16[128,2048]{1,0:T(8,128)(2,1)S(1)}, u32[]{:S(2)}, u32[]{:S(2)}) %collective-permute-start.109) | collective-permute-done | bytes 524320 | tf_op jit(solution)/shard_map/ppermute | solution.py:757
  923.3 10.6 %collective-permute-done.129 = bf16[8,14336]{1,0:T(8,128)(2,1)} collective-permute-done((bf16[8,14336]{1,0:T(8,128)(2,1)}, bf16[8,14336]{1,0:T(8,128)(2,1)}, u32[]{:S(2)}, u32[]{:S(2)}) %collective-permute-start.129) | collective-permute-done | bytes 229408 | tf_op jit(solution)/shard_map/ppermute | solution.py:800
  949.5 15.0 %collective-permute-done.136.refs_2_ = bf16[256,2048]{1,0:T(8,128)(2,1)S(1)} collective-permute-done((bf16[256,2048]{1,0:T(8,128)(2,1)S(1)}, bf16[256,2048]{1,0:T(8,128)(2,1)S(1)}, u32[]{:S(2)}, u32[]{:S(2)}) %collective-permute-start.136) | collective-permute-done | bytes 1048608 | tf_op jit(solution)/shard_map/ppermute | solution.py:359
  976.7 7.9 fusion.23
  (678 shorter events, 564.6 us)
Async XLA Ops:
  106.0 807.3 %all-gather.4.cloned.1.call-start = ((), (), s32[]{:S(2)}) async-start(), calls=%async_computation.1 | async-start | bytes 5242880 | tf_op jit(solution)/shard_map/all_gather | solution.py:1160
  205.6 32.0 %collective-permute-start.26 = (bf16[256,2048]{1,0:T(8,128)(2,1)S(1)}, bf16[256,2048]{1,0:T(8,128)(2,1)}, u32[]{:S(2)}, u32[]{:S(2)}) collective-permute-start(bf16[256,2048]{1,0:T(8,128)(2,1)S(1)} %copy-done.12), channel_id=1, source_target_pairs={{0,2},{2,4},{4,6},{6,7},{7,5},{5,3},{3,1},{1,0},{8,10},{10,12},{12... | collective-permute-start | bytes 3145736 | tf_op jit(solution)/shard_map/ppermute | solution.py:656
  206.4 31.2 %collective-permute-start.27 = (bf16[256,2048]{1,0:T(8,128)(2,1)S(1)}, bf16[256,2048]{1,0:T(8,128)(2,1)S(1)}, u32[]{:S(2)}, u32[]{:S(2)}) collective-permute-start(bf16[256,2048]{1,0:T(8,128)(2,1)S(1)} %dynamic-slice_bitcast_fusion.refs_0_), channel_id=1, source_target_pairs={{0,1},{2,0},{4,2},{6,4},{7,6},{5,7},{3,5},{1,3},{8,9},{10,8},{12,1... | collective-permute-start | bytes 3145736 | tf_op jit(solution)/shard_map/ppermute | solution.py:656
  410.9 32.1 %collective-permute-start.58 = (bf16[256,2048]{1,0:T(8,128)(2,1)S(1)}, bf16[256,2048]{1,0:T(8,128)(2,1)S(1)}, u32[]{:S(2)}, u32[]{:S(2)}) collective-permute-start(bf16[256,2048]{1,0:T(8,128)(2,1)S(1)} %copy-done.20), channel_id=1, source_target_pairs={{0,16},{8,24},{16,0},{24,8},{1,17},{9,25},{17,1},{25,9},{2,18},{10... | collective-permute-start | bytes 3145736 | tf_op jit(solution)/shard_map/ppermute | solution.py:359
  478.3 56.0 %collective-permute-start.68 = (bf16[1024,512]{1,0:T(8,128)(2,1)}, bf16[1024,512]{1,0:T(8,128)(2,1)S(1)}, u32[]{:S(2)}, u32[]{:S(2)}) collective-permute-start(bf16[1024,512]{1,0:T(8,128)(2,1)} %get-tuple-element.368.refs_0_.left_ref), channel_id=1, source_target_pairs={{0,16},{8,24},{16,0},{24,8},{1,17},{9,25},{17,1},{25,9},{2,18},{10... | collective-permute-start | bytes 3145736 | tf_op jit(solution)/shard_map/ppermute | solution.py:359
  490.7 35.6 %collective-permute-start.63 = (bf16[256,2048]{1,0:T(8,128)(2,1)}, bf16[256,2048]{1,0:T(8,128)(2,1)}, u32[]{:S(2)}, u32[]{:S(2)}) collective-permute-start(bf16[256,2048]{1,0:T(8,128)(2,1)} %get-tuple-element.361), channel_id=1, source_target_pairs={{0,16},{8,24},{16,0},{24,8},{1,17},{9,25},{17,1},{25,9},{2,18},{10... | collective-permute-start | bytes 3145736 | tf_op jit(solution)/shard_map/ppermute | solution.py:359
  536.8 27.2 %collective-permute-start.64 = (bf16[256,2048]{1,0:T(8,128)(2,1)S(1)}, bf16[256,2048]{1,0:T(8,128)(2,1)S(1)}, u32[]{:S(2)}, u32[]{:S(2)}) collective-permute-start(bf16[256,2048]{1,0:T(8,128)(2,1)S(1)} %get-tuple-element.524.refs_0_), channel_id=1, source_target_pairs={{0,16},{8,24},{16,0},{24,8},{1,17},{9,25},{17,1},{25,9},{2,18},{10... | collective-permute-start | bytes 3145736 | tf_op jit(solution)/shard_map/ppermute | solution.py:359
  594.6 27.3 %collective-permute-start.77 = (bf16[256,2048]{1,0:T(8,128)(2,1)}, bf16[256,2048]{1,0:T(8,128)(2,1)}, u32[]{:S(2)}, u32[]{:S(2)}) collective-permute-start(bf16[256,2048]{1,0:T(8,128)(2,1)} %get-tuple-element.388), channel_id=1, source_target_pairs={{0,2},{2,4},{4,6},{6,7},{7,5},{5,3},{3,1},{1,0},{8,10},{10,12},{12... | collective-permute-start | bytes 3145736 | tf_op jit(solution)/shard_map/ppermute | solution.py:757
  601.4 26.7 %collective-permute-start.76 = (bf16[256,2048]{1,0:T(8,128)(2,1)}, bf16[256,2048]{1,0:T(8,128)(2,1)}, u32[]{:S(2)}, u32[]{:S(2)}) collective-permute-start(bf16[256,2048]{1,0:T(8,128)(2,1)} %get-tuple-element.392), channel_id=1, source_target_pairs={{0,16},{8,24},{16,0},{24,8},{1,17},{9,25},{17,1},{25,9},{2,18},{10... | collective-permute-start | bytes 3145736 | tf_op jit(solution)/shard_map/ppermute | solution.py:359
  626.1 38.2 %collective-permute-start.80 = (bf16[256,2048]{1,0:T(8,128)(2,1)}, bf16[256,2048]{1,0:T(8,128)(2,1)}, u32[]{:S(2)}, u32[]{:S(2)}) collective-permute-start(bf16[256,2048]{1,0:T(8,128)(2,1)} %get-tuple-element.401), channel_id=1, source_target_pairs={{0,2},{2,4},{4,6},{6,7},{7,5},{5,3},{3,1},{1,0},{8,10},{10,12},{12... | collective-permute-start | bytes 3145736 | tf_op jit(solution)/shard_map/ppermute | solution.py:757
  627.8 36.6 %collective-permute-start.81 = (bf16[256,2048]{1,0:T(8,128)(2,1)}, bf16[256,2048]{1,0:T(8,128)(2,1)}, u32[]{:S(2)}, u32[]{:S(2)}) collective-permute-start(bf16[256,2048]{1,0:T(8,128)(2,1)} %get-tuple-element.402), channel_id=1, source_target_pairs={{0,1},{2,0},{4,2},{6,4},{7,6},{5,7},{3,5},{1,3},{8,9},{10,8},{12,1... | collective-permute-start | bytes 3145736 | tf_op jit(solution)/shard_map/ppermute | solution.py:757
  634.2 33.1 %collective-permute-start.79 = (bf16[256,2048]{1,0:T(8,128)(2,1)S(1)}, bf16[256,2048]{1,0:T(8,128)(2,1)S(1)}, u32[]{:S(2)}, u32[]{:S(2)}) collective-permute-start(bf16[256,2048]{1,0:T(8,128)(2,1)S(1)} %fusion.20.refs_0_), channel_id=1, source_target_pairs={{0,16},{8,24},{16,0},{24,8},{1,17},{9,25},{17,1},{25,9},{2,18},{10... | collective-permute-start | bytes 3145736 | tf_op jit(solution)/shard_map/ppermute | solution.py:359
  667.9 27.8 %collective-permute-start.88 = (bf16[256,2048]{1,0:T(8,128)(2,1)S(1)}, bf16[256,2048]{1,0:T(8,128)(2,1)S(1)}, u32[]{:S(2)}, u32[]{:S(2)}) collective-permute-start(bf16[256,2048]{1,0:T(8,128)(2,1)S(1)} %get-tuple-element.413), channel_id=1, source_target_pairs={{0,2},{2,4},{4,6},{6,7},{7,5},{5,3},{3,1},{1,0},{8,10},{10,12},{12... | collective-permute-start | bytes 3145736 | tf_op jit(solution)/shard_map/ppermute | solution.py:757
  669.2 27.2 %collective-permute-start.89 = (bf16[256,2048]{1,0:T(8,128)(2,1)S(1)}, bf16[256,2048]{1,0:T(8,128)(2,1)S(1)}, u32[]{:S(2)}, u32[]{:S(2)}) collective-permute-start(bf16[256,2048]{1,0:T(8,128)(2,1)S(1)} %get-tuple-element.414), channel_id=1, source_target_pairs={{0,1},{2,0},{4,2},{6,4},{7,6},{5,7},{3,5},{1,3},{8,9},{10,8},{12,1... | collective-permute-start | bytes 3145736 | tf_op jit(solution)/shard_map/ppermute | solution.py:757
  696.4 38.1 %collective-permute-start.98 = (bf16[1024,512]{1,0:T(8,128)(2,1)}, bf16[1024,512]{1,0:T(8,128)(2,1)}, u32[]{:S(2)}, u32[]{:S(2)}) collective-permute-start(bf16[1024,512]{1,0:T(8,128)(2,1)} %get-tuple-element.432.refs_0_.left_ref), channel_id=1, source_target_pairs={{0,16},{8,24},{16,0},{24,8},{1,17},{9,25},{17,1},{25,9},{2,18},{10... | collective-permute-start | bytes 3145736 | tf_op jit(solution)/shard_map/ppermute | solution.py:359
  708.4 27.1 %collective-permute-start.97 = (bf16[1024,512]{1,0:T(8,128)(2,1)}, bf16[1024,512]{1,0:T(8,128)(2,1)}, u32[]{:S(2)}, u32[]{:S(2)}) collective-permute-start(bf16[1024,512]{1,0:T(8,128)(2,1)} %get-tuple-element.432.refs_0_.left_ref), channel_id=1, source_target_pairs={{0,8},{8,0},{16,24},{24,16},{1,9},{9,1},{17,25},{25,17},{2,10},{10... | collective-permute-start | bytes 3145736 | tf_op jit(solution)/shard_map/ppermute | solution.py:359
  734.5 26.9 %collective-permute-start.92 = (bf16[256,2048]{1,0:T(8,128)(2,1)}, bf16[256,2048]{1,0:T(8,128)(2,1)}, u32[]{:S(2)}, u32[]{:S(2)}) collective-permute-start(bf16[256,2048]{1,0:T(8,128)(2,1)} %get-tuple-element.431), channel_id=1, source_target_pairs={{0,16},{8,24},{16,0},{24,8},{1,17},{9,25},{17,1},{25,9},{2,18},{10... | collective-permute-start | bytes 3145736 | tf_op jit(solution)/shard_map/ppermute | solution.py:359
  735.5 29.8 %collective-permute-start.100 = (bf16[256,2048]{1,0:T(8,128)(2,1)}, bf16[256,2048]{1,0:T(8,128)(2,1)S(1)}, u32[]{:S(2)}, u32[]{:S(2)}) collective-permute-start(bf16[256,2048]{1,0:T(8,128)(2,1)} %copy-done.61), channel_id=1, source_target_pairs={{0,8},{8,0},{16,24},{24,16},{1,9},{9,1},{17,25},{25,17},{2,10},{10... | collective-permute-start | bytes 3145736 | tf_op jit(solution)/shard_map/ppermute | solution.py:359
  735.6 30.2 %collective-permute-start.101 = (bf16[256,2048]{1,0:T(8,128)(2,1)}, bf16[256,2048]{1,0:T(8,128)(2,1)S(1)}, u32[]{:S(2)}, u32[]{:S(2)}) collective-permute-start(bf16[256,2048]{1,0:T(8,128)(2,1)} %copy-done.60), channel_id=1, source_target_pairs={{0,8},{8,0},{16,24},{24,16},{1,9},{9,1},{17,25},{25,17},{2,10},{10... | collective-permute-start | bytes 3145736 | tf_op jit(solution)/shard_map/ppermute | solution.py:359
  759.0 53.3 %collective-permute-start.111 = (bf16[256,2048]{1,0:T(8,128)(2,1)S(1)}, bf16[256,2048]{1,0:T(8,128)(2,1)S(1)}, u32[]{:S(2)}, u32[]{:S(2)}) collective-permute-start(bf16[256,2048]{1,0:T(8,128)(2,1)S(1)} %get-tuple-element.441), channel_id=1, source_target_pairs={{0,2},{2,4},{4,6},{6,7},{7,5},{5,3},{3,1},{1,0},{8,10},{10,12},{12... | collective-permute-start | bytes 3145736 | tf_op jit(solution)/shard_map/ppermute | solution.py:757
  761.5 50.8 %collective-permute-start.112 = (bf16[256,2048]{1,0:T(8,128)(2,1)S(1)}, bf16[256,2048]{1,0:T(8,128)(2,1)S(1)}, u32[]{:S(2)}, u32[]{:S(2)}) collective-permute-start(bf16[256,2048]{1,0:T(8,128)(2,1)S(1)} %get-tuple-element.442), channel_id=1, source_target_pairs={{0,1},{2,0},{4,2},{6,4},{7,6},{5,7},{3,5},{1,3},{8,9},{10,8},{12,1... | collective-permute-start | bytes 3145736 | tf_op jit(solution)/shard_map/ppermute | solution.py:757
  765.2 45.1 %collective-permute-start.103 = (bf16[128,2048]{1,0:T(8,128)(2,1)S(1)}, bf16[128,2048]{1,0:T(8,128)(2,1)S(1)}, u32[]{:S(2)}, u32[]{:S(2)}) collective-permute-start(bf16[128,2048]{1,0:T(8,128)(2,1)S(1)} %get-tuple-element.445), channel_id=1, source_target_pairs={{0,2},{2,4},{4,6},{6,7},{7,5},{5,3},{3,1},{1,0},{8,10},{10,12},{12... | collective-permute-start | bytes 1572872 | tf_op jit(solution)/shard_map/ppermute | solution.py:757
  765.9 44.4 %collective-permute-start.104 = (bf16[128,2048]{1,0:T(8,128)(2,1)S(1)}, bf16[128,2048]{1,0:T(8,128)(2,1)S(1)}, u32[]{:S(2)}, u32[]{:S(2)}) collective-permute-start(bf16[128,2048]{1,0:T(8,128)(2,1)S(1)} %get-tuple-element.446), channel_id=1, source_target_pairs={{0,1},{2,0},{4,2},{6,4},{7,6},{5,7},{3,5},{1,3},{8,9},{10,8},{12,1... | collective-permute-start | bytes 1572872 | tf_op jit(solution)/shard_map/ppermute | solution.py:757
  772.8 34.8 %collective-permute-start.106 = (bf16[128,2048]{1,0:T(8,128)(2,1)S(1)}, bf16[128,2048]{1,0:T(8,128)(2,1)S(1)}, u32[]{:S(2)}, u32[]{:S(2)}) collective-permute-start(bf16[128,2048]{1,0:T(8,128)(2,1)S(1)} %get-tuple-element.438), channel_id=1, source_target_pairs={{0,1},{2,0},{4,2},{6,4},{7,6},{5,7},{3,5},{1,3},{8,9},{10,8},{12,1... | collective-permute-start | bytes 1572872 | tf_op jit(solution)/shard_map/ppermute | solution.py:757
  816.6 121.8 %all-gather.6.cloned.1.call-start = ((), (), s32[]{:S(2)}) async-start(), calls=%async_computation.2 | async-start | bytes 5242880 | tf_op jit(solution)/shard_map/all_gather | solution.py:1160
  817.3 167.3 %all-gather.8.cloned.1.call-start = ((), (), s32[]{:S(2)}) async-start(), calls=%async_computation.3 | async-start | bytes 5242880 | tf_op jit(solution)/shard_map/all_gather | solution.py:1160
  817.4 42.2 %collective-permute-start.102 = (bf16[256,2048]{1,0:T(8,128)(2,1)}, bf16[256,2048]{1,0:T(8,128)(2,1)S(1)}, u32[]{:S(2)}, u32[]{:S(2)}) collective-permute-start(bf16[256,2048]{1,0:T(8,128)(2,1)} %copy-done.62), channel_id=1, source_target_pairs={{0,16},{8,24},{16,0},{24,8},{1,17},{9,25},{17,1},{25,9},{2,18},{10... | collective-permute-start | bytes 3145736 | tf_op jit(solution)/shard_map/ppermute | solution.py:359
  819.9 28.0 %collective-permute-start.107 = (bf16[128,2048]{1,0:T(8,128)(2,1)S(1)}, bf16[128,2048]{1,0:T(8,128)(2,1)S(1)}, u32[]{:S(2)}, u32[]{:S(2)}) collective-permute-start(bf16[128,2048]{1,0:T(8,128)(2,1)S(1)} %copy-done.68), channel_id=1, source_target_pairs={{0,2},{2,4},{4,6},{6,7},{7,5},{5,3},{3,1},{1,0},{8,10},{10,12},{12... | collective-permute-start | bytes 1572872 | tf_op jit(solution)/shard_map/ppermute | solution.py:757
  820.9 27.0 %collective-permute-start.108 = (bf16[128,2048]{1,0:T(8,128)(2,1)S(1)}, bf16[128,2048]{1,0:T(8,128)(2,1)S(1)}, u32[]{:S(2)}, u32[]{:S(2)}) collective-permute-start(bf16[128,2048]{1,0:T(8,128)(2,1)S(1)} %copy-done.66), channel_id=1, source_target_pairs={{0,1},{2,0},{4,2},{6,4},{7,6},{5,7},{3,5},{1,3},{8,9},{10,8},{12,1... | collective-permute-start | bytes 1572872 | tf_op jit(solution)/shard_map/ppermute | solution.py:757
  905.4 31.0 %collective-permute-start.125 = (bf16[128,2048]{1,0:T(8,128)(2,1)}, bf16[128,2048]{1,0:T(8,128)(2,1)}, u32[]{:S(2)}, u32[]{:S(2)}) collective-permute-start(bf16[128,2048]{1,0:T(8,128)(2,1)} %get-tuple-element.492), channel_id=1, source_target_pairs={{0,16},{8,24},{16,0},{24,8},{1,17},{9,25},{17,1},{25,9},{2,18},{10... | collective-permute-start | bytes 1572872 | tf_op jit(solution)/shard_map/ppermute | solution.py:359
  964.6 27.5 %collective-permute-start.137 = (bf16[256,2048]{1,0:T(8,128)(2,1)S(1)}, bf16[256,2048]{1,0:T(8,128)(2,1)S(1)}, u32[]{:S(2)}, u32[]{:S(2)}) collective-permute-start(bf16[256,2048]{1,0:T(8,128)(2,1)S(1)} %collective-permute-done.136.refs_2_), channel_id=1, source_target_pairs={{0,8},{8,0},{16,24},{24,16},{1,9},{9,1},{17,25},{25,17},{2,10},{10... | collective-permute-start | bytes 3145736 | tf_op jit(solution)/shard_map/ppermute | solution.py:359
  964.6 27.5 %collective-permute-start.135 = (bf16[256,2048]{1,0:T(8,128)(2,1)S(1)}, bf16[256,2048]{1,0:T(8,128)(2,1)}, u32[]{:S(2)}, u32[]{:S(2)}) collective-permute-start(bf16[256,2048]{1,0:T(8,128)(2,1)S(1)} %constant_dynamic-update-slice_fusion.7.refs_0_), channel_id=1, source_target_pairs={{0,8},{8,0},{16,24},{24,16},{1,9},{9,1},{17,25},{25,17},{2,10},{10... | collective-permute-start | bytes 3145736 | tf_op jit(solution)/shard_map/ppermute | solution.py:359
  (237 other events, 3097.5 us)
Sparse Core Ops, SparseCore 0:
  816.7 47.7 all-gather.3
  866.6 31.8 all-gather.5
  900.6 47.0 all-gather.7

commit v6 on v5

--- a/solution.py
+++ b/solution.py
@@ -1276,8 +1276,7 @@
     def self_step():
         if v.self_ring.reach():
             own = jnp.concatenate(v.self_ring.sums, axis=0)
-            far = swap(own, 2)
-            v.self_found = [own, swap(own, 1), far, swap(far, 1)]
+            v.self_found = [own, swap(own, 1), swap(own, 2)]
 
     def fin5():
         def finish(crossed):
@@ -1371,12 +1370,13 @@
         ]
 
     def self_out():
+        own, near, far = v.self_found
+        far = order.hold(far)
+        diagonal = swap(far, 1)
         v.qkv_grad, v.out_grad = [
             order.run(
-                lambda last: spread_peers(
-                    v.self_found[:-1] + [last], rank, start, count, part
-                ),
-                v.self_found[-1],
+                lambda last: spread_peers([own, near, far, last], rank, start, count, part),
+                diagonal,
             )
             for start, count in ((0, 3), (3, 1))
         ]

time: 1020 us -> 999 us (0.979)
    ppermute x42, waiting for transfers between devices: 111 us -> 122 us  [reach(): lax.ppermute(value, 'fsdp', ring_pairs(self.size, direction))]
    unnamed x260 -> x266, local copies, waits for them, and re-layouts: 36.3 us -> 36.1 us
  transfers between devices with their start and end apart: 142 -> 142, of which waited for: 75 -> 80; matrix products, arithmetic and copies ran while one was open for 6% -> 6% of each run, Pallas kernels for 30% -> 30%
where the time goes in v6:
time: 999 us; the launch traced here: 988 us
  waiting for transfers between devices  396 us (40%)
  Pallas kernels  355 us (36%)
  starting transfers between devices  120 us (12%)
  local copies, waits for them, and re-layouts  49.3 us (5%)
  other arithmetic  39.2 us (4%)
  between operations  17.1 us (2%)
  matrix products  10.6 us (1%)
    ppermute x28, waiting for transfers between devices, send(): lax.ppermute(self.pieces[-1], 'fsdp', ring_pairs(self.size, self.step))  154 us
    ppermute x42, waiting for transfers between devices, reach(): lax.ppermute(value, 'fsdp', ring_pairs(self.size, direction))  122 us
    pallas_call x14, Pallas kernels, multiply(): pl.pallas_call(kernel, grid=(columns // width,), in_specs=specs, out_spec...  94.9 us
    ppermute x60, waiting for transfers between devices, swap(): lax.ppermute(value, 'rep', [(peer, peer ^ mask) for peer in range(PEERS)])  61.9 us
    pallas_call x7, Pallas kernels, weight_term(): pl.pallas_call(kernel, grid_spec=pltpu.PrefetchScalarGridSpec(num_scalar_...  58.4 us
    pallas_call x24, Pallas kernels, ring_add(): pl.pallas_call(kernel, grid_spec=pltpu.PrefetchScalarGridSpec(num_scalar_...  56.6 us
    ppermute x3, waiting for transfers between devices, send(): self.got = lax.ppermute(self.value, 'fsdp', pairs)  44.8 us
    ppermute x42, starting transfers between devices, reach(): lax.ppermute(value, 'fsdp', ring_pairs(self.size, direction))  43.2 us
  transfers between devices with their start and end apart: 142, of which 80 were waited for; matrix products, arithmetic and copies ran while one was open for 6% of the time, Pallas kernels for 30%

profile of v6, /device:TPU:0, one launch (start us, length us, event | category | flops | bytes accessed | tf_op | source)
XLA Modules:
  0.0 987.6 jit_solution(11429959104730497402)
XLA Ops:
  29.1 10.5 %collective-permute-done.4.refs_1_ = bf16[256,2048]{1,0:T(8,128)(2,1)} collective-permute-done((bf16[256,2048]{1,0:T(8,128)(2,1)S(1)}, bf16[256,2048]{1,0:T(8,128)(2,1)}, u32[]{:S(2)}, u32[]{:S(2)}) %collective-permute-start.4) | collective-permute-done | bytes 1048608 | tf_op jit(solution)/shard_map/ppermute | solution.py:656
  43.8 21.5 %collective-permute-done.3 = f32[1,260]{1,0:T(1,128)S(1)} collective-permute-done((f32[1,260]{1,0:T(1,128)S(1)}, f32[1,260]{1,0:T(1,128)S(1)}, u32[]{:S(2)}, u32[]{:S(2)}) %collective-permute-start.3) | collective-permute-done | bytes 1072 | tf_op jit(solution)/shard_map/ppermute | solution.py:774
  70.0 20.5 %collective-permute-done.6 = f32[2,260]{1,0:T(2,128)S(1)} collective-permute-done((f32[2,260]{1,0:T(2,128)S(1)}, f32[2,260]{1,0:T(2,128)S(1)}, u32[]{:S(2)}, u32[]{:S(2)}) %collective-permute-start.6) | collective-permute-done | bytes 2112 | tf_op jit(solution)/shard_map/ppermute | solution.py:774
  106.4 11.8 %collective-permute-done.12.refs_4_ = bf16[256,2048]{1,0:T(8,128)(2,1)} collective-permute-done((bf16[256,2048]{1,0:T(8,128)(2,1)}, bf16[256,2048]{1,0:T(8,128)(2,1)}, u32[]{:S(2)}, u32[]{:S(2)}) %collective-permute-start.12) | collective-permute-done | bytes 1048608 | tf_op jit(solution)/shard_map/ppermute | solution.py:656
  119.8 7.6 all-to-all-done
  134.8 9.6 collective-permute-done.14.refs_1_
  155.6 18.5 %collective-permute-done.19.refs_6_ = bf16[256,2048]{1,0:T(8,128)(2,1)} collective-permute-done((bf16[256,2048]{1,0:T(8,128)(2,1)S(1)}, bf16[256,2048]{1,0:T(8,128)(2,1)}, u32[]{:S(2)}, u32[]{:S(2)}) %collective-permute-start.19) | collective-permute-done | bytes 1048608 | tf_op jit(solution)/shard_map/ppermute | solution.py:656
  184.6 14.1 %collective-permute-done.22.refs_7_ = bf16[256,2048]{1,0:T(8,128)(2,1)} collective-permute-done((bf16[256,2048]{1,0:T(8,128)(2,1)}, bf16[256,2048]{1,0:T(8,128)(2,1)}, u32[]{:S(2)}, u32[]{:S(2)}) %collective-permute-start.22) | collective-permute-done | bytes 1048608 | tf_op jit(solution)/shard_map/ppermute | solution.py:656
  212.0 10.2 %multiply.63.qkv_ref = bf16[1024,1536]{1,0:T(8,128)(2,1)S(1)} custom-call(bf16[1024,2048]{1,0:T(8,128)(2,1)} %stack_rows.7.refs_0_.left_ref, bf16[2048,1536]{1,0:T(8,128)(2,1)} %get-tuple-element.298.refs_1_.right_ref), custom_call_target="tpu_custom_call" | custom-call | flops 6442450944 | bytes 13631488 | tf_op jit(solution)/shard_map/multiply/pallas_call | solution.py:482
  262.2 15.2 %collective-permute-done.34.refs_2_ = bf16[256,2048]{1,0:T(8,128)(2,1)S(1)} collective-permute-done((bf16[256,2048]{1,0:T(8,128)(2,1)}, bf16[256,2048]{1,0:T(8,128)(2,1)S(1)}, u32[]{:S(2)}, u32[]{:S(2)}) %collective-permute-start.34) | collective-permute-done | bytes 1048608 | tf_op jit(solution)/shard_map/ppermute | solution.py:656
  283.7 18.4 %collective-permute-done.39.refs_3_ = bf16[256,2048]{1,0:T(8,128)(2,1)S(1)} collective-permute-done((bf16[256,2048]{1,0:T(8,128)(2,1)S(1)}, bf16[256,2048]{1,0:T(8,128)(2,1)S(1)}, u32[]{:S(2)}, u32[]{:S(2)}) %collective-permute-start.39) | collective-permute-done | bytes 1048608 | tf_op jit(solution)/shard_map/ppermute | solution.py:656
  308.0 17.3 %collective-permute-done.42.refs_4_ = bf16[256,2048]{1,0:T(8,128)(2,1)} collective-permute-done((bf16[256,2048]{1,0:T(8,128)(2,1)S(1)}, bf16[256,2048]{1,0:T(8,128)(2,1)}, u32[]{:S(2)}, u32[]{:S(2)}) %collective-permute-start.42) | collective-permute-done | bytes 1048608 | tf_op jit(solution)/shard_map/ppermute | solution.py:656
  362.0 16.3 %collective-permute-done.51.refs_6_ = bf16[256,2048]{1,0:T(8,128)(2,1)S(1)} collective-permute-done((bf16[256,2048]{1,0:T(8,128)(2,1)}, bf16[256,2048]{1,0:T(8,128)(2,1)S(1)}, u32[]{:S(2)}, u32[]{:S(2)}) %collective-permute-start.51) | collective-permute-done | bytes 1048608 | tf_op jit(solution)/shard_map/ppermute | solution.py:656
  389.2 12.7 %collective-permute-done.54.refs_7_ = bf16[256,2048]{1,0:T(8,128)(2,1)S(1)} collective-permute-done((bf16[256,2048]{1,0:T(8,128)(2,1)S(1)}, bf16[256,2048]{1,0:T(8,128)(2,1)S(1)}, u32[]{:S(2)}, u32[]{:S(2)}) %collective-permute-start.54) | collective-permute-done | bytes 1048608 | tf_op jit(solution)/shard_map/ppermute | solution.py:656
  422.9 18.1 %multiply.68 = (bf16[1024,2048]{1,0:T(8,128)(2,1)S(1)}, bf16[1024,2048]{1,0:T(8,128)(2,1)}) custom-call(bf16[1024,2048]{1,0:T(8,128)(2,1)} %stack_rows.10.refs_0_.left_ref, bf16[2048,2048]{1,0:T(8,128)(2,1)} %lay_out.6.refs_1_.right_ref), custom_call_target="tpu_custom_call" | custom-call | flops 8589934592 | bytes 16777216 | tf_op jit(solution)/shard_map/multiply/pallas_call | solution.py:482
  454.9 13.0 %multiply.69.refs_0_.left_ref.right_ref = bf16[1024,2048]{1,0:T(8,128)(2,1)S(1)} custom-call(bf16[1024,2048]{1,0:T(8,128)(2,1)} %stack_rows.11.refs_0_.right_ref, bf16[2048,2048]{1,0:T(8,128)(2,1)} %lay_out.7.refs_1_.right_ref, bf16[1024,2048]{1,0:T(8,128)(2,1)} %get-tuple-element.351.refs_2_), custom_call_target="tpu_custom_call" | custom-call | flops 8589934592 | bytes 16777216 | tf_op jit(solution)/shard_map/multiply/pallas_call | solution.py:482
  469.9 7.8 multiply.70
  482.0 8.7 multiply_rest.9
  492.0 13.8 %weight_term.7.refs_0_ = bf16[2048,2048]{1,0:T(8,128)(2,1)} custom-call(s32[1]{0:T(128)} %constant.347.clone.1.chosen_ref, bf16[1024,2048]{1,0:T(8,128)(2,1)S(1)} %copy-done.76, bf16[1024,2048]{1,0:T(8,128)(2,1)} %stack_rows.11.refs_0_.right_ref), custom_call_target="tpu_custom_call" | custom-call | flops 8589934592 | bytes 16777216 | tf_op jit(solution)/shard_map/weight_term/pallas_call | solution.py:507
  505.9 13.7 %weight_term.8.refs_1_ = bf16[2048,2048]{1,0:T(8,128)(2,1)} custom-call(s32[1]{0:T(128)} %constant.347.clone.1.chosen_ref, bf16[1024,2048]{1,0:T(8,128)(2,1)S(1)} %copy-done.11, bf16[1024,2048]{1,0:T(8,128)(2,1)} %copy-done.77), custom_call_target="tpu_custom_call" | custom-call | flops 8589934592 | bytes 16777216 | tf_op jit(solution)/shard_map/weight_term/pallas_call | solution.py:507
  542.7 7.8 multiply.71
  550.5 9.6 collective-permute-done.65.refs_2_
  643.8 17.0 %collective-permute-done.82.refs_2_ = bf16[128,2048]{1,0:T(8,128)(2,1)} collective-permute-done((bf16[128,2048]{1,0:T(8,128)(2,1)}, bf16[128,2048]{1,0:T(8,128)(2,1)}, u32[]{:S(2)}, u32[]{:S(2)}) %collective-permute-start.82) | collective-permute-done | bytes 524320 | tf_op jit(solution)/shard_map/ppermute | solution.py:757
  678.5 8.1 attend_self_back.1.refs_0_.left_ref.right_ref
  686.6 7.2 multiply.76
  700.7 7.6 collective-permute-done.86.refs_2_
  714.9 7.6 multiply_rest.11
  722.5 12.0 %weight_term.12.refs_0_ = bf16[2048,2048]{1,0:T(8,128)(2,1)} custom-call(s32[1]{0:T(128)} %constant.347.clone.1.chosen_ref, bf16[1024,2048]{1,0:T(8,128)(2,1)} %stack_rows.7.refs_0_.left_ref, bf16[1024,1536]{1,0:T(8,128)(2,1)S(1)} %copy-done.22), custom_call_target="tpu_custom_call" | custom-call | flops 6442450944 | bytes 13631488 | tf_op jit(solution)/shard_map/weight_term/pallas_call | solution.py:507
  776.6 7.9 multiply_rest.12
  785.8 21.8 %collective-permute-done.106.refs_3_ = bf16[128,2048]{1,0:T(8,128)(2,1)S(1)} collective-permute-done((bf16[128,2048]{1,0:T(8,128)(2,1)S(1)}, bf16[128,2048]{1,0:T(8,128)(2,1)S(1)}, u32[]{:S(2)}, u32[]{:S(2)}) %collective-permute-start.106) | collective-permute-done | bytes 524320 | tf_op jit(solution)/shard_map/ppermute | solution.py:757
  824.0 18.3 %collective-permute-done.109.refs_2_ = bf16[128,2048]{1,0:T(8,128)(2,1)S(1)} collective-permute-done((bf16[128,2048]{1,0:T(8,128)(2,1)S(1)}, bf16[128,2048]{1,0:T(8,128)(2,1)S(1)}, u32[]{:S(2)}, u32[]{:S(2)}) %collective-permute-start.109) | collective-permute-done | bytes 524320 | tf_op jit(solution)/shard_map/ppermute | solution.py:757
  851.6 8.0 collective-permute-done.102
  (684 shorter events, 558.1 us)
Async XLA Ops:
  13.4 26.2 %collective-permute-start.4 = (bf16[256,2048]{1,0:T(8,128)(2,1)S(1)}, bf16[256,2048]{1,0:T(8,128)(2,1)}, u32[]{:S(2)}, u32[]{:S(2)}) collective-permute-start(bf16[256,2048]{1,0:T(8,128)(2,1)S(1)} %copy-done.14), channel_id=1, source_target_pairs={{0,2},{2,4},{4,6},{6,7},{7,5},{5,3},{3,1},{1,0},{8,10},{10,12},{12... | collective-permute-start | bytes 3145736 | tf_op jit(solution)/shard_map/ppermute | solution.py:656
  106.0 811.6 %all-gather.4.cloned.1.call-start = ((), (), s32[]{:S(2)}) async-start(), calls=%async_computation.1 | async-start | bytes 5242880 | tf_op jit(solution)/shard_map/all_gather | solution.py:1160
  205.6 32.0 %collective-permute-start.26 = (bf16[256,2048]{1,0:T(8,128)(2,1)S(1)}, bf16[256,2048]{1,0:T(8,128)(2,1)}, u32[]{:S(2)}, u32[]{:S(2)}) collective-permute-start(bf16[256,2048]{1,0:T(8,128)(2,1)S(1)} %copy-done.12), channel_id=1, source_target_pairs={{0,2},{2,4},{4,6},{6,7},{7,5},{5,3},{3,1},{1,0},{8,10},{10,12},{12... | collective-permute-start | bytes 3145736 | tf_op jit(solution)/shard_map/ppermute | solution.py:656
  206.4 31.2 %collective-permute-start.27 = (bf16[256,2048]{1,0:T(8,128)(2,1)S(1)}, bf16[256,2048]{1,0:T(8,128)(2,1)S(1)}, u32[]{:S(2)}, u32[]{:S(2)}) collective-permute-start(bf16[256,2048]{1,0:T(8,128)(2,1)S(1)} %dynamic-slice_bitcast_fusion.refs_0_), channel_id=1, source_target_pairs={{0,1},{2,0},{4,2},{6,4},{7,6},{5,7},{3,5},{1,3},{8,9},{10,8},{12,1... | collective-permute-start | bytes 3145736 | tf_op jit(solution)/shard_map/ppermute | solution.py:656
  410.9 32.1 %collective-permute-start.58 = (bf16[256,2048]{1,0:T(8,128)(2,1)S(1)}, bf16[256,2048]{1,0:T(8,128)(2,1)S(1)}, u32[]{:S(2)}, u32[]{:S(2)}) collective-permute-start(bf16[256,2048]{1,0:T(8,128)(2,1)S(1)} %copy-done.20), channel_id=1, source_target_pairs={{0,16},{8,24},{16,0},{24,8},{1,17},{9,25},{17,1},{25,9},{2,18},{10... | collective-permute-start | bytes 3145736 | tf_op jit(solution)/shard_map/ppermute | solution.py:359
  478.3 56.0 %collective-permute-start.68 = (bf16[1024,512]{1,0:T(8,128)(2,1)}, bf16[1024,512]{1,0:T(8,128)(2,1)S(1)}, u32[]{:S(2)}, u32[]{:S(2)}) collective-permute-start(bf16[1024,512]{1,0:T(8,128)(2,1)} %get-tuple-element.369.refs_0_.left_ref), channel_id=1, source_target_pairs={{0,16},{8,24},{16,0},{24,8},{1,17},{9,25},{17,1},{25,9},{2,18},{10... | collective-permute-start | bytes 3145736 | tf_op jit(solution)/shard_map/ppermute | solution.py:359
  490.7 35.6 %collective-permute-start.63 = (bf16[256,2048]{1,0:T(8,128)(2,1)}, bf16[256,2048]{1,0:T(8,128)(2,1)}, u32[]{:S(2)}, u32[]{:S(2)}) collective-permute-start(bf16[256,2048]{1,0:T(8,128)(2,1)} %get-tuple-element.362), channel_id=1, source_target_pairs={{0,16},{8,24},{16,0},{24,8},{1,17},{9,25},{17,1},{25,9},{2,18},{10... | collective-permute-start | bytes 3145736 | tf_op jit(solution)/shard_map/ppermute | solution.py:359
  536.8 27.2 %collective-permute-start.64 = (bf16[256,2048]{1,0:T(8,128)(2,1)S(1)}, bf16[256,2048]{1,0:T(8,128)(2,1)S(1)}, u32[]{:S(2)}, u32[]{:S(2)}) collective-permute-start(bf16[256,2048]{1,0:T(8,128)(2,1)S(1)} %get-tuple-element.526.refs_0_), channel_id=1, source_target_pairs={{0,16},{8,24},{16,0},{24,8},{1,17},{9,25},{17,1},{25,9},{2,18},{10... | collective-permute-start | bytes 3145736 | tf_op jit(solution)/shard_map/ppermute | solution.py:359
  594.6 27.3 %collective-permute-start.77 = (bf16[256,2048]{1,0:T(8,128)(2,1)}, bf16[256,2048]{1,0:T(8,128)(2,1)}, u32[]{:S(2)}, u32[]{:S(2)}) collective-permute-start(bf16[256,2048]{1,0:T(8,128)(2,1)} %get-tuple-element.389), channel_id=1, source_target_pairs={{0,2},{2,4},{4,6},{6,7},{7,5},{5,3},{3,1},{1,0},{8,10},{10,12},{12... | collective-permute-start | bytes 3145736 | tf_op jit(solution)/shard_map/ppermute | solution.py:757
  601.4 26.7 %collective-permute-start.76 = (bf16[256,2048]{1,0:T(8,128)(2,1)}, bf16[256,2048]{1,0:T(8,128)(2,1)}, u32[]{:S(2)}, u32[]{:S(2)}) collective-permute-start(bf16[256,2048]{1,0:T(8,128)(2,1)} %get-tuple-element.393), channel_id=1, source_target_pairs={{0,16},{8,24},{16,0},{24,8},{1,17},{9,25},{17,1},{25,9},{2,18},{10... | collective-permute-start | bytes 3145736 | tf_op jit(solution)/shard_map/ppermute | solution.py:359
  626.1 38.2 %collective-permute-start.80 = (bf16[256,2048]{1,0:T(8,128)(2,1)}, bf16[256,2048]{1,0:T(8,128)(2,1)}, u32[]{:S(2)}, u32[]{:S(2)}) collective-permute-start(bf16[256,2048]{1,0:T(8,128)(2,1)} %get-tuple-element.402), channel_id=1, source_target_pairs={{0,2},{2,4},{4,6},{6,7},{7,5},{5,3},{3,1},{1,0},{8,10},{10,12},{12... | collective-permute-start | bytes 3145736 | tf_op jit(solution)/shard_map/ppermute | solution.py:757
  627.7 36.6 %collective-permute-start.81 = (bf16[256,2048]{1,0:T(8,128)(2,1)}, bf16[256,2048]{1,0:T(8,128)(2,1)}, u32[]{:S(2)}, u32[]{:S(2)}) collective-permute-start(bf16[256,2048]{1,0:T(8,128)(2,1)} %get-tuple-element.403), channel_id=1, source_target_pairs={{0,1},{2,0},{4,2},{6,4},{7,6},{5,7},{3,5},{1,3},{8,9},{10,8},{12,1... | collective-permute-start | bytes 3145736 | tf_op jit(solution)/shard_map/ppermute | solution.py:757
  634.2 33.1 %collective-permute-start.79 = (bf16[256,2048]{1,0:T(8,128)(2,1)S(1)}, bf16[256,2048]{1,0:T(8,128)(2,1)S(1)}, u32[]{:S(2)}, u32[]{:S(2)}) collective-permute-start(bf16[256,2048]{1,0:T(8,128)(2,1)S(1)} %fusion.20.refs_0_), channel_id=1, source_target_pairs={{0,16},{8,24},{16,0},{24,8},{1,17},{9,25},{17,1},{25,9},{2,18},{10... | collective-permute-start | bytes 3145736 | tf_op jit(solution)/shard_map/ppermute | solution.py:359
  667.9 27.8 %collective-permute-start.88 = (bf16[256,2048]{1,0:T(8,128)(2,1)S(1)}, bf16[256,2048]{1,0:T(8,128)(2,1)S(1)}, u32[]{:S(2)}, u32[]{:S(2)}) collective-permute-start(bf16[256,2048]{1,0:T(8,128)(2,1)S(1)} %get-tuple-element.414), channel_id=1, source_target_pairs={{0,2},{2,4},{4,6},{6,7},{7,5},{5,3},{3,1},{1,0},{8,10},{10,12},{12... | collective-permute-start | bytes 3145736 | tf_op jit(solution)/shard_map/ppermute | solution.py:757
  669.2 27.2 %collective-permute-start.89 = (bf16[256,2048]{1,0:T(8,128)(2,1)S(1)}, bf16[256,2048]{1,0:T(8,128)(2,1)S(1)}, u32[]{:S(2)}, u32[]{:S(2)}) collective-permute-start(bf16[256,2048]{1,0:T(8,128)(2,1)S(1)} %get-tuple-element.415), channel_id=1, source_target_pairs={{0,1},{2,0},{4,2},{6,4},{7,6},{5,7},{3,5},{1,3},{8,9},{10,8},{12,1... | collective-permute-start | bytes 3145736 | tf_op jit(solution)/shard_map/ppermute | solution.py:757
  696.4 38.1 %collective-permute-start.98 = (bf16[1024,512]{1,0:T(8,128)(2,1)}, bf16[1024,512]{1,0:T(8,128)(2,1)}, u32[]{:S(2)}, u32[]{:S(2)}) collective-permute-start(bf16[1024,512]{1,0:T(8,128)(2,1)} %get-tuple-element.433.refs_0_.left_ref), channel_id=1, source_target_pairs={{0,16},{8,24},{16,0},{24,8},{1,17},{9,25},{17,1},{25,9},{2,18},{10... | collective-permute-start | bytes 3145736 | tf_op jit(solution)/shard_map/ppermute | solution.py:359
  708.3 27.1 %collective-permute-start.97 = (bf16[1024,512]{1,0:T(8,128)(2,1)}, bf16[1024,512]{1,0:T(8,128)(2,1)}, u32[]{:S(2)}, u32[]{:S(2)}) collective-permute-start(bf16[1024,512]{1,0:T(8,128)(2,1)} %get-tuple-element.433.refs_0_.left_ref), channel_id=1, source_target_pairs={{0,8},{8,0},{16,24},{24,16},{1,9},{9,1},{17,25},{25,17},{2,10},{10... | collective-permute-start | bytes 3145736 | tf_op jit(solution)/shard_map/ppermute | solution.py:359
  709.4 26.2 %collective-permute-start.95 = (bf16[256,2048]{1,0:T(8,128)(2,1)}, bf16[256,2048]{1,0:T(8,128)(2,1)}, u32[]{:S(2)}, u32[]{:S(2)}) collective-permute-start(bf16[256,2048]{1,0:T(8,128)(2,1)} %get-tuple-element.424), channel_id=1, source_target_pairs={{0,2},{2,4},{4,6},{6,7},{7,5},{5,3},{3,1},{1,0},{8,10},{10,12},{12... | collective-permute-start | bytes 3145736 | tf_op jit(solution)/shard_map/ppermute | solution.py:757
  734.5 26.9 %collective-permute-start.92 = (bf16[256,2048]{1,0:T(8,128)(2,1)}, bf16[256,2048]{1,0:T(8,128)(2,1)}, u32[]{:S(2)}, u32[]{:S(2)}) collective-permute-start(bf16[256,2048]{1,0:T(8,128)(2,1)} %get-tuple-element.432), channel_id=1, source_target_pairs={{0,16},{8,24},{16,0},{24,8},{1,17},{9,25},{17,1},{25,9},{2,18},{10... | collective-permute-start | bytes 3145736 | tf_op jit(solution)/shard_map/ppermute | solution.py:359
  735.4 29.8 %collective-permute-start.100 = (bf16[256,2048]{1,0:T(8,128)(2,1)}, bf16[256,2048]{1,0:T(8,128)(2,1)S(1)}, u32[]{:S(2)}, u32[]{:S(2)}) collective-permute-start(bf16[256,2048]{1,0:T(8,128)(2,1)} %copy-done.59), channel_id=1, source_target_pairs={{0,8},{8,0},{16,24},{24,16},{1,9},{9,1},{17,25},{25,17},{2,10},{10... | collective-permute-start | bytes 3145736 | tf_op jit(solution)/shard_map/ppermute | solution.py:359
  735.6 30.3 %collective-permute-start.101 = (bf16[256,2048]{1,0:T(8,128)(2,1)}, bf16[256,2048]{1,0:T(8,128)(2,1)S(1)}, u32[]{:S(2)}, u32[]{:S(2)}) collective-permute-start(bf16[256,2048]{1,0:T(8,128)(2,1)} %copy-done.58), channel_id=1, source_target_pairs={{0,8},{8,0},{16,24},{24,16},{1,9},{9,1},{17,25},{25,17},{2,10},{10... | collective-permute-start | bytes 3145736 | tf_op jit(solution)/shard_map/ppermute | solution.py:359
  758.9 53.3 %collective-permute-start.111 = (bf16[256,2048]{1,0:T(8,128)(2,1)S(1)}, bf16[256,2048]{1,0:T(8,128)(2,1)S(1)}, u32[]{:S(2)}, u32[]{:S(2)}) collective-permute-start(bf16[256,2048]{1,0:T(8,128)(2,1)S(1)} %get-tuple-element.442), channel_id=1, source_target_pairs={{0,2},{2,4},{4,6},{6,7},{7,5},{5,3},{3,1},{1,0},{8,10},{10,12},{12... | collective-permute-start | bytes 3145736 | tf_op jit(solution)/shard_map/ppermute | solution.py:757
  761.4 50.8 %collective-permute-start.112 = (bf16[256,2048]{1,0:T(8,128)(2,1)S(1)}, bf16[256,2048]{1,0:T(8,128)(2,1)S(1)}, u32[]{:S(2)}, u32[]{:S(2)}) collective-permute-start(bf16[256,2048]{1,0:T(8,128)(2,1)S(1)} %get-tuple-element.443), channel_id=1, source_target_pairs={{0,1},{2,0},{4,2},{6,4},{7,6},{5,7},{3,5},{1,3},{8,9},{10,8},{12,1... | collective-permute-start | bytes 3145736 | tf_op jit(solution)/shard_map/ppermute | solution.py:757
  765.2 45.1 %collective-permute-start.103 = (bf16[128,2048]{1,0:T(8,128)(2,1)S(1)}, bf16[128,2048]{1,0:T(8,128)(2,1)S(1)}, u32[]{:S(2)}, u32[]{:S(2)}) collective-permute-start(bf16[128,2048]{1,0:T(8,128)(2,1)S(1)} %get-tuple-element.446), channel_id=1, source_target_pairs={{0,2},{2,4},{4,6},{6,7},{7,5},{5,3},{3,1},{1,0},{8,10},{10,12},{12... | collective-permute-start | bytes 1572872 | tf_op jit(solution)/shard_map/ppermute | solution.py:757
  765.9 44.4 %collective-permute-start.104 = (bf16[128,2048]{1,0:T(8,128)(2,1)S(1)}, bf16[128,2048]{1,0:T(8,128)(2,1)S(1)}, u32[]{:S(2)}, u32[]{:S(2)}) collective-permute-start(bf16[128,2048]{1,0:T(8,128)(2,1)S(1)} %get-tuple-element.447), channel_id=1, source_target_pairs={{0,1},{2,0},{4,2},{6,4},{7,6},{5,7},{3,5},{1,3},{8,9},{10,8},{12,1... | collective-permute-start | bytes 1572872 | tf_op jit(solution)/shard_map/ppermute | solution.py:757
  772.8 34.8 %collective-permute-start.106 = (bf16[128,2048]{1,0:T(8,128)(2,1)S(1)}, bf16[128,2048]{1,0:T(8,128)(2,1)S(1)}, u32[]{:S(2)}, u32[]{:S(2)}) collective-permute-start(bf16[128,2048]{1,0:T(8,128)(2,1)S(1)} %get-tuple-element.439), channel_id=1, source_target_pairs={{0,1},{2,0},{4,2},{6,4},{7,6},{5,7},{3,5},{1,3},{8,9},{10,8},{12,1... | collective-permute-start | bytes 1572872 | tf_op jit(solution)/shard_map/ppermute | solution.py:757
  816.6 122.9 %all-gather.6.cloned.1.call-start = ((), (), s32[]{:S(2)}) async-start(), calls=%async_computation.2 | async-start | bytes 5242880 | tf_op jit(solution)/shard_map/all_gather | solution.py:1160
  817.3 146.4 %all-gather.8.cloned.1.call-start = ((), (), s32[]{:S(2)}) async-start(), calls=%async_computation.3 | async-start | bytes 5242880 | tf_op jit(solution)/shard_map/all_gather | solution.py:1160
  817.4 42.2 %collective-permute-start.102 = (bf16[256,2048]{1,0:T(8,128)(2,1)}, bf16[256,2048]{1,0:T(8,128)(2,1)S(1)}, u32[]{:S(2)}, u32[]{:S(2)}) collective-permute-start(bf16[256,2048]{1,0:T(8,128)(2,1)} %copy-done.60), channel_id=1, source_target_pairs={{0,16},{8,24},{16,0},{24,8},{1,17},{9,25},{17,1},{25,9},{2,18},{10... | collective-permute-start | bytes 3145736 | tf_op jit(solution)/shard_map/ppermute | solution.py:359
  819.9 27.4 %collective-permute-start.107 = (bf16[128,2048]{1,0:T(8,128)(2,1)S(1)}, bf16[128,2048]{1,0:T(8,128)(2,1)S(1)}, u32[]{:S(2)}, u32[]{:S(2)}) collective-permute-start(bf16[128,2048]{1,0:T(8,128)(2,1)S(1)} %copy-done.70), channel_id=1, source_target_pairs={{0,2},{2,4},{4,6},{6,7},{7,5},{5,3},{3,1},{1,0},{8,10},{10,12},{12... | collective-permute-start | bytes 1572872 | tf_op jit(solution)/shard_map/ppermute | solution.py:757
  820.9 26.3 %collective-permute-start.108 = (bf16[128,2048]{1,0:T(8,128)(2,1)S(1)}, bf16[128,2048]{1,0:T(8,128)(2,1)S(1)}, u32[]{:S(2)}, u32[]{:S(2)}) collective-permute-start(bf16[128,2048]{1,0:T(8,128)(2,1)S(1)} %copy-done.68), channel_id=1, source_target_pairs={{0,1},{2,0},{4,2},{6,4},{7,6},{5,7},{3,5},{1,3},{8,9},{10,8},{12,1... | collective-permute-start | bytes 1572872 | tf_op jit(solution)/shard_map/ppermute | solution.py:757
  903.6 34.0 %collective-permute-start.125 = (bf16[128,2048]{1,0:T(8,128)(2,1)}, bf16[128,2048]{1,0:T(8,128)(2,1)}, u32[]{:S(2)}, u32[]{:S(2)}) collective-permute-start(bf16[128,2048]{1,0:T(8,128)(2,1)} %get-tuple-element.493), channel_id=1, source_target_pairs={{0,16},{8,24},{16,0},{24,8},{1,17},{9,25},{17,1},{25,9},{2,18},{10... | collective-permute-start | bytes 1572872 | tf_op jit(solution)/shard_map/ppermute | solution.py:359
  (240 other events, 2935.5 us)
Sparse Core Ops, SparseCore 0:
  816.7 47.7 all-gather.3
  866.6 32.0 all-gather.5
  900.9 45.4 all-gather.7
